TPU v7x, 128 devices: a whole 4x4x4 slice. The times are simulated.
128 devices in a mesh: ctx: 16 (over x, z), head: 8 (over y, core).
Axes of the slice: x: 4, y: 4, z: 4, core: 2. Of those that a mesh axis runs over, the one named last changes fastest.
Arguments:
- x_tokens: bfloat16 [16384, 16384], P('ctx', 'head'), may hold values from -6 to 6
- bc_tokens: bfloat16 [16384, 2, 8, 256], P('ctx', None, 'head'), may hold values from -6 to 6
- z_tokens: bfloat16 [16384, 16384], P('ctx', 'head'), may hold values from -6 to 6
- dt_tokens: float32 [16384, 256], P('ctx', 'head'), may hold values from -3.5 to 16384
- conv_x: bfloat16 [4, 16384], P(None, 'head'), may hold values from -3 to 3
- conv_bc: bfloat16 [4, 2, 8, 256], P(None, None, 'head'), may hold values from -3 to 3
- bias_x: bfloat16 [16384], P('head'), may hold values from -0.75 to -0.25
- bias_bc: bfloat16 [2, 8, 256], P(None, 'head'), may hold values from -3 to 3
- a_log: float32 [256], replicated, may hold values from -12 to 3
- dt_bias: float32 [256], replicated, may hold values from -5 to -2.9
- d_skip: float32 [256], replicated, may hold values from 0.5 to 1.5
- norm_gain: float32 [16384], replicated, may hold values from 0.5 to 1.5
- state_cache: bfloat16 [32, 256, 64, 256], P(None, ('ctx', 'head')), may hold values from -6 to 6
- traj_slot: int32 [32], replicated, may hold values from 0 to 31, each once
- row_traj: int32 [128], replicated, may hold values from 0 to 31, as said below
- x_decode: bfloat16 [4, 128, 16384], P(None, None, ('ctx', 'head')), may hold values from -20 to 20
- bc_decode: bfloat16 [4, 128, 2, 8, 256], replicated, may hold values from -6 to 6
- z_decode: bfloat16 [4, 128, 16384], P(None, None, ('ctx', 'head')), may hold values from -6 to 6
- dt_decode: float32 [4, 128, 256], P(None, None, ('ctx', 'head')), may hold values from -3 to 3
Outputs:
- prefill_out: bfloat16 [16384, 16384], P('ctx', 'head')
- decode_out: bfloat16 [4, 128, 16384], P(None, None, ('ctx', 'head'))
Inputs may be any that keep to these rules, and one draw needn't show every extreme that they name: `traj_slot`: each of the 32 slots once. `row_traj`: each trajectory is named by exactly 4 rows.
All inputs are finite; a program needn't handle non-finite values.
Results may differ from a plain program's by a relative error of at most 0.011.
Values may be sent and summed in bfloat16 or wider, within the bound.
No kernel may reach another device: no remote copies, remote signals or barrier semaphores. Data moves between devices by JAX's collectives and lax.ppermute only.
A program may use at most 384 MiB of HBM per device.

v0:
```python
import jax
import jax.numpy as jnp
from jax import lax
from jax.sharding import PartitionSpec as P

BLOCK = 128


EPSILON = 1e-05
HIGHEST = lax.Precision.HIGHEST


def shifted(block, axis, distance):
    devices = range(lax.axis_size(axis))
    route = [(i - distance, i) for i in devices if i - distance in devices]
    return lax.ppermute(block, axis, route)


def prefix(part, axis, combine, identity):
    place = lax.axis_index(axis)
    gathered = jax.tree.map(lambda a: lax.all_gather(a, axis), part)
    state = jax.tree.map(lambda a, e: jnp.zeros_like(a) + jnp.asarray(e, a.dtype), part, identity)

    def one(turn, state):
        return combine(
            state, jax.tree.map(lambda a: lax.dynamic_index_in_dim(a, turn, 0, False), gathered)
        )

    return lax.fori_loop(0, place, one, state)


def conv_apply(padded, weight, offset, length):
    total_sum = jnp.zeros((length,) + padded.shape[1:], jnp.float32) + offset.astype(jnp.float32)
    for tap_at in range(weight.shape[0]):
        total_sum = total_sum + weight[tap_at].astype(jnp.float32) * padded[
            tap_at : tap_at + length
        ].astype(jnp.float32)
    return jax.nn.silu(total_sum).astype(jnp.bfloat16)


def gated_norm(output, gate, gain_row):
    mixed_out = output * jax.nn.silu(gate.astype(jnp.float32))
    mean_sq = jnp.mean(mixed_out * mixed_out, axis=-1, keepdims=True)
    return (mixed_out * lax.rsqrt(mean_sq + EPSILON) * gain_row).astype(jnp.bfloat16)


def chain_combine(earlier, later):
    return (earlier[0] + later[0], jnp.exp(later[0])[..., None, None] * earlier[1] + later[1])


def local(
    x_tokens,
    bc_tokens,
    z_tokens,
    dt_tokens,
    conv_x,
    conv_bc,
    bias_x,
    bias_bc,
    a_log,
    dt_bias,
    d_skip,
    norm_gain,
    state_cache,
    traj_slot,
    row_traj,
    x_decode,
    bc_decode,
    z_decode,
    dt_decode,
):
    ctx_count = lax.axis_size("ctx")
    head_count = lax.axis_size("head")
    ctx_at = lax.axis_index("ctx")
    head_at = lax.axis_index("head")
    heads_all = a_log.shape[0]
    group_span = heads_all // head_count
    device_span = group_span // ctx_count
    tokens = x_tokens.shape[0]
    head_width = state_cache.shape[2]
    state_size = state_cache.shape[3]
    groups_here = bc_tokens.shape[2]
    group_heads = group_span // groups_here
    tap_count = conv_x.shape[0]
    blocks = tokens // BLOCK
    first_head = head_at * group_span
    x_cols = x_tokens.shape[1]
    edge_rows = jnp.concatenate(
        [
            x_tokens[tokens - tap_count + 1 :],
            bc_tokens[tokens - tap_count + 1 :].reshape(tap_count - 1, -1),
        ],
        1,
    )
    edge_rows = shifted(edge_rows, "ctx", 1)
    x_pad = jnp.concatenate([edge_rows[:, :x_cols], x_tokens], 0)
    bc_pad = jnp.concatenate(
        [edge_rows[:, x_cols:].reshape((tap_count - 1,) + bc_tokens.shape[1:]), bc_tokens], 0
    )
    x_conv = conv_apply(x_pad, conv_x, bias_x, tokens)
    bc_conv = conv_apply(bc_pad, conv_bc, bias_bc, tokens)
    decay_all = -jnp.exp(a_log)
    decay_here = lax.dynamic_slice_in_dim(decay_all, first_head, group_span, 0)
    bias_here = lax.dynamic_slice_in_dim(dt_bias, first_head, group_span, 0)
    skip_here = lax.dynamic_slice_in_dim(d_skip, first_head, group_span, 0).reshape(
        groups_here, group_heads
    )
    gain_here = lax.dynamic_slice_in_dim(
        norm_gain, first_head * head_width, group_span * head_width, 0
    ).reshape(groups_here, group_heads * head_width)
    dt_here = jax.nn.softplus(dt_tokens + bias_here)
    log_here = dt_here * decay_here
    x_blk = x_conv.reshape(blocks, BLOCK, groups_here, group_heads, head_width)
    b_blk = bc_conv[:, 0].reshape(blocks, BLOCK, groups_here, state_size)
    c_blk = bc_conv[:, 1].reshape(blocks, BLOCK, groups_here, state_size)
    dt_blk = dt_here.reshape(blocks, BLOCK, groups_here, group_heads)
    running = jnp.cumsum(log_here.reshape(blocks, BLOCK, groups_here, group_heads), axis=1)
    along_time = jnp.transpose(running, (0, 2, 3, 1))
    dt_along = jnp.transpose(dt_blk, (0, 2, 3, 1))
    scores = jnp.einsum("btgn,bsgn->bgts", c_blk, b_blk, preferred_element_type=jnp.float32)
    causal = jnp.arange(BLOCK)[:, None] >= jnp.arange(BLOCK)[None, :]
    log_gaps = jnp.where(causal, along_time[..., :, None] - along_time[..., None, :], -jnp.inf)
    weights = (jnp.exp(log_gaps) * dt_along[..., None, :] * scores[:, :, None]).astype(jnp.bfloat16)
    inner_out = jnp.einsum("bghts,bsghp->btghp", weights, x_blk, preferred_element_type=jnp.float32)
    tail_weight = jnp.exp(running[:, -1:] - running) * dt_blk
    carried = (x_blk.astype(jnp.float32) * tail_weight[..., None]).astype(jnp.bfloat16)
    fresh_state = jnp.einsum(
        "bsghp,bsgn->bghpn", carried, b_blk, preferred_element_type=jnp.float32
    )
    block_log = running[:, -1]
    local_state = jnp.zeros(fresh_state.shape[1:], jnp.float32)
    local_log = jnp.zeros(block_log.shape[1:], jnp.float32)
    local_in = []
    prior_logs = []
    for block_at in range(blocks):
        local_in.append(local_state)
        prior_logs.append(local_log)
        local_state = (
            jnp.exp(block_log[block_at])[..., None, None] * local_state + fresh_state[block_at]
        )
        local_log = local_log + block_log[block_at]
    local_in = jnp.stack(local_in)
    prior_logs = jnp.stack(prior_logs)
    own_prior = state_cache[traj_slot[0]]
    prior_all = lax.all_gather(own_prior, ("ctx", "head"), axis=0, tiled=True)
    initial = (
        lax.dynamic_slice_in_dim(prior_all, first_head, group_span, 0)
        .astype(jnp.float32)
        .reshape(groups_here, group_heads, head_width, state_size)
    )
    before_log, before_state = prefix(
        (local_log, local_state),
        "ctx",
        chain_combine,
        (jnp.zeros_like(local_log), jnp.zeros_like(local_state)),
    )
    entering = jnp.exp(before_log)[..., None, None] * initial + before_state
    block_states = jnp.exp(prior_logs)[..., None, None] * entering[None] + local_in
    outer_out = jnp.exp(running)[..., None] * jnp.einsum(
        "btgn,bghpn->btghp",
        c_blk,
        block_states.astype(jnp.bfloat16),
        preferred_element_type=jnp.float32,
    )
    output = inner_out + outer_out + skip_here[..., None] * x_blk.astype(jnp.float32)
    output = output.reshape(tokens, groups_here, group_heads * head_width)
    prefill_out = gated_norm(
        output, z_tokens.reshape(tokens, groups_here, group_heads * head_width), gain_here
    ).reshape(tokens, group_span * head_width)
    leaving = jnp.exp(local_log)[..., None, None] * entering + local_state
    leaving = jnp.where(ctx_at == ctx_count - 1, leaving, 0.0)
    leaving = leaving.reshape(group_span, head_width, state_size)
    spread_out = lax.dynamic_update_slice_in_dim(
        jnp.zeros((heads_all, head_width, state_size), jnp.float32), leaving, first_head, 0
    )
    final_here = lax.psum_scatter(spread_out, ("ctx", "head"), scatter_dimension=0, tiled=True)
    group_total = bc_decode.shape[3]
    heads_per_group = heads_all // group_total
    dec_first = (ctx_at * head_count + head_at) * device_span
    decay_dec = lax.dynamic_slice_in_dim(decay_all, dec_first, device_span, 0)
    bias_dec = lax.dynamic_slice_in_dim(dt_bias, dec_first, device_span, 0)
    skip_dec = lax.dynamic_slice_in_dim(d_skip, dec_first, device_span, 0)
    gain_dec = lax.dynamic_slice_in_dim(
        norm_gain, dec_first * head_width, device_span * head_width, 0
    ).reshape(device_span, head_width)
    group_ids = (dec_first + jnp.arange(device_span, dtype=jnp.int32)) // heads_per_group
    selector = (group_ids[:, None] == jnp.arange(group_total, dtype=jnp.int32)[None, :]).astype(
        jnp.float32
    )
    picked = jnp.einsum(
        "srcgn,hg->srchn",
        bc_decode,
        selector.astype(jnp.bfloat16),
        preferred_element_type=jnp.float32,
    )
    cached = state_cache[traj_slot[row_traj]].astype(jnp.float32)
    ssm_state = jnp.where((row_traj == 0)[:, None, None, None], final_here[None], cached)
    row_count = row_traj.shape[0]
    norm_count = heads_per_group * head_width
    results = []
    for step_at in range(x_decode.shape[0]):
        dt_now = jax.nn.softplus(dt_decode[step_at] + bias_dec)
        x_now = x_decode[step_at].reshape(row_count, device_span, head_width).astype(jnp.float32)
        ssm_state = (
            jnp.exp(dt_now * decay_dec)[:, :, None, None] * ssm_state
            + (dt_now[:, :, None] * x_now)[..., None] * picked[step_at, :, 0][:, :, None, :]
        )
        output = (
            jnp.einsum("rhpn,rhn->rhp", ssm_state, picked[step_at, :, 1], precision=HIGHEST)
            + skip_dec[:, None] * x_now
        )
        mixed_out = output * jax.nn.silu(
            z_decode[step_at].reshape(row_count, device_span, head_width).astype(jnp.float32)
        )
        partial_sq = jnp.einsum(
            "rh,hg->rg", jnp.sum(mixed_out * mixed_out, axis=-1), selector, precision=HIGHEST
        )
        total_sq = lax.psum(partial_sq, ("ctx", "head"))
        mean_sq = jnp.einsum("rg,hg->rh", total_sq, selector, precision=HIGHEST) / norm_count
        normed = mixed_out * lax.rsqrt(mean_sq + EPSILON)[..., None] * gain_dec
        results.append(normed.astype(jnp.bfloat16).reshape(row_count, device_span * head_width))
    decode_out = jnp.stack(results)
    return (prefill_out, decode_out)


def solution(mesh):
    in_specs = (
        P("ctx", "head"),
        P("ctx", None, "head", None),
        P("ctx", "head"),
        P("ctx", "head"),
        P(None, "head"),
        P(None, None, "head", None),
        P("head"),
        P(None, "head", None),
        P(),
        P(),
        P(),
        P(),
        P(None, ("ctx", "head"), None, None),
        P(),
        P(),
        P(None, None, ("ctx", "head")),
        P(),
        P(None, None, ("ctx", "head")),
        P(None, None, ("ctx", "head")),
    )
    out_specs = (P("ctx", "head"), P(None, None, ("ctx", "head")))
    return jax.shard_map(local, mesh=mesh, in_specs=in_specs, out_specs=out_specs, check_vma=False)
```

profile of v0, /device:TPU:3, one launch (start us, length us, event | category | flops | bytes accessed | tf_op | source)
XLA Modules:
  0.0 1203.9 jit_solution(16224912255724442984)
XLA Ops:
  8.9 3.5 collective-permute-start
  15.3 23.3 %fusion.136 = f32[8,128,1,32]{3,0,1,2:T(8,128)S(1)} fusion(f32[8,128,1,32]{3,0,1,2:T(8,128)S(1)} %copy.166), kind=kOutput, calls=%fused_computation.272 | output fusion | flops 4161536 | bytes 262144 | tf_op jit(solution)/shard_map/jit(cumsum)/reduce_window_sum | solution.py:117
  42.4 1.5 broadcast_dynamic-update-slice_fusion
  44.0 2.4 copy.171
  46.4 6.4 copy.164
  52.9 3.6 multiply_convert_fusion.7
  58.5 16.6 %convert_bitcast_fusion = (f32[256,8,8,128]{3,1,2,0:T(8,128)}, bf16[1024,2048]{0,1:T(8,128)(2,1)S(1)}) fusion(bf16[1024,2048]{0,1:T(8,128)(2,1)} %copy.164, f32[2048]{0:T(1024)S(1)} %bitcast.320, bf16[3,2048]{0,1:T(8,128)(2,1)} %copy.163, f32[2048]{0:T(1024)S(1)} %bitcast.321, f32[2048]{0:T(1024)S(1)} %bitcast.319, f32[2048]{0:T(1024)S(1)} %bitcast.318, ...), kind=kLoop, calls=%fused_computation.30 | loop fusion | flops 56623104 | bytes 16830464
  78.1 2.3 fusion.63
  80.5 5.1 slice_add_fusion
  85.6 3.8 copy-done.5
  90.3 15.6 %all-gather = f32[16,1,1,32]{3,2,1,0:T(1,128)S(1)} all-gather(f32[1,1,1,32]{3,2,1,0:T(1,128)S(1)} %bitcast.325), channel_id=2, replica_groups=mesh['ctx'=16,'head'=8] {'ctx'}, dimensions={0}, use_global_device_ids=true | all-gather | bytes 2176 | tf_op jit(solution)/shard_map/all_gather | solution.py:21
  105.9 183.0 %all-gather.6.cloned.1.call-done = f32[16,32,64,256]{3,2,1,0:T(8,128)} async-done(((f32[1,32,64,256]{3,2,1,0:T(8,128)}), f32[16,32,64,256]{3,2,1,0:T(8,128)}) %all-gather.6.cloned.1.call-update) | async-done | bytes 33554448 | tf_op jit(solution)/shard_map/all_gather | solution.py:21
  289.0 1.7 broadcast.379
  290.7 16.0 %while.12 = (s32[]{:T(128)}, f32[1,32]{1,0:T(1,128)S(1)}, f32[1,32,64,256]{3,2,1,0:T(8,128)}, s32[]{:T(128)}, f32[16,1,32]{2,1,0:T(1,128)S(1)}, /*index=5*/f32[1...) while((s32[]{:T(128)}, f32[1,32]{1,0:T(1,128)S(1)}, f32[1,32,64,256]{3,2,1,0:T(8,128)}, s32[]{:T(128)}, ...), condition=%wide.region_2.3_spmd, body=%wide.region_1.2_spmd.sunk | while | flops 1048613 | bytes 6292371 | solution.py:29
  290.7 4.0 bitcast_add_fusion.20
  294.7 4.0 bitcast_add_fusion.20
  298.7 4.0 bitcast_add_fusion.20
  302.7 4.0 bitcast_add_fusion.20
  306.6 54.3 %all-gather.8.cloned.1.call-done = bf16[1,256,64,256]{3,2,0,1:T(8,128)(2,1)} async-done(((bf16[1,2,64,256]{3,2,0,1:T(8,128)(2,1)}), bf16[1,256,64,256]{3,2,0,1:T(8,128)(2,1)}) %all-gather.8.cloned.1.call-update) | async-done | bytes 8388624 | tf_op jit(solution)/shard_map/all_gather | solution.py:145
  360.9 7.9 broadcast_in_dim.26
  368.8 3.1 bitcast_dynamic-update-slice_fusion
  372.0 1.4 dynamic_slice.42
  373.4 1.3 dynamic_slice.46
  375.3 1.3 dynamic_slice.44
  376.5 6.6 copy.185
  389.4 6.7 gather_fusion.1
  406.7 3.5 convolution_bitcast_fusion
  410.2 1.6 slice_bitcast_fusion.6
  411.8 8.9 copy.229
  420.7 1.5 constant_dynamic-update-slice_fusion.2
  422.2 3.4 fusion.86
  425.6 1.5 constant_dynamic-update-slice_fusion.1
  427.1 3.4 fusion.87
  430.6 1.5 constant_dynamic-update-slice_fusion
  432.4 3.2 fusion.88
  435.7 1.5 fusion.79
  437.2 11.5 fusion.12
  448.7 14.5 %fusion.14 = f32[8,128,1,32,64]{1,4,3,0,2:T(8,128)} fusion(f32[8,32,64,128]{3,2,1,0:T(8,128)} %fusion.12, f32[8,128,1,32,64]{1,0,4,3,2:T(8,128)} %bitcast.291, f32[32]{0:T(128)S(1)} %copy-done.49, f32[8,128,32]{1,2,0:T(8,128)} %get-tuple-element.155, f32[8,128,128]{2,1,0:T(8,128)S(1)} %fusion.137, f32[8,32,128]{2,1,0:T(8,128)} %copy.169, ...), kind=kOutput, calls=%fused_computation.28 | convolution fusion | flops 566231040 | bytes 30294144 | tf_op jit(solution)/shard_map/bghts,bsghp->btghp/dot_general | solution.py:124
  463.2 11.2 copy.184
  474.5 4.4 multiply_reduce_fusion
  478.9 4.5 multiply_convert_fusion.2
  483.4 6.5 copy.202
  489.9 462.9 %reduce-scatter.2.cloned.1.call-done = f32[2,64,256]{2,1,0:T(8,128)} async-done(((f32[256,64,256]{2,1,0:T(8,128)}), f32[2,64,256]{2,1,0:T(8,128)}) %reduce-scatter.2.cloned.1.call-update) | async-done | bytes 131088 | tf_op jit(solution)/shard_map/reduce_scatter | solution.py:176
  953.0 19.4 %fusion.4 = f32[128,2,1,64]{3,2,1,0:T(1,128)S(1)} fusion(bf16[128,2,64,256]{3,2,1,0:T(8,128)(2,1)} %gather_fusion.1, f32[128,2,256]{2,1,0:T(2,128)S(1)} %copy-done.17, f32[128,2,64]{2,1,0:T(2,128)S(1)} %copy-done.21, f32[2,64,256]{2,1,0:T(8,128)} %reduce-scatter.2.cloned.1.call-done, f32[128,2]{1,0:T(8,128)S(1)} %copy-done.26, ...), kind=kOutput, calls=%fused_computation.13 | convolution fusion | flops 71303168 | bytes 9176192 | tf_op jit(solution)/shard_map/rhpn,rhn->rhp/dot_general | solution.py:209
  973.1 21.2 %fusion.5 = f32[128,2,1,64]{3,2,1,0:T(1,128)S(1)} fusion(bf16[128,2,64,256]{3,2,1,0:T(8,128)(2,1)} %gather_fusion.1, f32[128,2,256]{2,1,0:T(2,128)S(1)} %copy-done.16, f32[128,2,64]{2,1,0:T(2,128)S(1)} %copy-done.22, f32[128,2]{1,0:T(8,128)S(1)} %copy-done.27, f32[128,2,256]{2,1,0:T(2,128)S(1)} %copy-done.17, f32[128,2,64]{2,1,0:T(2,128)S(1)} %copy-done.21, ...), kind=kOutput, calls=%fused_computation.16 | convolution fusion | flops 83886080 | bytes 9504896 | tf_op jit(solution)/shard_map/rhpn,rhn->rhp/dot_general | solution.py:209
  995.0 23.0 %fusion.6 = f32[128,2,1,64]{3,2,1,0:T(1,128)S(1)} fusion(bf16[128,2,64,256]{3,2,1,0:T(8,128)(2,1)} %gather_fusion.1, f32[128,2,256]{2,1,0:T(2,128)S(1)} %copy-done.15, f32[128,2,64]{2,1,0:T(2,128)S(1)} %copy-done.23, f32[128,2]{1,0:T(8,128)S(1)} %copy-done.28, f32[128,2,256]{2,1,0:T(2,128)S(1)} %copy-done.16, f32[128,2,64]{2,1,0:T(2,128)S(1)} %copy-done.22, ...), kind=kOutput, calls=%fused_computation.17 | convolution fusion | flops 96468992 | bytes 9833600 | tf_op jit(solution)/shard_map/rhpn,rhn->rhp/dot_general | solution.py:209
  1018.7 28.5 %fusion = f32[128,2,1,64]{3,2,1,0:T(1,128)} fusion(bf16[128,2,64,256]{3,2,1,0:T(8,128)(2,1)} %gather_fusion.1, f32[128,2,256]{2,1,0:T(2,128)S(1)} %copy-done.14, f32[128,2,64]{2,1,0:T(2,128)} %copy.200, f32[128,2]{1,0:T(8,128)} %copy.198, f32[128,2,256]{2,1,0:T(2,128)S(1)} %copy-done.15, f32[128,2,64]{2,1,0:T(2,128)} %copy.196, f32[128,2]{1,0:T(8,128)} %copy.194, ...), kind=kOutput, calls=%fused_computation.6 | convolution fusion | flops 109051904 | bytes 10162304 | tf_op jit(solution)/shard_map/rhpn,rhn->rhp/dot_general | solution.py:209
  1050.3 145.2 %all-reduce = (f32[128,8]{0,1:T(8,128)S(1)}, f32[128,8]{0,1:T(8,128)S(1)}, f32[128,8]{0,1:T(8,128)S(1)}, f32[128,8]{0,1:T(8,128)S(1)}) all-reduce(f32[128,8]{0,1:T(8,128)S(1)} %fusion.110, f32[128,8]{0,1:T(8,128)S(1)} %fusion.111, f32[128,8]{0,1:T(8,128)S(1)} %fusion.112, ...), channel_id=1, replica_groups=mesh['ctx'=16,'head'=8] {'ctx','head'}, use_global_device_ids=true, to_apply=%region_12.13 | all-reduce | flops 4096 | bytes 32768 | tf_op jit(solution)/shard_map/psum | solution.py:218
  (203 shorter events, 39.0 us)
Async XLA Ops:
  7.2 82.4 %copy-start = (bf16[32,2,64,256]{3,2,1,0:T(8,128)(2,1)S(1)}, bf16[32,2,64,256]{3,2,1,0:T(8,128)(2,1)}, u32[]{:S(2)}) copy-start(bf16[32,2,64,256]{3,2,1,0:T(8,128)(2,1)} %param.33) | copy-start | bytes 6291460
  7.2 45.6 %copy-start.34 = (bf16[2048]{0:T(1024)(128)(2,1)S(1)}, bf16[2048]{0:T(1024)(128)(2,1)}, u32[]{:S(2)}) copy-start(bf16[2048]{0:T(1024)(128)(2,1)} %param.27) | copy-start | bytes 12292
  7.2 281.8 %all-gather.6.cloned.1.call-start = ((), (), s32[]{:S(2)}) async-start(), calls=%async_computation.2 | async-start | bytes 35651584 | tf_op jit(solution)/shard_map/all_gather | solution.py:21
  8.9 44.0 %collective-permute-start = (bf16[3,2560]{1,0:T(4,128)(2,1)S(1)}, bf16[3,2560]{1,0:T(4,128)(2,1)S(1)}, u32[]{:S(2)}, u32[]{:S(2)}) collective-permute-start(bf16[3,2560]{1,0:T(4,128)(2,1)S(1)} %pad_maximum_fusion.3), channel_id=1, source_target_pairs={{0,8},{8,16},{16,24},{24,32},{32,40},{40,48},{48,56},{56,64},{64,7... | collective-permute-start | bytes 46088 | tf_op jit(solution)/shard_map/ppermute | solution.py:16
  13.1 25.7 %copy-start.40 = (f32[256]{0:T(256)}, f32[256]{0:T(256)S(1)}, u32[]{:S(2)}) copy-start(f32[256]{0:T(256)S(1)} %exponential_negate_fusion) | copy-start | bytes 3076
  39.4 41.1 %copy-start.30 = (f32[32]{0:T(128)}, f32[32]{0:T(128)S(1)}, u32[]{:S(2)}) copy-start(f32[32]{0:T(128)S(1)} %get-tuple-element.143) | copy-start | bytes 388
  39.4 41.1 %copy-start.32 = (f32[32]{0:T(128)}, f32[32]{0:T(128)S(1)}, u32[]{:S(2)}) copy-start(f32[32]{0:T(128)S(1)} %get-tuple-element.141) | copy-start | bytes 388
  80.5 8.9 copy-start.5
  80.5 9.0 copy-start.2
  89.4 271.5 %all-gather.8.cloned.1.call-start = ((), (), s32[]{:S(2)}) async-start(), calls=%async_computation.3 | async-start | bytes 8454144 | tf_op jit(solution)/shard_map/all_gather | solution.py:145
  90.2 862.6 %reduce-scatter.2.cloned.1.call-start = ((), (), s32[]{:S(2)}) async-start(), calls=%async_computation.1 | async-start | bytes 16908288 | tf_op jit(solution)/shard_map/reduce_scatter | solution.py:176
  306.6 62.2 %copy-start.36 = (f32[32]{0:T(128)}, f32[32]{0:T(128)S(1)}, u32[]{:S(2)}) copy-start(f32[32]{0:T(128)S(1)} %exponential_bitcast_fusion.5) | copy-start | bytes 388
  360.9 7.9 copy-start.3
  360.9 7.9 copy-start.10
  372.0 12.2 %copy-start.38 = (f32[1,32]{1,0:T(1,128)S(1)}, f32[1,32]{1,0:T(1,128)}, u32[]{:S(2)}) copy-start(f32[1,32]{1,0:T(1,128)} %get-tuple-element.133) | copy-start | bytes 388
  372.0 14.5 %copy-start.24 = (bf16[4,128,128]{2,1,0:T(8,128)(2,1)S(1)}, bf16[4,128,128]{2,1,0:T(8,128)(2,1)}, u32[]{:S(2)}) copy-start(bf16[4,128,128]{2,1,0:T(8,128)(2,1)} %param.38) | copy-start | bytes 393220
  372.0 15.3 %copy-start.25 = (bf16[4,128,128]{2,1,0:T(8,128)(2,1)S(1)}, bf16[4,128,128]{2,1,0:T(8,128)(2,1)}, u32[]{:S(2)}) copy-start(bf16[4,128,128]{2,1,0:T(8,128)(2,1)} %param.36) | copy-start | bytes 393220
  389.4 6.8 copy-start.35
  389.4 6.8 copy-start.44
  389.4 6.8 copy-start.45
  389.4 15.3 %copy-start.29 = (f32[16384]{0:T(1024)S(1)}, f32[16384]{0:T(1024)}, u32[]{:S(2)}) copy-start(f32[16384]{0:T(1024)} %param.32) | copy-start | bytes 196612
  389.4 16.7 %copy-start.48 = (s32[128]{0:T(128)S(1)}, s32[128]{0:T(128)}, u32[]{:S(2)}) copy-start(s32[128]{0:T(128)} %param.35) | copy-start | bytes 1540
  411.8 8.9 copy-start.9
  411.8 10.4 copy-start.33
  422.2 8.4 copy-start.7
  427.1 8.5 copy-start.4
  427.1 8.5 copy-start.37
  437.2 11.5 copy-start.49
  463.2 11.2 copy-start.6
  483.4 469.5 %copy-start.17 = (f32[128,2,256]{2,1,0:T(2,128)S(1)}, f32[128,2,256]{2,1,0:T(2,128)}, u32[]{:S(2)}) copy-start(f32[128,2,256]{2,1,0:T(2,128)} %get-tuple-element.130) | copy-start | bytes 786436
  483.4 469.5 %copy-start.20 = (f32[128,2,256,1]{2,1,0,3:T(2,128)S(1)}, f32[128,2,256,1]{2,1,0,3:T(2,128)}, u32[]{:S(2)}) copy-start(f32[128,2,256,1]{2,1,0,3:T(2,128)} %get-tuple-element.123) | copy-start | bytes 786436
  483.4 469.5 %copy-start.21 = (f32[128,2,64]{2,1,0:T(2,128)S(1)}, f32[128,2,64]{2,1,0:T(2,128)}, u32[]{:S(2)}) copy-start(f32[128,2,64]{2,1,0:T(2,128)} %copy.188) | copy-start | bytes 196612
  483.4 469.5 %copy-start.26 = (f32[128,2]{1,0:T(8,128)S(1)}, f32[128,2]{1,0:T(8,128)}, u32[]{:S(2)}) copy-start(f32[128,2]{1,0:T(8,128)} %copy.186) | copy-start | bytes 3076
  483.4 469.5 %copy-start.50 = (pred[128]{0:T(512)(128)(4,1)S(1)}, pred[128]{0:T(512)(128)(4,1)}, u32[]{:S(2)}) copy-start(pred[128]{0:T(512)(128)(4,1)} %broadcast_compare_fusion) | copy-start | bytes 388
  952.9 20.1 %copy-start.16 = (f32[128,2,256]{2,1,0:T(2,128)S(1)}, f32[128,2,256]{2,1,0:T(2,128)}, u32[]{:S(2)}) copy-start(f32[128,2,256]{2,1,0:T(2,128)} %get-tuple-element.129) | copy-start | bytes 786436
  952.9 20.1 %copy-start.19 = (f32[128,2,256,1]{2,1,0,3:T(2,128)S(1)}, f32[128,2,256,1]{2,1,0,3:T(2,128)}, u32[]{:S(2)}) copy-start(f32[128,2,256,1]{2,1,0,3:T(2,128)} %get-tuple-element.128) | copy-start | bytes 786436
  952.9 20.1 %copy-start.22 = (f32[128,2,64]{2,1,0:T(2,128)S(1)}, f32[128,2,64]{2,1,0:T(2,128)}, u32[]{:S(2)}) copy-start(f32[128,2,64]{2,1,0:T(2,128)} %copy.192) | copy-start | bytes 196612
  952.9 20.1 %copy-start.27 = (f32[128,2]{1,0:T(8,128)S(1)}, f32[128,2]{1,0:T(8,128)}, u32[]{:S(2)}) copy-start(f32[128,2]{1,0:T(8,128)} %copy.190) | copy-start | bytes 3076
  953.0 20.1 %copy-start.47 = (f32[2,64,256]{2,1,0:T(8,128)S(1)}, f32[2,64,256]{2,1,0:T(8,128)}, u32[]{:S(2)}) copy-start(f32[2,64,256]{2,1,0:T(8,128)} %reduce-scatter.2.cloned.1.call-done) | copy-start | bytes 393220
  973.1 21.9 %copy-start.15 = (f32[128,2,256]{2,1,0:T(2,128)S(1)}, f32[128,2,256]{2,1,0:T(2,128)}, u32[]{:S(2)}) copy-start(f32[128,2,256]{2,1,0:T(2,128)} %get-tuple-element.127) | copy-start | bytes 786436
  973.1 21.9 %copy-start.18 = (f32[128,2,256,1]{2,1,0,3:T(2,128)S(1)}, f32[128,2,256,1]{2,1,0,3:T(2,128)}, u32[]{:S(2)}) copy-start(f32[128,2,256,1]{2,1,0,3:T(2,128)} %get-tuple-element.126) | copy-start | bytes 786436
  973.1 21.9 %copy-start.23 = (f32[128,2,64]{2,1,0:T(2,128)S(1)}, f32[128,2,64]{2,1,0:T(2,128)}, u32[]{:S(2)}) copy-start(f32[128,2,64]{2,1,0:T(2,128)} %copy.196) | copy-start | bytes 196612
  973.1 21.9 %copy-start.28 = (f32[128,2]{1,0:T(8,128)S(1)}, f32[128,2]{1,0:T(8,128)}, u32[]{:S(2)}) copy-start(f32[128,2]{1,0:T(8,128)} %copy.194) | copy-start | bytes 3076
  995.0 23.7 %copy-start.14 = (f32[128,2,256]{2,1,0:T(2,128)S(1)}, f32[128,2,256]{2,1,0:T(2,128)}, u32[]{:S(2)}) copy-start(f32[128,2,256]{2,1,0:T(2,128)} %get-tuple-element.125) | copy-start | bytes 786436
  1018.7 29.5 %copy-start.46 = (f32[2]{0:T(128)S(1)}, f32[2]{0:T(128)}, u32[]{:S(2)}) copy-start(f32[2]{0:T(128)} %dynamic_slice.46) | copy-start | bytes 28
  1018.7 30.6 %copy-start.43 = (s32[2]{0:T(128)S(1)}, s32[2]{0:T(128)}, u32[]{:S(2)}) copy-start(s32[2]{0:T(128)} %copy-done.42) | copy-start | bytes 28
  1018.7 177.5 %copy-start.39 = (f32[2,64]{1,0:T(2,128)S(1)}, f32[2,64]{1,0:T(2,128)}, u32[]{:S(2)}) copy-start(f32[2,64]{1,0:T(2,128)} %mul.792) | copy-start | bytes 1540
  1018.7 178.5 %copy-start.1 = (bf16[32,2,64,256]{3,2,1,0:T(8,128)(2,1)S(1)}, bf16[32,2,64,256]{3,2,1,0:T(8,128)(2,1)}, u32[]{:S(2)}) copy-start(bf16[32,2,64,256]{3,2,1,0:T(8,128)(2,1)} %param.33) | copy-start | bytes 6291460
  (8 other events, 36.5 us)
Sparse Core Ops, SparseCore 0:
  89.5 199.3 all-gather.5
  291.9 68.9 all-gather.7
  372.1 580.7 reduce-scatter.1
where the time goes:
time: 1220 us; the launch traced here: 1200 us
  waiting for transfers between devices  700 us (57%)
  blocking collectives  161 us (13%)
  matrix products  126 us (10%)
  local copies, waits for them, and re-layouts  99.9 us (8%)
  other arithmetic  98.6 us (8%)
  between operations  14.7 us (1%)
    reduce_scatter x1, waiting for transfers between devices, local(): lax.psum_scatter(spread_out, ('ctx', 'head'), scatter_dimension=0, tiled=...  463 us
    all_gather x1, waiting for transfers between devices, prefix(): gathered = jax.tree.map(lambda a: lax.all_gather(a, axis), part)  183 us
    psum x1, blocking collectives, local(): total_sq = lax.psum(partial_sq, ('ctx', 'head'))  145 us
    dot_general x4, matrix products, local(): jnp.einsum('rhpn,rhn->rhp', ssm_state, picked[step_at, :, 1], precision=H...  92 us
    all_gather x1, waiting for transfers between devices, local(): prior_all = lax.all_gather(own_prior, ('ctx', 'head'), axis=0, tiled=True)  54.3 us
    unnamed x126, local copies, waits for them, and re-layouts  48.4 us
    unnamed x4, other arithmetic  24.5 us
  transfers between devices with their start and end apart: 4, of which 3 were waited for; matrix products, arithmetic and copies ran while one was open for 15% of the time, Pallas kernels for 0%

commit v1 on v0

v1 whole, which is shorter than its diff:
```python
import jax
import jax.numpy as jnp
from jax import lax
from jax.experimental import pallas as pl
from jax.experimental.pallas import tpu as pltpu
from jax.sharding import PartitionSpec as P

BLOCK = 128
HEAD = 64
STATE = 256
SPAN = 32
WIDTH = SPAN * HEAD
RANKS = 16
ROWS = 128
STEPS = 4
QUAD = 256
EPSILON = 1e-05
LOG2E = 1.4426950408889634
F32 = jnp.float32
BF16 = jnp.bfloat16


def dot(a, b, dims=((1,), (0,))):
    return lax.dot_general(a, b, (dims, ((), ())), preferred_element_type=F32)


def halves(v):
    hi = v.astype(BF16)
    return hi, (v - hi.astype(F32)).astype(BF16)


def thirds(v):
    hi, mid = halves(v)
    return hi, mid, (v - hi.astype(F32) - mid.astype(F32)).astype(BF16)


def softplus(v):
    return jnp.maximum(v, 0.0) + jnp.log1p(jnp.exp(-jnp.abs(v)))


def silu(v):
    h = 0.5 * v
    return h + h * jnp.tanh(h)


def iota(shape, dim):
    return lax.broadcasted_iota(jnp.int32, shape, dim)


def fill_expander(ref):
    shape = (2 * SPAN, WIDTH)
    ref[...] = jnp.where(iota(shape, 1) // HEAD == iota(shape, 0) % SPAN, 1.0, 0.0).astype(BF16)


def conv(block, before, taps):
    joined = jnp.concatenate([before, block], 0)
    h = taps[4:5] + taps[0:1] * pltpu.roll(joined, 3, 0)[8:]
    h = h + taps[1:2] * pltpu.roll(joined, 2, 0)[8:]
    h = h + taps[2:3] * pltpu.roll(joined, 1, 0)[8:]
    h = h + taps[3:4] * block
    return (h + h * jnp.tanh(h)).astype(BF16)


def own_heads(head_at, alog_ref, bias_ref, skip_ref):
    rows = jnp.concatenate([alog_ref[...], bias_ref[...]] + [skip_ref[...]] * 6, 0)
    shape = (SPAN, rows.shape[1])
    mine = jnp.where(iota(shape, 1) == iota(shape, 0) + head_at * SPAN, 1.0, 0.0).astype(BF16)
    return sum(dot(mine, piece, ((1,), (1,))) for piece in thirds(rows))


def spread_heads(rows, spread):
    return dot(rows, spread)


def pair_halves(rows):
    return jnp.concatenate(halves(rows), 1)


def prep_kernel(at_ref, x_ref, bc_ref, edge_ref, dt_ref, alog_ref, bias_ref, skip_ref, cw_ref, cb_ref,
                bw_ref, bb_ref, xc_ref, car_ref, bco_ref, rdt_ref, send_ref,
                prevx, prevbc, state, rc, spread, own, wx, wbc):
    block_at = pl.program_id(0)

    @pl.when(block_at == 0)
    def _():
        fill_expander(spread)
        own[...] = own_heads(at_ref[0], alog_ref, bias_ref, skip_ref)
        state[...] = jnp.zeros_like(state)
        rc[...] = jnp.zeros_like(rc)
        prevx[...] = jnp.zeros_like(prevx)
        prevbc[...] = jnp.zeros_like(prevbc)
        edge = edge_ref[...].astype(F32)
        prevx[5:8, :] = edge[:, :WIDTH]
        prevbc[5:8, :] = edge[:, WIDTH:]
        wx[0:4, :] = cw_ref[...].astype(F32) * 0.5
        offset = cb_ref[...].astype(F32) * 0.5
        for i in range(WIDTH // 128):
            wx[4:5, i * 128:(i + 1) * 128] = offset[i:i + 1]
        taps = bw_ref[...].astype(F32) * 0.5
        offset = bb_ref[...].astype(F32) * 0.5
        for i in range(2):
            wbc[0:4, i * STATE:(i + 1) * STATE] = taps[:, i, :]
            wbc[4:5, i * STATE:(i + 1) * STATE] = offset[i:i + 1]

    bc_in = bc_ref[...].astype(F32)
    bc = conv(bc_in, prevbc[...], wbc[...])
    prevbc[...] = bc_in[BLOCK - 8:]
    bco_ref[...] = bc
    b_across = bc[:, :STATE].astype(F32).T.astype(BF16)

    dt = softplus(dt_ref[...] + own[:, 1:2])
    log = dt * (jnp.exp(own[:, 0:1]) * (-LOG2E))
    tri = jnp.where(iota((BLOCK, BLOCK), 0) <= iota((BLOCK, BLOCK), 1), 1.0, 0.0).astype(BF16)
    r = sum(dot(piece, tri) for piece in thirds(log))
    rdt_ref[0] = jnp.concatenate([r, dt], 0)
    r_last = r[:, BLOCK - 1:BLOCK]
    rc[...] = rc[...] + r_last
    tail = jnp.exp2(r_last - r) * dt
    decay = jnp.exp2(jnp.broadcast_to(r_last, (SPAN, BLOCK)))
    factors = jnp.concatenate([pair_halves(tail.T), pair_halves(decay.T[:16])], 0)

    for q in range(WIDTH // QUAD):
        cols = slice(q * QUAD, (q + 1) * QUAD)
        x_in = x_ref[:, cols].astype(F32)
        xc = conv(x_in, prevx[:, cols], wx[:, cols])
        prevx[:, cols] = x_in[BLOCK - 8:]
        xc_ref[:, cols] = xc
        factor = spread_heads(factors, spread[:, cols])
        carried = (xc.astype(F32) * factor[:BLOCK]).astype(BF16)
        car_ref[:, cols] = carried
        fresh = dot(b_across, carried)
        state[:, cols] = state[:, cols] * factor[BLOCK:BLOCK + 1] + fresh

    @pl.when(block_at == pl.num_programs(0) - 1)
    def _():
        decays = spread_heads(pair_halves(jnp.exp2(rc[...]).T[:16]), spread[...])
        for c in range(RANKS):
            cols = slice(c * 128, (c + 1) * 128)
            send_ref[c, 0:STATE, :] = state[:, cols]
            send_ref[c, STATE:, :] = decays[0:8, cols]


def inner_kernel(at_ref, xc_ref, bc_ref, rdt_ref, alog_ref, bias_ref, skip_ref, yl_ref, skip):
    @pl.when(pl.program_id(0) == 0)
    def _():
        spread = jnp.where(
            iota((SPAN, WIDTH), 1) // HEAD == iota((SPAN, WIDTH), 0), 1.0, 0.0).astype(BF16)
        own = own_heads(at_ref[0], alog_ref, bias_ref, skip_ref)
        skip[...] = sum(dot(p, spread, ((0,), (0,))) for p in thirds(own))

    b_now = bc_ref[:, :STATE]
    c_now = bc_ref[:, STATE:]
    scores = dot(c_now, b_now, ((1,), (1,)))
    scores = jnp.where(iota((BLOCK, BLOCK), 1) <= iota((BLOCK, BLOCK), 0), scores, 0.0)
    along = rdt_ref[0]
    r = along.T
    left = iota((BLOCK, 128), 1) < HEAD

    for q in range(WIDTH // QUAD):
        cols = slice(q * QUAD, (q + 1) * QUAD)
        xq = xc_ref[:, cols]
        parts = []
        for pair in range(2):
            weights = []
            for h in (4 * q + 2 * pair, 4 * q + 2 * pair + 1):
                gap = jnp.minimum(r[:, h:h + 1] - along[h:h + 1, :], 0.0)
                weight = jnp.exp2(gap) * (scores * along[SPAN + h:SPAN + h + 1, :])
                weights.append(weight.astype(BF16))
            xp = xq[:, pair * 128:(pair + 1) * 128]
            none = jnp.zeros_like(xp)
            rhs = jnp.concatenate([jnp.where(left, xp, none), jnp.where(left, none, xp)], 0)
            parts.append(dot(jnp.concatenate(weights, 1), rhs))
        out = jnp.concatenate(parts, 1) + skip[2:3, cols] * xq.astype(F32)
        yl_ref[:, cols] = out.astype(BF16)


def chosen_rows(traj):
    hit = jnp.broadcast_to(jnp.where(traj == 0, 1.0, 0.0), (8, ROWS))
    ahead = jnp.where(iota((ROWS, ROWS), 0) < iota((ROWS, ROWS), 1), 1.0, 0.0).astype(BF16)
    rank = dot(hit.astype(BF16), ahead)
    return jnp.where((rank == iota((8, ROWS), 0).astype(F32)) & (hit > 0.5), 1.0, 0.0)


def last_kernel(got_ref, prior_ref, reads_ref, first_ref, state):
    @pl.when(pl.program_id(0) == 0)
    def _():
        state[...] = prior_ref[...].astype(F32).T

    held = state[...]
    for c in range(got_ref.shape[0]):
        held = held * got_ref[c, STATE:STATE + 1, :] + got_ref[c, 0:STATE, :]
    state[...] = held

    @pl.when(pl.program_id(0) == pl.num_programs(0) - 1)
    def _():
        hi, lo = halves(held)
        reads = reads_ref[...].astype(BF16)
        first_ref[...] = dot(reads, hi) + dot(reads, lo)


def scan_kernel(got_ref, prior_ref, first_ref, enter_ref, state):
    @pl.when(pl.program_id(0) == 0)
    def _():
        state[...] = prior_ref[...].astype(F32).T

    held = state[...]
    for c in range(got_ref.shape[0]):
        enter_ref[c] = held
        held = held * got_ref[c, STATE:STATE + 1, :] + got_ref[c, 0:STATE, :]
    state[...] = held


def out_kernel(at_ref, yl_ref, car_ref, bc_ref, rdt_ref, in_ref, z_ref, gain_ref, out_ref,
               spread, state, mixed):
    @pl.when(pl.program_id(0) == 0)
    def _():
        fill_expander(spread)
        for c in range(RANKS):
            state[:, c * 128:(c + 1) * 128] = in_ref[c]

    b_across = bc_ref[:, :STATE].astype(F32).T.astype(BF16)
    c_now = bc_ref[:, STATE:]
    factors = pair_halves(jnp.exp2(rdt_ref[0, 0:SPAN, :]).T)
    total = jnp.zeros((BLOCK, 128), F32)
    for q in range(WIDTH // QUAD):
        cols = slice(q * QUAD, (q + 1) * QUAD)
        factor = spread_heads(factors, spread[:, cols])
        held = state[:, cols]
        y = yl_ref[:, cols].astype(F32) + dot(c_now, held.astype(BF16)) * factor
        fresh = dot(b_across, car_ref[:, cols])
        state[:, cols] = held * factor[BLOCK - 1:BLOCK] + fresh
        m = y * silu(z_ref[:, cols].astype(F32))
        mixed[:, cols] = m
        sq = m * m
        total = total + sq[:, :128] + sq[:, 128:]
    mean = jnp.sum(total, axis=1, keepdims=True) * (1.0 / WIDTH)
    scale = lax.rsqrt(mean + EPSILON)
    for q in range(WIDTH // QUAD):
        cols = slice(q * QUAD, (q + 1) * QUAD)
        out_ref[:, cols] = (mixed[:, cols] * scale * gain_ref[:, cols]).astype(BF16)


def two_heads(at_ref, ref):
    first = at_ref[0]
    lane = iota((1, 128), 1)
    return jnp.where(lane < HEAD, ref[first], ref[first + 1])


def decode_kernel(at_ref, alog_ref, bias_ref, skip_ref, slot_ref, cache_ref, bc_ref, x_ref, dt_ref,
                  traj_ref, y_ref, d_ref, reads_ref, order, held_b, held_c, sorted_c, reads):
    step = pl.program_id(0)

    @pl.when(step == 0)
    def _():
        traj = jnp.broadcast_to(traj_ref[...].astype(F32), (ROWS, ROWS))
        sub, lane = iota((ROWS, ROWS), 0), iota((ROWS, ROWS), 1)
        rank = jnp.sum(jnp.where((traj == traj.T) & (sub < lane), 1.0, 0.0), axis=0, keepdims=True)
        place = traj_ref[...].astype(F32) * 4.0 + rank
        order[...] = jnp.where(sub.astype(F32) == place, 1.0, 0.0).astype(BF16)

    shape = (96, 512)
    out, line = iota(shape, 0), iota(shape, 1)
    group = jnp.where(out < 64, at_ref[1], at_ref[2])
    wanted = (out % 32) * 16 + jnp.where(out < 32, 0, 8) + group
    pick = jnp.where(line == wanted, 1.0, 0.0).astype(BF16)
    prefill_c = []
    for g in range(ROWS // 32):
        got = dot(pick, bc_ref[g * 512:(g + 1) * 512, :]).astype(BF16)
        held_b[step, g * 32:(g + 1) * 32, :] = got[0:32]
        held_c[step, g * 32:(g + 1) * 32, :] = got[32:64]
        prefill_c.append(got[64:96])
    sorted_c[step] = dot(order[...], held_c[step]).astype(BF16)
    chosen = chosen_rows(traj_ref[...]).astype(BF16)
    reads_ref[...] = dot(chosen, jnp.concatenate(prefill_c, 0))

    @pl.when(step == STEPS - 1)
    def _():
        for g in range(ROWS // 16):
            lhs = jnp.concatenate([sorted_c[k, g * 16:(g + 1) * 16, :] for k in range(STEPS)], 0)
            row = iota((16 * STEPS, 128), 0) % 16 // 4
            out = jnp.zeros((16 * STEPS, 128), F32)
            for i in range(4):
                if g == 0 and i == 0:
                    continue
                got = dot(lhs, cache_ref[slot_ref[4 * g + i]], ((1,), (1,)))
                out = jnp.where(row == i, got, out)
            for k in range(STEPS):
                reads[k, g * 16:(g + 1) * 16, :] = out[k * 16:(k + 1) * 16]

        rate = jnp.exp(two_heads(at_ref, alog_ref)) * (-LOG2E)
        bias = two_heads(at_ref, bias_ref)
        skip = two_heads(at_ref, skip_ref)
        upper = iota((128, ROWS), 0) < HEAD
        total = jnp.ones((ROWS, 128), F32)
        pushed = []
        for k in range(STEPS):
            raw = dt_ref[k]
            dt = softplus(jnp.where(upper, raw[0:1, :], raw[1:2, :]).T + bias)
            x_now = x_ref[k].astype(F32)
            decay = jnp.exp2(dt * rate)
            total = total * decay
            pushed = [p * decay for p in pushed] + [dt * x_now]
            hi, lo = halves(reads[k])
            back = dot(order[...], hi, ((0,), (0,))) + dot(order[...], lo, ((0,), (0,)))
            y = total * back + skip * x_now
            c_now = held_c[k].astype(F32)
            for j in range(k + 1):
                met = jnp.sum(held_b[j].astype(F32) * c_now, axis=1, keepdims=True)
                y = y + pushed[j] * met
            y_ref[k] = y
            d_ref[k] = total


def mix_kernel(y_ref, d_ref, first_ref, z_ref, traj_ref, m_ref, sq_ref):
    pick = chosen_rows(traj_ref[...]).astype(BF16)
    ones = jnp.ones((8, 128), BF16)
    sq_ref[...] = jnp.zeros_like(sq_ref)
    for k in range(STEPS):
        hi, lo = halves(first_ref[k * 8:(k + 1) * 8, :])
        read = dot(pick, hi, ((0,), (0,))) + dot(pick, lo, ((0,), (0,)))
        m = (y_ref[k] + d_ref[k] * read) * silu(z_ref[k].astype(F32))
        m_ref[k] = m
        hi, lo = halves(m * m)
        sums = dot(ones, hi, ((1,), (1,))) + dot(ones, lo, ((1,), (1,)))
        sq_ref[k:k + 1, :] = sums[0:1]


def norm_kernel(at_ref, m_ref, sq_ref, gain_ref, out_ref):
    for k in range(STEPS):
        scale = lax.rsqrt(sq_ref[k:k + 1, :] * (1.0 / WIDTH) + EPSILON)
        scale = jnp.broadcast_to(scale, (ROWS, ROWS)).T
        out_ref[k] = (m_ref[k] * scale * gain_ref[...]).astype(BF16)


def full(shape):
    return pl.BlockSpec(shape, lambda *_: (0,) * len(shape))


def params(mib=60):
    return pltpu.CompilerParams(vmem_limit_bytes=mib * 2**20)


def cost(flops, nbytes):
    return pl.CostEstimate(flops=flops, bytes_accessed=nbytes, transcendentals=0)


def local(x_tokens, bc_tokens, z_tokens, dt_tokens, conv_x, conv_bc, bias_x, bias_bc, a_log, dt_bias,
          d_skip, norm_gain, state_cache, traj_slot, row_traj, x_decode, bc_decode, z_decode,
          dt_decode):
    ctx_at = lax.axis_index("ctx").astype(jnp.int32)
    head_at = lax.axis_index("head").astype(jnp.int32)
    flat = ctx_at * 8 + head_at
    tokens = x_tokens.shape[0]
    blocks = tokens // BLOCK
    vmem = pl.BlockSpec(memory_space=pltpu.VMEM)
    smem = pl.BlockSpec(memory_space=pltpu.SMEM)

    bc_flat = bc_tokens.reshape(tokens, 2 * STATE)
    edge = jnp.concatenate(
        [x_tokens[tokens - 3:], bc_tokens[tokens - 3:].reshape(3, 2 * STATE)], 1)
    edge = lax.ppermute(edge, "ctx", [(i, i + 1) for i in range(RANKS - 1)])
    owners = [(16 * g + c, 8 * c + g) for c in range(RANKS) for g in range(8)]
    prior = state_cache[traj_slot[0]].reshape(128, STATE)
    prior = lax.ppermute(prior, ("ctx", "head"), owners)

    traj = row_traj.reshape(1, ROWS)
    here = jnp.reshape(head_at, (1,))
    per_head = [v.reshape(1, -1) for v in (a_log, dt_bias, d_skip)]
    head_specs = [full((1, a_log.shape[0]))] * 3

    rows = lambda width, at=0: pl.BlockSpec((BLOCK, width), lambda b, *_: (b, at))
    times = pl.BlockSpec((1, 2 * SPAN, BLOCK), lambda b, *_: (b, 0, 0))
    xc, car, bc, rdt, send = pl.pallas_call(
        prep_kernel,
        grid_spec=pltpu.PrefetchScalarGridSpec(
            num_scalar_prefetch=1,
            grid=(blocks,),
            in_specs=[rows(WIDTH), rows(2 * STATE), full((3, WIDTH + 2 * STATE)),
                      pl.BlockSpec((SPAN, BLOCK), lambda b, *_: (0, b)), *head_specs,
                      full((4, WIDTH)), full((WIDTH // 128, 128)), full((4, 2, STATE)),
                      full((2, STATE))],
            out_specs=[rows(WIDTH), rows(WIDTH), rows(2 * STATE), times,
                       full((RANKS, STATE + 8, 128))],
            scratch_shapes=[pltpu.VMEM((8, WIDTH), F32), pltpu.VMEM((8, 2 * STATE), F32),
                            pltpu.VMEM((STATE, WIDTH), F32), pltpu.VMEM((SPAN, BLOCK), F32),
                            pltpu.VMEM((2 * SPAN, WIDTH), BF16), pltpu.VMEM((SPAN, 8), F32),
                            pltpu.VMEM((8, WIDTH), F32), pltpu.VMEM((8, 2 * STATE), F32)],
        ),
        out_shape=[
            jax.ShapeDtypeStruct((tokens, WIDTH), BF16),
            jax.ShapeDtypeStruct((tokens, WIDTH), BF16),
            jax.ShapeDtypeStruct((tokens, 2 * STATE), BF16),
            jax.ShapeDtypeStruct((blocks, 2 * SPAN, BLOCK), F32),
            jax.ShapeDtypeStruct((RANKS, STATE + 8, 128), F32),
        ],
        compiler_params=params(),
        cost_estimate=cost(8 * 10**9, 20 * 2**20),
        name="prep",
    )(here, x_tokens, bc_flat, edge, dt_tokens.T, *per_head, conv_x, bias_x.reshape(-1, 128),
      conv_bc.reshape(4, 2, STATE), bias_bc.reshape(2, STATE))

    got = lax.all_to_all(send, "ctx", 0, 0)

    yl = pl.pallas_call(
        inner_kernel,
        grid_spec=pltpu.PrefetchScalarGridSpec(
            num_scalar_prefetch=1,
            grid=(blocks,),
            in_specs=[rows(WIDTH), rows(2 * STATE), times, *head_specs],
            out_specs=rows(WIDTH),
            scratch_shapes=[pltpu.VMEM((8, WIDTH), F32)],
        ),
        out_shape=jax.ShapeDtypeStruct((tokens, WIDTH), BF16),
        compiler_params=params(),
        cost_estimate=cost(8 * 10**9, 20 * 2**20),
        name="inner",
    )(here, xc, bc, rdt, *per_head)

    got, yl = lax.optimization_barrier((got, yl))

    lines = ROWS * 16
    at = jnp.stack([flat * 2, ctx_at // 2, head_at])
    whole = full((STEPS, ROWS, 128))
    y_dec, d_dec, reads = pl.pallas_call(
        decode_kernel,
        grid_spec=pltpu.PrefetchScalarGridSpec(
            num_scalar_prefetch=1,
            grid=(STEPS,),
            in_specs=[smem] * 4 + [full(state_cache.reshape(-1, 128, STATE).shape),
                                   pl.BlockSpec((lines, STATE), lambda k, *_: (k, 0)),
                                   whole, full((STEPS, 2, ROWS)), full((1, ROWS))],
            out_specs=[whole, whole, pl.BlockSpec((8, STATE), lambda k, *_: (k, 0))],
            scratch_shapes=[pltpu.VMEM((ROWS, ROWS), BF16)]
            + [pltpu.VMEM((STEPS, ROWS, STATE), BF16)] * 3
            + [pltpu.VMEM((STEPS, ROWS, 128), F32)],
        ),
        out_shape=[jax.ShapeDtypeStruct((STEPS, ROWS, 128), F32)] * 2
        + [jax.ShapeDtypeStruct((8 * STEPS, STATE), F32)],
        compiler_params=params(),
        cost_estimate=cost(2 * 10**9, 6 * 2**20),
        name="decode",
    )(at, a_log, dt_bias, d_skip, traj_slot, state_cache.reshape(-1, 128, STATE),
      bc_decode.reshape(STEPS * lines, STATE), x_decode, jnp.swapaxes(dt_decode, 1, 2), traj)

    some = RANKS // 4
    got_spec = pl.BlockSpec((some, STATE + 8, 128), lambda i: (i, 0, 0))
    first = pl.pallas_call(
        last_kernel,
        grid=(4,),
        in_specs=[got_spec, full((128, STATE)), full((8 * STEPS, STATE))],
        out_specs=full((8 * STEPS, 128)),
        out_shape=jax.ShapeDtypeStruct((8 * STEPS, 128), F32),
        scratch_shapes=[pltpu.VMEM((STATE, 128), F32)],
        compiler_params=params(),
        cost_estimate=cost(10**8, 2 * 2**20),
        name="last",
    )(got, prior, reads)
    enter = pl.pallas_call(
        scan_kernel,
        grid=(4,),
        in_specs=[got_spec, full((128, STATE)), full((8 * STEPS, 128))],
        out_specs=pl.BlockSpec((some, STATE, 128), lambda i: (i, 0, 0)),
        out_shape=jax.ShapeDtypeStruct((RANKS, STATE, 128), F32),
        scratch_shapes=[pltpu.VMEM((STATE, 128), F32)],
        compiler_params=params(),
        cost_estimate=cost(10**8, 4 * 2**20),
        name="scan",
    )(got, prior, first)

    first = lax.ppermute(first, ("ctx", "head"), [(b, a) for a, b in owners])
    enter = lax.all_to_all(enter, "ctx", 0, 0)

    mixed, squares = pl.pallas_call(
        mix_kernel,
        in_specs=[vmem] * 5,
        out_specs=[vmem] * 2,
        out_shape=[jax.ShapeDtypeStruct((STEPS, ROWS, 128), F32),
                   jax.ShapeDtypeStruct((8, ROWS), F32)],
        compiler_params=params(),
        cost_estimate=cost(10**8, 2**20),
        name="mix",
    )(y_dec, d_dec, first, z_decode, traj)

    for away in ((1, 2, 3), (4, 8, 12)):
        squares = squares + sum(
            lax.ppermute(squares, ("ctx", "head"), [(i, i ^ d) for i in range(128)]) for d in away)

    enter, squares = lax.optimization_barrier((enter, squares))
    prefill_out = pl.pallas_call(
        out_kernel,
        grid_spec=pltpu.PrefetchScalarGridSpec(
            num_scalar_prefetch=1,
            grid=(blocks,),
            in_specs=[rows(WIDTH), rows(WIDTH), rows(2 * STATE), times, full((RANKS, STATE, 128)),
                      rows(WIDTH), pl.BlockSpec((1, WIDTH), lambda b, at: (0, at[0]))],
            out_specs=rows(WIDTH),
            scratch_shapes=[pltpu.VMEM((2 * SPAN, WIDTH), BF16), pltpu.VMEM((STATE, WIDTH), F32),
                            pltpu.VMEM((BLOCK, WIDTH), F32)],
        ),
        out_shape=jax.ShapeDtypeStruct((tokens, WIDTH), BF16),
        compiler_params=params(),
        cost_estimate=cost(4 * 10**9, 16 * 2**20),
        name="gate",
    )(here, yl, car, bc, rdt, enter, z_tokens, norm_gain.reshape(1, -1))

    decode_out = pl.pallas_call(
        norm_kernel,
        grid_spec=pltpu.PrefetchScalarGridSpec(
            num_scalar_prefetch=1,
            grid=(1,),
            in_specs=[full((STEPS, ROWS, 128)), full((8, ROWS)),
                      pl.BlockSpec((1, 128), lambda b, at: (0, at[0]))],
            out_specs=full((STEPS, ROWS, 128)),
        ),
        out_shape=jax.ShapeDtypeStruct((STEPS, ROWS, 128), BF16),
        compiler_params=params(),
        cost_estimate=cost(10**7, 2**19),
        name="norm",
    )(jnp.reshape(flat, (1,)), mixed, squares, norm_gain.reshape(1, -1))
    return (prefill_out, decode_out)


def solution(mesh):
    in_specs = (
        P("ctx", "head"),
        P("ctx", None, "head", None),
        P("ctx", "head"),
        P("ctx", "head"),
        P(None, "head"),
        P(None, None, "head", None),
        P("head"),
        P(None, "head", None),
        P(),
        P(),
        P(),
        P(),
        P(None, ("ctx", "head"), None, None),
        P(),
        P(),
        P(None, None, ("ctx", "head")),
        P(),
        P(None, None, ("ctx", "head")),
        P(None, None, ("ctx", "head")),
    )
    out_specs = (P("ctx", "head"), P(None, None, ("ctx", "head")))
    return jax.shard_map(local, mesh=mesh, in_specs=in_specs, out_specs=out_specs, check_vma=False)
```

time: 1220 us -> 146 us (0.12)
  the two profiles are of different devices: /device:TPU:3 before, /device:TPU:0 now
where the time goes in v1:
time: 146 us; the launch traced here: 144 us
  Pallas kernels  64.8 us (44%)
  starting transfers between devices  52.2 us (36%)
  waiting for transfers between devices  17.3 us (12%)
  local copies, waits for them, and re-layouts  7.32 us (5%)
  other arithmetic  1.97 us (1%)
    ppermute x6, starting transfers between devices, local(): lax.ppermute(squares, ('ctx', 'head'), [(i, i ^ d) for i in range(128)])  33.7 us
    pallas_call x1, Pallas kernels, local(): pl.pallas_call(prep_kernel, grid_spec=pltpu.PrefetchScalarGridSpec(num_sc...  20.2 us
    pallas_call x1, Pallas kernels, local(): pl.pallas_call(out_kernel, grid_spec=pltpu.PrefetchScalarGridSpec(num_sca...  14 us
    pallas_call x1, Pallas kernels, local(): pl.pallas_call(inner_kernel, grid_spec=pltpu.PrefetchScalarGridSpec(num_s...  11.3 us
    all_to_all x1, waiting for transfers between devices, local(): got = lax.all_to_all(send, 'ctx', 0, 0)  9.5 us
    ppermute x6, waiting for transfers between devices, local(): lax.ppermute(squares, ('ctx', 'head'), [(i, i ^ d) for i in range(128)])  7.74 us
    pallas_call x1, Pallas kernels, local(): pl.pallas_call(decode_kernel, grid_spec=pltpu.PrefetchScalarGridSpec(num_...  7.5 us
    all_to_all x1, starting transfers between devices, local(): got = lax.all_to_all(send, 'ctx', 0, 0)  7.44 us
  transfers between devices with their start and end apart: 11, of which 5 were waited for; matrix products, arithmetic and copies ran while one was open for 4% of the time, Pallas kernels for 15%

profile of v1, /device:TPU:0, one launch (start us, length us, event | category | flops | bytes accessed | tf_op | source)
XLA Modules:
  0.0 144.5 jit_solution(12994435165213315687)
XLA Ops:
  0.6 0.7 slice_bitcast_fusion
  1.3 0.8 slice.9
  2.1 3.9 %collective-permute-start = (bf16[3,2560]{1,0:T(4,128)(2,1)S(1)}, bf16[3,2560]{1,0:T(4,128)(2,1)S(1)}, u32[]{:S(2)}, u32[]{:S(2)}) collective-permute-start(bf16[3,2560]{1,0:T(4,128)(2,1)S(1)} %pad_maximum_fusion), channel_id=1, source_target_pairs={{0,8},{8,16},{16,24},{24,32},{32,40},{40,48},{48,56},{56,64},{64,7... | collective-permute-start | bytes 46088 | tf_op jit(solution)/shard_map/ppermute | solution.py:361
  6.0 2.4 %copy.21 = bf16[128,8,2,256]{3,1,2,0:T(8,128)(2,1)} copy(bf16[128,8,2,256]{3,2,1,0:T(2,128)(2,1)} %bitcast.28) | data formatting | bytes 2097152
  8.5 0.0 collective-permute-done.edge_ref
  8.5 0.0 copy-start.6
  8.5 0.6 copy-done.6
  9.1 20.2 %prep.1 = (bf16[1024,2048]{1,0:T(8,128)(2,1)}, bf16[1024,2048]{1,0:T(8,128)(2,1)}, bf16[1024,512]{1,0:T(8,128)(2,1)}, f32[8,64,128]{2,1,0:T(8,128)}, f32[16,264,128]{2,1,0:T(8,128)}) custom-call(s32[1]{0:T(128)} %bitcast.at_ref, bf16[1024,2048]{1,0:T(8,128)(2,1)} %x_ref.2, bf16[1024,512]{1,0:T(8,128)(2,1)} %bitcast.29, bf16[3,2560]{1,0:T(4,128)(2,1)} %copy-done.6, ...), custom_call_target="tpu_custom_call" | custom-call | flops 8000000000 | bytes 20971520 | tf_op jit(solution)/shard_map/prep/pallas_call | solution.py:373
  29.3 0.0 copy-start.5
  29.3 7.4 %all-to-all-start = ((f32[16,264,128]{2,1,0:T(8,128)}), f32[16,264,128]{2,1,0:T(8,128)S(1)}, u32[]{:S(2)}, u32[]{:S(2)}) async-start(f32[16,264,128]{2,1,0:T(8,128)} %get-tuple-element.16), calls=%async_computation | async-start | bytes 4325376 | tf_op jit(solution)/shard_map/all_to_all | solution.py:402
  36.8 0.0 copy-done.5
  36.9 0.8 constant_dynamic-slice_fusion
  37.8 0.7 collective-permute-start.1
  38.4 0.7 pad_add_fusion.at_ref
  39.1 7.5 %decode.1 = (f32[4,128,128]{2,1,0:T(8,128)}, f32[4,128,128]{2,1,0:T(8,128)}, f32[32,256]{1,0:T(8,128)}) custom-call(s32[3]{0:T(128)} %pad_add_fusion.at_ref, f32[256]{0:T(256)} %alog_ref.1, f32[256]{0:T(256)} %bias_ref.1, f32[256]{0:T(256)} %skip_ref.1, s32[32]{0:T(128)} %slot_ref.1, bf16[32,128,256]{2,1,0:T(8,128)(2,1)} %bitcast.34, ...), custom_call_target="tpu_custom_call" | custom-call | flops 2000000000 | bytes 6291456 | tf_op jit(solution)/shard_map/decode/pallas_call | solution.py:424
  46.6 11.3 %inner.1.yl_ref = bf16[1024,2048]{1,0:T(8,128)(2,1)} custom-call(s32[1]{0:T(128)} %bitcast.at_ref, bf16[1024,2048]{1,0:T(8,128)(2,1)} %get-tuple-element.17.xc_ref, bf16[1024,512]{1,0:T(8,128)(2,1)} %get-tuple-element.18.bc_ref, f32[8,64,128]{2,1,0:T(8,128)} %get-tuple-element.19.rdt_ref, f32[1,256]{1,0:T(1,128)} %bitcast.47, f32[1,256]{1,0:T(1,128)} %bitcast.49, ...), custom_call_target="tpu_custom_call" | custom-call | flops 8000000000 | bytes 20971520 | tf_op jit(solution)/shard_map/inner/pallas_call | solution.py:404
  57.9 9.5 %all-to-all-done.got_ref = f32[16,264,128]{2,1,0:T(8,128)S(1)} async-done(((f32[16,264,128]{2,1,0:T(8,128)}), f32[16,264,128]{2,1,0:T(8,128)S(1)}, u32[]{:S(2)}, u32[]{:S(2)}) %all-to-all-start) | async-done | bytes 2162720 | tf_op jit(solution)/shard_map/all_to_all | solution.py:402
  67.4 0.0 copy-start
  67.4 0.0 collective-permute-done.1.prior_ref
  67.5 1.3 copy-done
  68.8 0.0 copy-done.2
  68.8 3.2 %last.1.first_ref = f32[32,128]{1,0:T(8,128)} custom-call(f32[16,264,128]{2,1,0:T(8,128)} %copy-done, bf16[128,256]{1,0:T(8,128)(2,1)} %copy-done.2, f32[32,256]{1,0:T(8,128)} %get-tuple-element.23.reads_ref), custom_call_target="tpu_custom_call" | custom-call | flops 100000000 | bytes 2097152 | tf_op jit(solution)/shard_map/last/pallas_call | solution.py:447
  72.0 4.0 %scan.1 = f32[16,256,128]{2,1,0:T(8,128)} custom-call(f32[16,264,128]{2,1,0:T(8,128)} %copy-done, bf16[128,256]{1,0:T(8,128)(2,1)} %copy-done.2, f32[32,128]{1,0:T(8,128)} %last.1.first_ref), custom_call_target="tpu_custom_call" | custom-call | flops 100000000 | bytes 4194304 | tf_op jit(solution)/shard_map/scan/pallas_call | solution.py:458
  76.0 5.8 %all-to-all-start.1 = ((f32[16,256,128]{2,1,0:T(8,128)}), f32[16,256,128]{2,1,0:T(8,128)S(1)}, u32[]{:S(2)}, u32[]{:S(2)}) async-start(f32[16,256,128]{2,1,0:T(8,128)} %scan.1), calls=%async_computation.1 | async-start | bytes 4194304 | tf_op jit(solution)/shard_map/all_to_all | solution.py:471
  81.9 0.0 copy-done.3
  81.9 0.7 collective-permute-start.2
  82.6 0.0 collective-permute-done.2.first_ref
  82.6 0.0 copy-start.4
  82.6 0.6 copy-done.4
  83.2 2.6 %mix.1 = (f32[4,128,128]{2,1,0:T(8,128)}, f32[8,128]{1,0:T(8,128)}) custom-call(f32[4,128,128]{2,1,0:T(8,128)} %get-tuple-element.24.y_ref, f32[4,128,128]{2,1,0:T(8,128)} %get-tuple-element.25.d_ref, f32[32,128]{1,0:T(8,128)} %copy-done.4, bf16[4,128,128]{2,1,0:T(8,128)(2,1)} %z_ref.2, s32[1,128]{1,0:T(1,128)} %bitcast.36), custom_call_target="tpu_custom_call" | custom-call | flops 100000000 | bytes 1048576 | tf_op jit(solution)/shard_map/mix/pallas_call | solution.py:473
  85.8 21.9 %collective-permute-start.5 = (f32[8,128]{1,0:T(8,128)}, f32[8,128]{1,0:T(8,128)S(1)}, u32[]{:S(2)}, u32[]{:S(2)}) collective-permute-start(f32[8,128]{1,0:T(8,128)} %get-tuple-element.26), channel_id=1, source_target_pairs={{0,3},{1,2},{2,1},{3,0},{4,7},{5,6},{6,5},{7,4},{8,11},{9,10},{10,... | collective-permute-start | bytes 12296 | tf_op jit(solution)/shard_map/ppermute | solution.py:486
  107.6 1.8 %collective-permute-start.3 = (f32[8,128]{1,0:T(8,128)}, f32[8,128]{1,0:T(8,128)S(1)}, u32[]{:S(2)}, u32[]{:S(2)}) collective-permute-start(f32[8,128]{1,0:T(8,128)} %get-tuple-element.26), channel_id=1, source_target_pairs={{0,1},{1,0},{2,3},{3,2},{4,5},{5,4},{6,7},{7,6},{8,9},{9,8},{10,11... | collective-permute-start | bytes 12296 | tf_op jit(solution)/shard_map/ppermute | solution.py:486
  109.4 0.0 collective-permute-start.4
  109.4 0.0 collective-permute-done.5
  109.4 1.0 collective-permute-done.3
  110.4 2.8 %collective-permute-done.4 = f32[8,128]{1,0:T(8,128)S(1)} collective-permute-done((f32[8,128]{1,0:T(8,128)}, f32[8,128]{1,0:T(8,128)S(1)}, u32[]{:S(2)}, u32[]{:S(2)}) %collective-permute-start.4) | collective-permute-done | bytes 4128 | tf_op jit(solution)/shard_map/ppermute | solution.py:486
  113.2 0.7 add_add_fusion.1
  113.9 8.9 %collective-permute-start.8 = (f32[8,128]{1,0:T(8,128)S(1)}, f32[8,128]{1,0:T(8,128)S(1)}, u32[]{:S(2)}, u32[]{:S(2)}) collective-permute-start(f32[8,128]{1,0:T(8,128)S(1)} %add_add_fusion.1), channel_id=1, source_target_pairs={{0,12},{1,13},{2,14},{3,15},{4,8},{5,9},{6,10},{7,11},{8,4},{9,5},... | collective-permute-start | bytes 12296 | tf_op jit(solution)/shard_map/ppermute | solution.py:486
  122.8 0.8 collective-permute-start.6
  123.6 0.4 collective-permute-start.7
  124.0 0.4 collective-permute-done.8
  124.4 3.5 %collective-permute-done.6 = f32[8,128]{1,0:T(8,128)S(1)} collective-permute-done((f32[8,128]{1,0:T(8,128)S(1)}, f32[8,128]{1,0:T(8,128)S(1)}, u32[]{:S(2)}, u32[]{:S(2)}) %collective-permute-start.6) | collective-permute-done | bytes 4128 | tf_op jit(solution)/shard_map/ppermute | solution.py:486
  128.0 0.0 collective-permute-done.7
  128.0 0.6 add_add_fusion.sq_ref
  128.6 0.0 all-to-all-done.1.in_ref
  128.6 1.9 %norm.1 = bf16[4,128,128]{2,1,0:T(8,128)(2,1)} custom-call(s32[1]{0:T(128)} %bitcast.17.at_ref, f32[4,128,128]{2,1,0:T(8,128)} %get-tuple-element.28.m_ref, f32[8,128]{1,0:T(8,128)} %add_add_fusion.sq_ref, f32[1,16384]{1,0:T(1,128)} %bitcast.30), custom_call_target="tpu_custom_call" | custom-call | flops 10000000 | bytes 524288 | tf_op jit(solution)/shard_map/norm/pallas_call | solution.py:506
  130.5 0.0 copy-done.1
  130.5 14.0 %gate.1 = bf16[1024,2048]{1,0:T(8,128)(2,1)} custom-call(s32[1]{0:T(128)} %bitcast.at_ref, bf16[1024,2048]{1,0:T(8,128)(2,1)} %inner.1.yl_ref, bf16[1024,2048]{1,0:T(8,128)(2,1)} %get-tuple-element.21.car_ref, bf16[1024,512]{1,0:T(8,128)(2,1)} %get-tuple-element.18.bc_ref, f32[8,64,128]{2,1,0:T(8,128)} %get-tuple-element.19.rdt_ref, ...), custom_call_target="tpu_custom_call" | custom-call | flops 4000000000 | bytes 16777216 | tf_op jit(solution)/shard_map/gate/pallas_call | solution.py:489
  (5 shorter events, 0.0 us)
Async XLA Ops:
  2.1 6.4 %collective-permute-start = (bf16[3,2560]{1,0:T(4,128)(2,1)S(1)}, bf16[3,2560]{1,0:T(4,128)(2,1)S(1)}, u32[]{:S(2)}, u32[]{:S(2)}) collective-permute-start(bf16[3,2560]{1,0:T(4,128)(2,1)S(1)} %pad_maximum_fusion), channel_id=1, source_target_pairs={{0,8},{8,16},{16,24},{24,32},{32,40},{40,48},{48,56},{56,64},{64,7... | collective-permute-start | bytes 46088 | tf_op jit(solution)/shard_map/ppermute | solution.py:361
  8.5 0.6 copy-start.6
  29.3 7.5 %copy-start.5 = (s32[32]{0:T(128)S(1)}, s32[32]{0:T(128)}, u32[]{:S(2)}) copy-start(s32[32]{0:T(128)} %slot_ref.1) | copy-start | bytes 388
  29.3 38.1 %all-to-all-start = ((f32[16,264,128]{2,1,0:T(8,128)}), f32[16,264,128]{2,1,0:T(8,128)S(1)}, u32[]{:S(2)}, u32[]{:S(2)}) async-start(f32[16,264,128]{2,1,0:T(8,128)} %get-tuple-element.16), calls=%async_computation | async-start | bytes 4325376 | tf_op jit(solution)/shard_map/all_to_all | solution.py:402
  37.8 29.7 %collective-permute-start.1 = (bf16[128,256]{1,0:T(8,128)(2,1)S(1)}, bf16[128,256]{1,0:T(8,128)(2,1)S(1)}, u32[]{:S(2)}, u32[]{:S(2)}) collective-permute-start(bf16[128,256]{1,0:T(8,128)(2,1)S(1)} %bitcast.32), channel_id=1, source_target_pairs={{0,0},{16,1},{32,2},{48,3},{64,4},{80,5},{96,6},{112,7},{1,8},{17,... | collective-permute-start | bytes 196616 | tf_op jit(solution)/shard_map/ppermute | solution.py:364
  67.4 1.3 copy-start
  67.5 1.3 copy-start.2
  72.0 9.9 %copy-start.3 = (f32[32,128]{1,0:T(8,128)S(1)}, f32[32,128]{1,0:T(8,128)}, u32[]{:S(2)}) copy-start(f32[32,128]{1,0:T(8,128)} %last.1.first_ref) | copy-start | bytes 49156
  76.0 52.5 %all-to-all-start.1 = ((f32[16,256,128]{2,1,0:T(8,128)}), f32[16,256,128]{2,1,0:T(8,128)S(1)}, u32[]{:S(2)}, u32[]{:S(2)}) async-start(f32[16,256,128]{2,1,0:T(8,128)} %scan.1), calls=%async_computation.1 | async-start | bytes 4194304 | tf_op jit(solution)/shard_map/all_to_all | solution.py:471
  81.9 0.7 collective-permute-start.2
  82.6 0.6 copy-start.4
  85.8 23.6 %collective-permute-start.5 = (f32[8,128]{1,0:T(8,128)}, f32[8,128]{1,0:T(8,128)S(1)}, u32[]{:S(2)}, u32[]{:S(2)}) collective-permute-start(f32[8,128]{1,0:T(8,128)} %get-tuple-element.26), channel_id=1, source_target_pairs={{0,3},{1,2},{2,1},{3,0},{4,7},{5,6},{6,5},{7,4},{8,11},{9,10},{10,... | collective-permute-start | bytes 12296 | tf_op jit(solution)/shard_map/ppermute | solution.py:486
  107.6 2.8 %collective-permute-start.3 = (f32[8,128]{1,0:T(8,128)}, f32[8,128]{1,0:T(8,128)S(1)}, u32[]{:S(2)}, u32[]{:S(2)}) collective-permute-start(f32[8,128]{1,0:T(8,128)} %get-tuple-element.26), channel_id=1, source_target_pairs={{0,1},{1,0},{2,3},{3,2},{4,5},{5,4},{6,7},{7,6},{8,9},{9,8},{10,11... | collective-permute-start | bytes 12296 | tf_op jit(solution)/shard_map/ppermute | solution.py:486
  109.4 3.8 %collective-permute-start.4 = (f32[8,128]{1,0:T(8,128)}, f32[8,128]{1,0:T(8,128)S(1)}, u32[]{:S(2)}, u32[]{:S(2)}) collective-permute-start(f32[8,128]{1,0:T(8,128)} %get-tuple-element.26), channel_id=1, source_target_pairs={{0,2},{1,3},{2,0},{3,1},{4,6},{5,7},{6,4},{7,5},{8,10},{9,11},{10,... | collective-permute-start | bytes 12296 | tf_op jit(solution)/shard_map/ppermute | solution.py:486
  113.9 10.5 %collective-permute-start.8 = (f32[8,128]{1,0:T(8,128)S(1)}, f32[8,128]{1,0:T(8,128)S(1)}, u32[]{:S(2)}, u32[]{:S(2)}) collective-permute-start(f32[8,128]{1,0:T(8,128)S(1)} %add_add_fusion.1), channel_id=1, source_target_pairs={{0,12},{1,13},{2,14},{3,15},{4,8},{5,9},{6,10},{7,11},{8,4},{9,5},... | collective-permute-start | bytes 12296 | tf_op jit(solution)/shard_map/ppermute | solution.py:486
  122.8 5.1 %collective-permute-start.6 = (f32[8,128]{1,0:T(8,128)S(1)}, f32[8,128]{1,0:T(8,128)S(1)}, u32[]{:S(2)}, u32[]{:S(2)}) collective-permute-start(f32[8,128]{1,0:T(8,128)S(1)} %add_add_fusion.1), channel_id=1, source_target_pairs={{0,4},{1,5},{2,6},{3,7},{4,0},{5,1},{6,2},{7,3},{8,12},{9,13},{10,... | collective-permute-start | bytes 12296 | tf_op jit(solution)/shard_map/ppermute | solution.py:486
  123.6 4.3 %collective-permute-start.7 = (f32[8,128]{1,0:T(8,128)S(1)}, f32[8,128]{1,0:T(8,128)S(1)}, u32[]{:S(2)}, u32[]{:S(2)}) collective-permute-start(f32[8,128]{1,0:T(8,128)S(1)} %add_add_fusion.1), channel_id=1, source_target_pairs={{0,8},{1,9},{2,10},{3,11},{4,12},{5,13},{6,14},{7,15},{8,0},{9,1},... | collective-permute-start | bytes 12296 | tf_op jit(solution)/shard_map/ppermute | solution.py:486
  128.6 1.9 %copy-start.1 = (f32[16,256,128]{2,1,0:T(8,128)}, f32[16,256,128]{2,1,0:T(8,128)S(1)}, u32[]{:S(2)}) copy-start(f32[16,256,128]{2,1,0:T(8,128)S(1)} %all-to-all-done.1.in_ref) | copy-start | bytes 6291460

commit v2 on v1

v2 whole, which is shorter than its diff:
```python
import jax
import jax.numpy as jnp
from jax import lax
from jax.experimental import pallas as pl
from jax.experimental.pallas import tpu as pltpu
from jax.sharding import PartitionSpec as P

BLOCK = 128
HEAD = 64
STATE = 256
HEADS = 256
SPAN = 32
WIDTH = SPAN * HEAD
RANKS = 16
ROWS = 128
STEPS = 4
SUBS = 2
QUAD = 256
EPSILON = 1e-05
LOG2E = 1.4426950408889634
F32 = jnp.float32
BF16 = jnp.bfloat16


def dot(a, b, dims=((1,), (0,))):
    return lax.dot_general(a, b, (dims, ((), ())), preferred_element_type=F32)


def halves(v):
    hi = v.astype(BF16)
    return hi, (v - hi.astype(F32)).astype(BF16)


def thirds(v):
    hi, mid = halves(v)
    return hi, mid, (v - hi.astype(F32) - mid.astype(F32)).astype(BF16)


def softplus(v):
    return jnp.maximum(v, 0.0) + jnp.log1p(jnp.exp(-jnp.abs(v)))


def silu(v):
    h = 0.5 * v
    return h + h * jnp.tanh(h)


def iota(shape, dim):
    return lax.broadcasted_iota(jnp.int32, shape, dim)


def fill_expander(ref):
    shape = (2 * SPAN, WIDTH)
    ref[...] = jnp.where(iota(shape, 1) // HEAD == iota(shape, 0) % SPAN, 1.0, 0.0).astype(BF16)


def conv(block, before, taps):
    joined = jnp.concatenate([before, block], 0)
    h = taps[4:5] + taps[0:1] * pltpu.roll(joined, 3, 0)[8:]
    h = h + taps[1:2] * pltpu.roll(joined, 2, 0)[8:]
    h = h + taps[2:3] * pltpu.roll(joined, 1, 0)[8:]
    h = h + taps[3:4] * block
    return (h + h * jnp.tanh(h)).astype(BF16)


def own_heads(head_at, alog_ref, bias_ref, skip_ref):
    rows = jnp.concatenate([alog_ref[...], bias_ref[...]] + [skip_ref[...]] * 6, 0)
    shape = (SPAN, rows.shape[1])
    mine = jnp.where(iota(shape, 1) == iota(shape, 0) + head_at * SPAN, 1.0, 0.0).astype(BF16)
    return sum(dot(mine, piece, ((1,), (1,))) for piece in thirds(rows))


def spread_heads(rows, spread):
    return dot(rows, spread)


def pair_halves(rows):
    return jnp.concatenate(halves(rows), 1)


def prep_kernel(at_ref, x_ref, bc_ref, edge_ref, dt_ref, alog_ref, bias_ref, skip_ref, cw_ref, cb_ref,
                bw_ref, bb_ref, xc_ref, car_ref, bco_ref, bt_ref, rdt_ref, er_ref, send_ref,
                prevx, state, spread, wx, wbc, factors, decays):
    step = pl.program_id(0)
    blocks = rdt_ref.shape[0]

    @pl.when(step == 0)
    def _():
        fill_expander(spread)
        own = own_heads(at_ref[0], alog_ref, bias_ref, skip_ref)
        state[...] = jnp.zeros_like(state)
        wx[0:4, :] = cw_ref[...].astype(F32) * 0.5
        offset = cb_ref[...].astype(F32) * 0.5
        for i in range(WIDTH // 128):
            wx[4:5, i * 128:(i + 1) * 128] = offset[i:i + 1]
        taps = bw_ref[...].astype(F32) * 0.5
        offset = bb_ref[...].astype(F32) * 0.5
        for i in range(2):
            wbc[0:4, i * STATE:(i + 1) * STATE] = taps[:, i, :]
            wbc[4:5, i * STATE:(i + 1) * STATE] = offset[i:i + 1]
        edge = edge_ref[...].astype(F32)
        prevx[...] = jnp.zeros_like(prevx)
        prevx[5:8, :] = edge[:, :WIDTH]
        before = jnp.concatenate([jnp.zeros((5, 2 * STATE), F32), edge[:, WIDTH:]], 0)

        dt = softplus(dt_ref[...] + own[:, 1:2])
        log = dt * (jnp.exp(own[:, 0:1]) * (-LOG2E))
        spans = [slice(b * BLOCK, (b + 1) * BLOCK) for b in range(blocks)]
        dt = jnp.concatenate([dt[:, span] for span in spans], 0)
        log = jnp.concatenate([log[:, span] for span in spans], 0)
        tri = jnp.where(iota((BLOCK, BLOCK), 0) <= iota((BLOCK, BLOCK), 1), 1.0, 0.0).astype(BF16)
        r = sum(dot(piece, tri) for piece in thirds(log))
        r_last = r[:, BLOCK - 1:BLOCK]
        tail = jnp.exp2(r_last - r) * dt
        er = jnp.exp2(r)
        wide = jnp.broadcast_to(r_last, r.shape)
        decay = jnp.exp2(wide)
        whole = jnp.zeros((SPAN, BLOCK), F32)
        for b in range(blocks):
            heads = slice(b * SPAN, (b + 1) * SPAN)
            rdt_ref[b] = jnp.concatenate([r[heads], dt[heads]], 0)
            er_ref[b] = pair_halves(er[heads].T)
            factors[b, 0:BLOCK, :] = pair_halves(tail[heads].T)
            factors[b, BLOCK:, :] = pair_halves(decay[heads].T[:16])
            whole = whole + wide[heads]
        decays[...] = pair_halves(jnp.exp2(whole).T[:16])
        for b in range(blocks):
            bc_in = bc_ref[spans[b], :].astype(F32)
            bc = conv(bc_in, before, wbc[...])
            before = bc_in[BLOCK - 8:]
            bco_ref[spans[b], :] = bc
            bt_ref[b] = bc[:, :STATE].astype(F32).T.astype(BF16)

    for sub in range(x_ref.shape[0] // BLOCK):
        block_at = step * (x_ref.shape[0] // BLOCK) + sub
        span = slice(sub * BLOCK, (sub + 1) * BLOCK)
        b_across = bt_ref[block_at]
        lhs = factors[block_at]
        for q in range(WIDTH // QUAD):
            cols = slice(q * QUAD, (q + 1) * QUAD)
            x_in = x_ref[span, cols].astype(F32)
            xc = conv(x_in, prevx[:, cols], wx[:, cols])
            prevx[:, cols] = x_in[BLOCK - 8:]
            xc_ref[span, cols] = xc
            factor = spread_heads(lhs, spread[:, cols])
            carried = (xc.astype(F32) * factor[:BLOCK]).astype(BF16)
            car_ref[span, cols] = carried
            fresh = dot(b_across, carried)
            state[:, cols] = state[:, cols] * factor[BLOCK:BLOCK + 1] + fresh

    @pl.when(step == pl.num_programs(0) - 1)
    def _():
        rows = spread_heads(decays[...], spread[...])
        for c in range(RANKS):
            cols = slice(c * 128, (c + 1) * 128)
            send_ref[c, 0:STATE, :] = state[:, cols]
            send_ref[c, STATE:, :] = rows[0:8, cols]


def inner_kernel(at_ref, xc_ref, bc_ref, rdt_ref, alog_ref, bias_ref, skip_ref, yl_ref, skip):
    @pl.when(pl.program_id(0) == 0)
    def _():
        spread = jnp.where(
            iota((SPAN, WIDTH), 1) // HEAD == iota((SPAN, WIDTH), 0), 1.0, 0.0).astype(BF16)
        own = own_heads(at_ref[0], alog_ref, bias_ref, skip_ref)
        skip[...] = sum(dot(p, spread, ((0,), (0,))) for p in thirds(own))

    b_now = bc_ref[:, :STATE]
    c_now = bc_ref[:, STATE:]
    scores = dot(c_now, b_now, ((1,), (1,)))
    scores = jnp.where(iota((BLOCK, BLOCK), 1) <= iota((BLOCK, BLOCK), 0), scores, 0.0)
    along = rdt_ref[0]
    r = along.T
    left = iota((BLOCK, 128), 1) < HEAD

    for q in range(WIDTH // QUAD):
        cols = slice(q * QUAD, (q + 1) * QUAD)
        xq = xc_ref[:, cols]
        parts = []
        for pair in range(2):
            weights = []
            for h in (4 * q + 2 * pair, 4 * q + 2 * pair + 1):
                gap = jnp.minimum(r[:, h:h + 1] - along[h:h + 1, :], 0.0)
                weight = jnp.exp2(gap) * (scores * along[SPAN + h:SPAN + h + 1, :])
                weights.append(weight.astype(BF16))
            xp = xq[:, pair * 128:(pair + 1) * 128]
            none = jnp.zeros_like(xp)
            rhs = jnp.concatenate([jnp.where(left, xp, none), jnp.where(left, none, xp)], 0)
            parts.append(dot(jnp.concatenate(weights, 1), rhs))
        out = jnp.concatenate(parts, 1) + skip[2:3, cols] * xq.astype(F32)
        yl_ref[:, cols] = out.astype(BF16)


def chosen_rows(traj):
    hit = jnp.broadcast_to(jnp.where(traj == 0, 1.0, 0.0), (8, ROWS))
    ahead = jnp.where(iota((ROWS, ROWS), 0) < iota((ROWS, ROWS), 1), 1.0, 0.0).astype(BF16)
    rank = dot(hit.astype(BF16), ahead)
    return jnp.where((rank == iota((8, ROWS), 0).astype(F32)) & (hit > 0.5), 1.0, 0.0)


def scan_kernel(got_ref, prior_ref, reads_ref, rows_ref, enter_ref, mixed_ref):
    held = prior_ref[...].astype(F32).T
    for c in range(RANKS):
        enter_ref[c, 0:STATE, :] = held
        held = held * got_ref[c, STATE:STATE + 1, :] + got_ref[c, 0:STATE, :]
    hi, lo = halves(held)
    reads = reads_ref[...].astype(BF16)
    count = 8 * STEPS
    y = rows_ref[0:count] + rows_ref[count:2 * count] * (dot(reads, hi) + dot(reads, lo))
    m = y * rows_ref[2 * count:]
    mixed_ref[...] = m
    sums = row_sums(jnp.concatenate([m * m, jnp.zeros((128 - count, 128), F32)], 0))
    for c in range(RANKS):
        enter_ref[c, STATE:, :] = sums


def row_sums(v):
    ones = jnp.ones((8, v.shape[1]), BF16)
    hi, lo = halves(v)
    return dot(ones, hi, ((1,), (1,))) + dot(ones, lo, ((1,), (1,)))


def scales(sums):
    scale = lax.rsqrt(sums * (1.0 / WIDTH) + EPSILON)
    return jnp.broadcast_to(scale, (128, 128)).T


def rows_kernel(at_ref, sums_ref, mixed_ref, gain_ref, rows_ref):
    total = sums_ref[0]
    for c in range(1, RANKS):
        total = total + sums_ref[c]
    scale = scales(total[0:1])[:8 * STEPS]
    rows_ref[...] = (mixed_ref[...] * scale * gain_ref[...]).astype(BF16)


def out_kernel(at_ref, yl_ref, car_ref, c_ref, bt_ref, er_ref, in_ref, z_ref, gain_ref, out_ref,
               spread, state, mixed):
    @pl.when(pl.program_id(0) == 0)
    def _():
        fill_expander(spread)
        for c in range(RANKS):
            state[:, c * 128:(c + 1) * 128] = in_ref[c, 0:STATE, :]

    subs = yl_ref.shape[0] // BLOCK
    for sub in range(subs):
        span = slice(sub * BLOCK, (sub + 1) * BLOCK)
        b_across = bt_ref[sub]
        c_now = c_ref[span, :]
        factors = er_ref[sub]
        total = jnp.zeros((BLOCK, 128), F32)
        for q in range(WIDTH // QUAD):
            cols = slice(q * QUAD, (q + 1) * QUAD)
            factor = spread_heads(factors, spread[:, cols])
            held = state[:, cols]
            y = yl_ref[span, cols].astype(F32) + dot(c_now, held.astype(BF16)) * factor
            fresh = dot(b_across, car_ref[span, cols])
            state[:, cols] = held * factor[BLOCK - 1:BLOCK] + fresh
            m = y * silu(z_ref[span, cols].astype(F32))
            mixed[span, cols] = m
            sq = m * m
            total = total + sq[:, :128] + sq[:, 128:]
        mean = jnp.sum(total, axis=1, keepdims=True) * (1.0 / WIDTH)
        scale = lax.rsqrt(mean + EPSILON)
        for q in range(WIDTH // QUAD):
            cols = slice(q * QUAD, (q + 1) * QUAD)
            out_ref[span, cols] = (mixed[span, cols] * scale * gain_ref[:, cols]).astype(BF16)


def two_heads(at_ref, ref):
    first = at_ref[0]
    lane = iota((1, 128), 1)
    return jnp.where(lane < HEAD, ref[first], ref[first + 1])


def decode_kernel(at_ref, alog_ref, bias_ref, skip_ref, slot_ref, cache_ref, bc_ref, x_ref, dt_ref,
                  traj_ref, z_ref, m_ref, sq_ref, rows_ref, reads_ref,
                  order, held_b, held_c, sorted_c, reads):
    step = pl.program_id(0)

    @pl.when(step == 0)
    def _():
        traj = jnp.broadcast_to(traj_ref[...].astype(F32), (ROWS, ROWS))
        sub, lane = iota((ROWS, ROWS), 0), iota((ROWS, ROWS), 1)
        rank = jnp.sum(jnp.where((traj == traj.T) & (sub < lane), 1.0, 0.0), axis=0, keepdims=True)
        place = traj_ref[...].astype(F32) * 4.0 + rank
        order[...] = jnp.where(sub.astype(F32) == place, 1.0, 0.0).astype(BF16)

    shape = (96, 512)
    out, line = iota(shape, 0), iota(shape, 1)
    group = jnp.where(out < 64, at_ref[1], at_ref[2])
    wanted = (out % 32) * 16 + jnp.where(out < 32, 0, 8) + group
    pick = jnp.where(line == wanted, 1.0, 0.0).astype(BF16)
    prefill_c = []
    for g in range(ROWS // 32):
        got = dot(pick, bc_ref[g * 512:(g + 1) * 512, :]).astype(BF16)
        held_b[step, g * 32:(g + 1) * 32, :] = got[0:32]
        held_c[step, g * 32:(g + 1) * 32, :] = got[32:64]
        prefill_c.append(got[64:96])
    sorted_c[step] = dot(order[...], held_c[step]).astype(BF16)
    chosen = chosen_rows(traj_ref[...]).astype(BF16)
    reads_ref[...] = dot(chosen, jnp.concatenate(prefill_c, 0))

    @pl.when(step == STEPS - 1)
    def _():
        for g in range(ROWS // 16):
            lhs = jnp.concatenate([sorted_c[k, g * 16:(g + 1) * 16, :] for k in range(STEPS)], 0)
            row = iota((16 * STEPS, 128), 0) % 16 // 4
            out = jnp.zeros((16 * STEPS, 128), F32)
            for i in range(4):
                if g == 0 and i == 0:
                    continue
                got = dot(lhs, cache_ref[slot_ref[4 * g + i]], ((1,), (1,)))
                out = jnp.where(row == i, got, out)
            for k in range(STEPS):
                reads[k, g * 16:(g + 1) * 16, :] = out[k * 16:(k + 1) * 16]

        rate = jnp.exp(two_heads(at_ref, alog_ref)) * (-LOG2E)
        bias = two_heads(at_ref, bias_ref)
        skip = two_heads(at_ref, skip_ref)
        upper = iota((128, ROWS), 0) < HEAD
        sq_ref[...] = jnp.zeros_like(sq_ref)
        total = jnp.ones((ROWS, 128), F32)
        pushed = []
        for k in range(STEPS):
            raw = dt_ref[k]
            dt = softplus(jnp.where(upper, raw[0:1, :], raw[1:2, :]).T + bias)
            x_now = x_ref[k].astype(F32)
            decay = jnp.exp2(dt * rate)
            total = total * decay
            pushed = [p * decay for p in pushed] + [dt * x_now]
            hi, lo = halves(reads[k])
            back = dot(order[...], hi, ((0,), (0,))) + dot(order[...], lo, ((0,), (0,)))
            y = total * back + skip * x_now
            c_now = held_c[k].astype(F32)
            for j in range(k + 1):
                met = jnp.sum(held_b[j].astype(F32) * c_now, axis=1, keepdims=True)
                y = y + pushed[j] * met
            gate = silu(z_ref[k].astype(F32))
            m = y * gate
            m_ref[k] = m
            sq_ref[k:k + 1, :] = row_sums(m * m)[0:1]
            for i, part in enumerate((y, total, gate)):
                hi, lo = halves(part)
                at = 8 * (STEPS * i + k)
                rows_ref[at:at + 8, :] = dot(chosen, hi) + dot(chosen, lo)


def norm_kernel(at_ref, m_ref, sq_ref, rows_ref, traj_ref, gain_ref, out_ref):
    chosen = chosen_rows(traj_ref[...]).astype(BF16)
    first = dot(chosen, jnp.ones((8, 128), BF16), ((0,), (0,))) > 0.5
    for k in range(STEPS):
        out = m_ref[k] * scales(sq_ref[k:k + 1, :]) * gain_ref[...]
        rows = dot(chosen, rows_ref[k * 8:(k + 1) * 8, :].astype(BF16), ((0,), (0,)))
        out_ref[k] = jnp.where(first, rows, out).astype(BF16)


def full(shape):
    return pl.BlockSpec(shape, lambda *_: (0,) * len(shape))


def far(x):
    return pltpu.with_memory_space_constraint(x, pltpu.HBM)


def params(mib=24):
    return pltpu.CompilerParams(vmem_limit_bytes=mib * 2**20)


def cost(flops, nbytes):
    return pl.CostEstimate(flops=flops, bytes_accessed=nbytes, transcendentals=0)


def block_rows(width):
    return pl.BlockSpec((BLOCK, width), lambda b, *_: (b, 0))


def block_times():
    return pl.BlockSpec((1, 2 * SPAN, BLOCK), lambda b, *_: (b, 0, 0))


def prep_call(here, x, *rest):
    tokens = x.shape[0]
    blocks = tokens // BLOCK
    rows = pl.BlockSpec((SUBS * BLOCK, WIDTH), lambda b, *_: (b, 0))
    shapes = [((tokens, WIDTH), BF16), ((tokens, WIDTH), BF16), ((tokens, 2 * STATE), BF16),
              ((blocks, STATE, BLOCK), BF16), ((blocks, 2 * SPAN, BLOCK), F32),
              ((blocks, BLOCK, 2 * SPAN), BF16), ((RANKS, STATE + 8, 128), F32)]
    return pl.pallas_call(
        prep_kernel,
        grid_spec=pltpu.PrefetchScalarGridSpec(
            num_scalar_prefetch=1,
            grid=(blocks // SUBS,),
            in_specs=[rows, full((tokens, 2 * STATE)), full((3, WIDTH + 2 * STATE)),
                      full((SPAN, tokens)), *[full((1, HEADS))] * 3, full((4, WIDTH)),
                      full((WIDTH // 128, 128)), full((4, 2, STATE)), full((2, STATE))],
            out_specs=[rows, rows] + [full(shape) for shape, _ in shapes[2:]],
            scratch_shapes=[pltpu.VMEM((8, WIDTH), F32), pltpu.VMEM((STATE, WIDTH), F32),
                            pltpu.VMEM((2 * SPAN, WIDTH), BF16), pltpu.VMEM((8, WIDTH), F32),
                            pltpu.VMEM((8, 2 * STATE), F32),
                            pltpu.VMEM((blocks, BLOCK + 16, 2 * SPAN), BF16),
                            pltpu.VMEM((16, 2 * SPAN), BF16)],
        ),
        out_shape=[pltpu.HBM(shape, dtype) for shape, dtype in shapes],
        compiler_params=params(),
        cost_estimate=cost(8 * 10**9, 20 * 2**20),
        name="prep",
    )(here, x, *rest)


def inner_call(here, xc, *rest):
    tokens = xc.shape[0]
    blocks = tokens // BLOCK
    rows, times, head_specs = block_rows, block_times(), [full((1, HEADS))] * 3
    return pl.pallas_call(
        inner_kernel,
        grid_spec=pltpu.PrefetchScalarGridSpec(
            num_scalar_prefetch=1,
            grid=(blocks,),
            in_specs=[rows(WIDTH), rows(2 * STATE), times, *head_specs],
            out_specs=rows(WIDTH),
            scratch_shapes=[pltpu.VMEM((8, WIDTH), F32)],
        ),
        out_shape=pltpu.HBM((tokens, WIDTH), BF16),
        compiler_params=params(),
        cost_estimate=cost(8 * 10**9, 20 * 2**20),
        name="inner",
    )(here, xc, *rest)


def gate_call(here, yl, *rest):
    tokens = yl.shape[0]
    rows = pl.BlockSpec((SUBS * BLOCK, WIDTH), lambda b, *_: (b, 0))
    return pl.pallas_call(
        out_kernel,
        grid_spec=pltpu.PrefetchScalarGridSpec(
            num_scalar_prefetch=1,
            grid=(tokens // BLOCK // SUBS,),
            in_specs=[rows, rows, pl.BlockSpec((SUBS * BLOCK, STATE), lambda b, *_: (b, 1)),
                      pl.BlockSpec((SUBS, STATE, BLOCK), lambda b, *_: (b, 0, 0)),
                      pl.BlockSpec((SUBS, BLOCK, 2 * SPAN), lambda b, *_: (b, 0, 0)),
                      full((RANKS, STATE + 8, 128)), rows,
                      pl.BlockSpec((1, WIDTH), lambda b, at: (0, at[0]))],
            out_specs=rows,
            scratch_shapes=[pltpu.VMEM((2 * SPAN, WIDTH), BF16), pltpu.VMEM((STATE, WIDTH), F32),
                            pltpu.VMEM((SUBS * BLOCK, WIDTH), F32)],
        ),
        out_shape=jax.ShapeDtypeStruct((tokens, WIDTH), BF16),
        compiler_params=params(),
        cost_estimate=cost(4 * 10**9, 16 * 2**20),
        name="gate",
    )(here, yl, *rest)


def local(x_tokens, bc_tokens, z_tokens, dt_tokens, conv_x, conv_bc, bias_x, bias_bc, a_log, dt_bias,
          d_skip, norm_gain, state_cache, traj_slot, row_traj, x_decode, bc_decode, z_decode,
          dt_decode):
    ctx_at = lax.axis_index("ctx").astype(jnp.int32)
    head_at = lax.axis_index("head").astype(jnp.int32)
    flat = ctx_at * 8 + head_at
    tokens = x_tokens.shape[0]
    vmem = pl.BlockSpec(memory_space=pltpu.VMEM)
    smem = pl.BlockSpec(memory_space=pltpu.SMEM)

    bc_flat = bc_tokens.reshape(tokens, 2 * STATE)
    edge = jnp.concatenate(
        [x_tokens[tokens - 3:], bc_tokens[tokens - 3:].reshape(3, 2 * STATE)], 1)
    edge = lax.ppermute(edge, "ctx", [(i, i + 1) for i in range(RANKS - 1)])
    owners = [(16 * g + c, 8 * c + g) for c in range(RANKS) for g in range(8)]
    prior = state_cache[traj_slot[0]].reshape(128, STATE)
    prior = lax.ppermute(prior, ("ctx", "head"), owners)

    traj = far(row_traj.reshape(1, ROWS))
    here = jnp.reshape(head_at, (1,))
    per_head = [far(v.reshape(1, -1)) for v in (a_log, dt_bias, d_skip)]

    xc, car, bc, bt, rdt, er, send = prep_call(
        here, far(x_tokens), bc_flat, edge, far(dt_tokens.T), *per_head, far(conv_x),
        far(bias_x.reshape(-1, 128)), far(conv_bc.reshape(4, 2, STATE)),
        far(bias_bc.reshape(2, STATE)))

    got = lax.all_to_all(send, "ctx", 0, 0)

    yl = inner_call(here, far(xc), far(bc), far(rdt), *per_head)

    got, yl = lax.optimization_barrier((got, yl))

    lines = ROWS * 16
    at = jnp.stack([flat * 2, ctx_at // 2, head_at])
    whole = full((STEPS, ROWS, 128))
    mixed, squares, rows_dec, reads = pl.pallas_call(
        decode_kernel,
        grid_spec=pltpu.PrefetchScalarGridSpec(
            num_scalar_prefetch=1,
            grid=(STEPS,),
            in_specs=[smem] * 4 + [full(state_cache.reshape(-1, 128, STATE).shape),
                                   pl.BlockSpec((lines, STATE), lambda k, *_: (k, 0)),
                                   whole, full((STEPS, 2, ROWS)), full((1, ROWS)), whole],
            out_specs=[whole, full((8, ROWS)), full((24 * STEPS, 128)),
                       pl.BlockSpec((8, STATE), lambda k, *_: (k, 0))],
            scratch_shapes=[pltpu.VMEM((ROWS, ROWS), BF16)]
            + [pltpu.VMEM((STEPS, ROWS, STATE), BF16)] * 3
            + [pltpu.VMEM((STEPS, ROWS, 128), F32)],
        ),
        out_shape=[jax.ShapeDtypeStruct((STEPS, ROWS, 128), F32),
                   jax.ShapeDtypeStruct((8, ROWS), F32),
                   jax.ShapeDtypeStruct((24 * STEPS, 128), F32),
                   jax.ShapeDtypeStruct((8 * STEPS, STATE), F32)],
        compiler_params=params(),
        cost_estimate=cost(2 * 10**9, 6 * 2**20),
        name="decode",
    )(at, a_log, dt_bias, d_skip, traj_slot, far(state_cache.reshape(-1, 128, STATE)),
      far(bc_decode.reshape(STEPS * lines, STATE)), far(x_decode),
      far(jnp.swapaxes(dt_decode, 1, 2)), traj, far(z_decode))
    rows_dec = lax.ppermute(rows_dec, ("ctx", "head"), owners)

    enter, first = pl.pallas_call(
        scan_kernel,
        in_specs=[vmem] * 4,
        out_specs=[vmem] * 2,
        out_shape=[pltpu.HBM((RANKS, STATE + 8, 128), F32),
                   jax.ShapeDtypeStruct((8 * STEPS, 128), F32)],
        compiler_params=params(16),
        cost_estimate=cost(10**8, 4 * 2**20),
        name="scan",
    )(got, prior, reads, rows_dec)
    enter = lax.all_to_all(enter, "ctx", 0, 0)

    for away in ((1, 2, 3), (4, 8, 12)):
        squares = squares + sum(
            lax.ppermute(squares, ("ctx", "head"), [(i, i ^ d) for i in range(128)]) for d in away)

    enter, squares = lax.optimization_barrier((enter, squares))
    first = pl.pallas_call(
        rows_kernel,
        grid_spec=pltpu.PrefetchScalarGridSpec(
            num_scalar_prefetch=1,
            grid=(1,),
            in_specs=[pl.BlockSpec((RANKS, 8, 128), lambda b, at: (0, STATE // 8, 0)),
                      full((8 * STEPS, 128)), pl.BlockSpec((1, 128), lambda b, at: (0, at[0]))],
            out_specs=full((8 * STEPS, 128)),
        ),
        out_shape=jax.ShapeDtypeStruct((8 * STEPS, 128), BF16),
        compiler_params=params(),
        cost_estimate=cost(10**7, 2**18),
        name="rows",
    )(jnp.reshape(head_at * RANKS + ctx_at, (1,)), enter, first, far(norm_gain.reshape(1, -1)))
    first = lax.ppermute(first, ("ctx", "head"), [(b, a) for a, b in owners])

    prefill_out = gate_call(here, far(yl), far(car), far(bc), far(bt), far(er), enter, far(z_tokens),
                            far(norm_gain.reshape(1, -1)))

    decode_out = pl.pallas_call(
        norm_kernel,
        grid_spec=pltpu.PrefetchScalarGridSpec(
            num_scalar_prefetch=1,
            grid=(1,),
            in_specs=[full((STEPS, ROWS, 128)), full((8, ROWS)), full((8 * STEPS, 128)),
                      full((1, ROWS)), pl.BlockSpec((1, 128), lambda b, at: (0, at[0]))],
            out_specs=full((STEPS, ROWS, 128)),
        ),
        out_shape=jax.ShapeDtypeStruct((STEPS, ROWS, 128), BF16),
        compiler_params=params(),
        cost_estimate=cost(10**7, 2**19),
        name="norm",
    )(jnp.reshape(flat, (1,)), mixed, squares, first, traj,
      far(norm_gain.reshape(1, -1)))
    return (prefill_out, decode_out)


def solution(mesh):
    in_specs = (
        P("ctx", "head"),
        P("ctx", None, "head", None),
        P("ctx", "head"),
        P("ctx", "head"),
        P(None, "head"),
        P(None, None, "head", None),
        P("head"),
        P(None, "head", None),
        P(),
        P(),
        P(),
        P(),
        P(None, ("ctx", "head"), None, None),
        P(),
        P(),
        P(None, None, ("ctx", "head")),
        P(),
        P(None, None, ("ctx", "head")),
        P(None, None, ("ctx", "head")),
    )
    out_specs = (P("ctx", "head"), P(None, None, ("ctx", "head")))
    return jax.shard_map(local, mesh=mesh, in_specs=in_specs, out_specs=out_specs, check_vma=False)
```

time: 146 us -> 127 us (0.87)
  the two profiles are of different devices: /device:TPU:0 before, /device:TPU:3 now
where the time goes in v2:
time: 127 us; the launch traced here: 126 us
  Pallas kernels  53.1 us (42%)
  starting transfers between devices  47.2 us (37%)
  waiting for transfers between devices  20.7 us (16%)
  local copies, waits for them, and re-layouts  3.79 us (3%)
    pallas_call x1, Pallas kernels, prep_call(): pl.pallas_call(prep_kernel, grid_spec=pltpu.PrefetchScalarGridSpec(num_sc...  18.8 us
    ppermute x6, waiting for transfers between devices, local(): lax.ppermute(squares, ('ctx', 'head'), [(i, i ^ d) for i in range(128)])  16.3 us
    ppermute x1, starting transfers between devices, local(): first = lax.ppermute(first, ('ctx', 'head'), [(b, a) for a, b in owners])  11.9 us
    pallas_call x1, Pallas kernels, inner_call(): pl.pallas_call(inner_kernel, grid_spec=pltpu.PrefetchScalarGridSpec(num_s...  11.3 us
    pallas_call x1, Pallas kernels, gate_call(): pl.pallas_call(out_kernel, grid_spec=pltpu.PrefetchScalarGridSpec(num_sca...  11.3 us
    ppermute x6, starting transfers between devices, local(): lax.ppermute(squares, ('ctx', 'head'), [(i, i ^ d) for i in range(128)])  7.76 us
    pallas_call x1, Pallas kernels, local(): pl.pallas_call(decode_kernel, grid_spec=pltpu.PrefetchScalarGridSpec(num_...  7.32 us
    all_to_all x1, starting transfers between devices, local(): enter = lax.all_to_all(enter, 'ctx', 0, 0)  6.32 us
  transfers between devices with their start and end apart: 12, of which 7 were waited for; matrix products, arithmetic and copies ran while one was open for 2% of the time, Pallas kernels for 24%

profile of v2, /device:TPU:3, one launch (start us, length us, event | category | flops | bytes accessed | tf_op | source)
XLA Modules:
  0.0 125.7 jit_solution(2798232281059447392)
XLA Ops:
  0.6 0.7 slice_bitcast_fusion
  1.3 0.8 slice.9
  2.1 3.5 %collective-permute-start = (bf16[3,2560]{1,0:T(4,128)(2,1)S(1)}, bf16[3,2560]{1,0:T(4,128)(2,1)S(1)}, u32[]{:S(2)}, u32[]{:S(2)}) collective-permute-start(bf16[3,2560]{1,0:T(4,128)(2,1)S(1)} %pad_maximum_fusion), channel_id=1, source_target_pairs={{0,8},{8,16},{16,24},{24,32},{32,40},{40,48},{48,56},{56,64},{64,7... | collective-permute-start | bytes 46088 | tf_op jit(solution)/shard_map/ppermute | solution.py:467
  5.7 1.4 %copy.21 = bf16[128,8,2,256]{3,1,2,0:T(8,128)(2,1)S(1)} copy(bf16[128,8,2,256]{3,2,1,0:T(2,128)(2,1)} %bitcast.39) | data formatting | bytes 2097152
  7.1 1.8 %collective-permute-done.edge_ref = bf16[3,2560]{1,0:T(4,128)(2,1)S(1)} collective-permute-done((bf16[3,2560]{1,0:T(4,128)(2,1)S(1)}, bf16[3,2560]{1,0:T(4,128)(2,1)S(1)}, u32[]{:S(2)}, u32[]{:S(2)}) %collective-permute-start) | collective-permute-done | bytes 15392 | tf_op jit(solution)/shard_map/ppermute | solution.py:467
  8.9 18.8 %prep.1 = (bf16[1024,2048]{1,0:T(8,128)(2,1)}, bf16[1024,2048]{1,0:T(8,128)(2,1)}, bf16[1024,512]{1,0:T(8,128)(2,1)}, bf16[8,256,128]{2,1,0:T(8,128)(2,1)}, f32[...) custom-call(s32[1]{0:T(128)} %bitcast.at_ref, bf16[1024,2048]{1,0:T(8,128)(2,1)} %x_ref.2, ...), custom_call_target="tpu_custom_call" | custom-call | flops 8000000000 | bytes 20971520 | tf_op jit(solution)/shard_map/prep/pallas_call | solution.py:388
  27.7 0.0 copy-start
  27.7 0.0 copy-start.1
  27.7 0.0 copy-start.2
  27.8 0.0 copy-start.3
  27.8 5.7 %all-to-all-start = ((f32[16,264,128]{2,1,0:T(8,128)}), f32[16,264,128]{2,1,0:T(8,128)S(1)}, u32[]{:S(2)}, u32[]{:S(2)}) async-start(f32[16,264,128]{2,1,0:T(8,128)} %get-tuple-element.19), calls=%async_computation | async-start | bytes 4325376 | tf_op jit(solution)/shard_map/all_to_all | solution.py:481
  33.5 0.0 copy-done
  33.6 0.8 constant_dynamic-slice_fusion
  34.4 6.3 %collective-permute-start.1 = (bf16[128,256]{1,0:T(8,128)(2,1)S(1)}, bf16[128,256]{1,0:T(8,128)(2,1)S(1)}, u32[]{:S(2)}, u32[]{:S(2)}) collective-permute-start(bf16[128,256]{1,0:T(8,128)(2,1)S(1)} %bitcast.43), channel_id=1, source_target_pairs={{0,0},{16,1},{32,2},{48,3},{64,4},{80,5},{96,6},{112,7},{1,8},{17,... | collective-permute-start | bytes 196616 | tf_op jit(solution)/shard_map/ppermute | solution.py:470
  40.7 0.1 pad_add_fusion.at_ref
  40.8 0.0 copy-done.1
  40.8 0.0 copy-done.2
  40.8 0.0 copy-done.3
  40.8 7.3 %decode.1 = (f32[4,128,128]{2,1,0:T(8,128)S(1)}, f32[8,128]{1,0:T(8,128)S(1)}, f32[96,128]{1,0:T(8,128)S(1)}, f32[32,256]{1,0:T(8,128)S(1)}) custom-call(s32[3]{0:T(128)S(1)} %pad_add_fusion.at_ref, f32[256]{0:T(256)S(1)} %copy-done.1, f32[256]{0:T(256)S(1)} %copy-done.2, f32[256]{0:T(256)S(1)} %copy-done.3, s32[32]{0:T(128)S(1)} %copy-done, ...), custom_call_target="tpu_custom_call" | custom-call | flops 2000000000 | bytes 6291456 | tf_op jit(solution)/shard_map/decode/pallas_call | solution.py:490
  48.2 5.7 %collective-permute-start.2 = (f32[96,128]{1,0:T(8,128)S(1)}, f32[96,128]{1,0:T(8,128)S(1)}, u32[]{:S(2)}, u32[]{:S(2)}) collective-permute-start(f32[96,128]{1,0:T(8,128)S(1)} %get-tuple-element.29), channel_id=1, source_target_pairs={{0,0},{16,1},{32,2},{48,3},{64,4},{80,5},{96,6},{112,7},{1,8},{17,... | collective-permute-start | bytes 147464 | tf_op jit(solution)/shard_map/ppermute | solution.py:514
  53.8 11.3 %inner.1.yl_ref = bf16[1024,2048]{1,0:T(8,128)(2,1)} custom-call(s32[1]{0:T(128)} %bitcast.at_ref, bf16[1024,2048]{1,0:T(8,128)(2,1)} %get-tuple-element.20.xc_ref, bf16[1024,512]{1,0:T(8,128)(2,1)} %get-tuple-element.21.bc_ref.c_ref, f32[8,64,128]{2,1,0:T(8,128)} %get-tuple-element.22.rdt_ref, f32[1,256]{1,0:T(1,128)} %bitcast.34, f32[1,256]{1,0:T(1,128)} %bitcast.36, ...), custom_call_target="tpu_custom_call" | custom-call | flops 8000000000 | bytes 20971520 | tf_op jit(solution)/shard_map/inner/pallas_call | solution.py:414
  65.2 0.0 all-to-all-done.got_ref
  65.2 1.7 %collective-permute-done.2.rows_ref = f32[96,128]{1,0:T(8,128)S(1)} collective-permute-done((f32[96,128]{1,0:T(8,128)S(1)}, f32[96,128]{1,0:T(8,128)S(1)}, u32[]{:S(2)}, u32[]{:S(2)}) %collective-permute-start.2) | collective-permute-done | bytes 49184 | tf_op jit(solution)/shard_map/ppermute | solution.py:514
  66.9 0.0 collective-permute-done.1.prior_ref
  66.9 1.9 %scan.1 = (f32[16,264,128]{2,1,0:T(8,128)}, f32[32,128]{1,0:T(8,128)S(1)}) custom-call(f32[16,264,128]{2,1,0:T(8,128)S(1)} %all-to-all-done.got_ref, bf16[128,256]{1,0:T(8,128)(2,1)S(1)} %collective-permute-done.1.prior_ref, f32[32,256]{1,0:T(8,128)S(1)} %get-tuple-element.28.reads_ref, f32[96,128]{1,0:T(8,128)S(1)} %collective-permute-done.2.rows_ref), custom_call_target="tpu_custom_call" | custom-call | flops 100000000 | bytes 4194304 | tf_op jit(solution)/shard_map/scan/pallas_call | solution.py:516
  68.8 6.3 %all-to-all-start.1 = ((f32[16,264,128]{2,1,0:T(8,128)}), f32[16,264,128]{2,1,0:T(8,128)S(1)}, u32[]{:S(2)}, u32[]{:S(2)}) async-start(f32[16,264,128]{2,1,0:T(8,128)} %get-tuple-element.30), calls=%async_computation.1 | async-start | bytes 4325376 | tf_op jit(solution)/shard_map/all_to_all | solution.py:526
  75.1 0.0 collective-permute-start.5
  75.1 2.3 %collective-permute-start.3 = (f32[8,128]{1,0:T(8,128)S(1)}, f32[8,128]{1,0:T(8,128)S(1)}, u32[]{:S(2)}, u32[]{:S(2)}) collective-permute-start(f32[8,128]{1,0:T(8,128)S(1)} %get-tuple-element.31), channel_id=1, source_target_pairs={{0,1},{1,0},{2,3},{3,2},{4,5},{5,4},{6,7},{7,6},{8,9},{9,8},{10,11... | collective-permute-start | bytes 12296 | tf_op jit(solution)/shard_map/ppermute | solution.py:530
  77.5 1.3 %collective-permute-start.4 = (f32[8,128]{1,0:T(8,128)S(1)}, f32[8,128]{1,0:T(8,128)S(1)}, u32[]{:S(2)}, u32[]{:S(2)}) collective-permute-start(f32[8,128]{1,0:T(8,128)S(1)} %get-tuple-element.31), channel_id=1, source_target_pairs={{0,2},{1,3},{2,0},{3,1},{4,6},{5,7},{6,4},{7,5},{8,10},{9,11},{10,... | collective-permute-start | bytes 12296 | tf_op jit(solution)/shard_map/ppermute | solution.py:530
  78.7 0.0 collective-permute-done.5
  78.7 0.0 collective-permute-done.3
  78.7 1.5 %collective-permute-done.4 = f32[8,128]{1,0:T(8,128)S(1)} collective-permute-done((f32[8,128]{1,0:T(8,128)S(1)}, f32[8,128]{1,0:T(8,128)S(1)}, u32[]{:S(2)}, u32[]{:S(2)}) %collective-permute-start.4) | collective-permute-done | bytes 4128 | tf_op jit(solution)/shard_map/ppermute | solution.py:530
  80.2 1.0 collective-permute-start.8
  81.3 2.8 %collective-permute-start.6 = (f32[8,128]{1,0:T(8,128)S(1)}, f32[8,128]{1,0:T(8,128)S(1)}, u32[]{:S(2)}, u32[]{:S(2)}) collective-permute-start(f32[8,128]{1,0:T(8,128)S(1)} %add_add_fusion.1), channel_id=1, source_target_pairs={{0,4},{1,5},{2,6},{3,7},{4,0},{5,1},{6,2},{7,3},{8,12},{9,13},{10,... | collective-permute-start | bytes 12296 | tf_op jit(solution)/shard_map/ppermute | solution.py:530
  84.1 0.3 collective-permute-start.7
  84.4 1.0 collective-permute-done.8
  85.4 0.1 collective-permute-done.6
  85.5 13.7 %collective-permute-done.7 = f32[8,128]{1,0:T(8,128)S(1)} collective-permute-done((f32[8,128]{1,0:T(8,128)S(1)}, f32[8,128]{1,0:T(8,128)S(1)}, u32[]{:S(2)}, u32[]{:S(2)}) %collective-permute-start.7) | collective-permute-done | bytes 4128 | tf_op jit(solution)/shard_map/ppermute | solution.py:530
  99.2 0.9 all-to-all-done.1.in_ref.sums_ref
  100.1 0.7 rows.1
  100.8 11.9 %collective-permute-start.9 = (bf16[32,128]{1,0:T(8,128)(2,1)S(1)}, bf16[32,128]{1,0:T(8,128)(2,1)S(1)}, u32[]{:S(2)}, u32[]{:S(2)}) collective-permute-start(bf16[32,128]{1,0:T(8,128)(2,1)S(1)} %rows.1), channel_id=1, source_target_pairs={{0,0},{1,16},{2,32},{3,48},{4,64},{5,80},{6,96},{7,112},{8,1},{9,1... | collective-permute-start | bytes 24584 | tf_op jit(solution)/shard_map/ppermute | solution.py:547
  112.7 11.3 %gate.1 = bf16[1024,2048]{1,0:T(8,128)(2,1)} custom-call(s32[1]{0:T(128)} %bitcast.at_ref, bf16[1024,2048]{1,0:T(8,128)(2,1)} %inner.1.yl_ref, bf16[1024,2048]{1,0:T(8,128)(2,1)} %get-tuple-element.24.car_ref, bf16[1024,512]{1,0:T(8,128)(2,1)} %get-tuple-element.21.bc_ref.c_ref, bf16[8,256,128]{2,1,0:T(8,128)(2,1)} %get-tuple-element.25.bt_ref, ...), custom_call_target="tpu_custom_call" | custom-call | flops 4000000000 | bytes 16777216 | tf_op jit(solution)/shard_map/gate/pallas_call | solution.py:433
  124.0 0.0 collective-permute-done.9.rows_ref
  124.0 1.7 %norm.1 = bf16[4,128,128]{2,1,0:T(8,128)(2,1)} custom-call(s32[1]{0:T(128)} %bitcast.17.at_ref, f32[4,128,128]{2,1,0:T(8,128)S(1)} %get-tuple-element.33.m_ref, f32[8,128]{1,0:T(8,128)S(1)} %add_add_fusion.sq_ref, bf16[32,128]{1,0:T(8,128)(2,1)S(1)} %collective-permute-done.9.rows_ref, s32[1,128]{1,0:T(1,128)} %bitcast.47, f32[1,16384]{1,0:T(1,128)} %bitcast.42), custom_call_target="tpu_custom_call" | custom-call | flops 10000000 | bytes 524288 | tf_op jit(solution)/shard_map/norm/pallas_call | solution.py:552
  (4 shorter events, 0.0 us)
Async XLA Ops:
  2.1 6.8 %collective-permute-start = (bf16[3,2560]{1,0:T(4,128)(2,1)S(1)}, bf16[3,2560]{1,0:T(4,128)(2,1)S(1)}, u32[]{:S(2)}, u32[]{:S(2)}) collective-permute-start(bf16[3,2560]{1,0:T(4,128)(2,1)S(1)} %pad_maximum_fusion), channel_id=1, source_target_pairs={{0,8},{8,16},{16,24},{24,32},{32,40},{40,48},{48,56},{56,64},{64,7... | collective-permute-start | bytes 46088 | tf_op jit(solution)/shard_map/ppermute | solution.py:467
  27.7 5.7 %copy-start = (s32[32]{0:T(128)S(1)}, s32[32]{0:T(128)}, u32[]{:S(2)}) copy-start(s32[32]{0:T(128)} %slot_ref.1) | copy-start | bytes 388
  27.7 13.1 %copy-start.1 = (f32[256]{0:T(256)S(1)}, f32[256]{0:T(256)}, u32[]{:S(2)}) copy-start(f32[256]{0:T(256)} %alog_ref.1) | copy-start | bytes 3076
  27.7 13.1 %copy-start.2 = (f32[256]{0:T(256)S(1)}, f32[256]{0:T(256)}, u32[]{:S(2)}) copy-start(f32[256]{0:T(256)} %bias_ref.1) | copy-start | bytes 3076
  27.8 13.1 %copy-start.3 = (f32[256]{0:T(256)S(1)}, f32[256]{0:T(256)}, u32[]{:S(2)}) copy-start(f32[256]{0:T(256)} %skip_ref.1) | copy-start | bytes 3076
  27.8 37.4 %all-to-all-start = ((f32[16,264,128]{2,1,0:T(8,128)}), f32[16,264,128]{2,1,0:T(8,128)S(1)}, u32[]{:S(2)}, u32[]{:S(2)}) async-start(f32[16,264,128]{2,1,0:T(8,128)} %get-tuple-element.19), calls=%async_computation | async-start | bytes 4325376 | tf_op jit(solution)/shard_map/all_to_all | solution.py:481
  34.4 32.5 %collective-permute-start.1 = (bf16[128,256]{1,0:T(8,128)(2,1)S(1)}, bf16[128,256]{1,0:T(8,128)(2,1)S(1)}, u32[]{:S(2)}, u32[]{:S(2)}) collective-permute-start(bf16[128,256]{1,0:T(8,128)(2,1)S(1)} %bitcast.43), channel_id=1, source_target_pairs={{0,0},{16,1},{32,2},{48,3},{64,4},{80,5},{96,6},{112,7},{1,8},{17,... | collective-permute-start | bytes 196616 | tf_op jit(solution)/shard_map/ppermute | solution.py:470
  48.2 18.7 %collective-permute-start.2 = (f32[96,128]{1,0:T(8,128)S(1)}, f32[96,128]{1,0:T(8,128)S(1)}, u32[]{:S(2)}, u32[]{:S(2)}) collective-permute-start(f32[96,128]{1,0:T(8,128)S(1)} %get-tuple-element.29), channel_id=1, source_target_pairs={{0,0},{16,1},{32,2},{48,3},{64,4},{80,5},{96,6},{112,7},{1,8},{17,... | collective-permute-start | bytes 147464 | tf_op jit(solution)/shard_map/ppermute | solution.py:514
  68.8 31.3 %all-to-all-start.1 = ((f32[16,264,128]{2,1,0:T(8,128)}), f32[16,264,128]{2,1,0:T(8,128)S(1)}, u32[]{:S(2)}, u32[]{:S(2)}) async-start(f32[16,264,128]{2,1,0:T(8,128)} %get-tuple-element.30), calls=%async_computation.1 | async-start | bytes 4325376 | tf_op jit(solution)/shard_map/all_to_all | solution.py:526
  75.1 3.6 %collective-permute-start.5 = (f32[8,128]{1,0:T(8,128)S(1)}, f32[8,128]{1,0:T(8,128)S(1)}, u32[]{:S(2)}, u32[]{:S(2)}) collective-permute-start(f32[8,128]{1,0:T(8,128)S(1)} %get-tuple-element.31), channel_id=1, source_target_pairs={{0,3},{1,2},{2,1},{3,0},{4,7},{5,6},{6,5},{7,4},{8,11},{9,10},{10,... | collective-permute-start | bytes 12296 | tf_op jit(solution)/shard_map/ppermute | solution.py:530
  75.1 3.6 %collective-permute-start.3 = (f32[8,128]{1,0:T(8,128)S(1)}, f32[8,128]{1,0:T(8,128)S(1)}, u32[]{:S(2)}, u32[]{:S(2)}) collective-permute-start(f32[8,128]{1,0:T(8,128)S(1)} %get-tuple-element.31), channel_id=1, source_target_pairs={{0,1},{1,0},{2,3},{3,2},{4,5},{5,4},{6,7},{7,6},{8,9},{9,8},{10,11... | collective-permute-start | bytes 12296 | tf_op jit(solution)/shard_map/ppermute | solution.py:530
  77.5 2.8 %collective-permute-start.4 = (f32[8,128]{1,0:T(8,128)S(1)}, f32[8,128]{1,0:T(8,128)S(1)}, u32[]{:S(2)}, u32[]{:S(2)}) collective-permute-start(f32[8,128]{1,0:T(8,128)S(1)} %get-tuple-element.31), channel_id=1, source_target_pairs={{0,2},{1,3},{2,0},{3,1},{4,6},{5,7},{6,4},{7,5},{8,10},{9,11},{10,... | collective-permute-start | bytes 12296 | tf_op jit(solution)/shard_map/ppermute | solution.py:530
  80.2 5.2 %collective-permute-start.8 = (f32[8,128]{1,0:T(8,128)S(1)}, f32[8,128]{1,0:T(8,128)S(1)}, u32[]{:S(2)}, u32[]{:S(2)}) collective-permute-start(f32[8,128]{1,0:T(8,128)S(1)} %add_add_fusion.1), channel_id=1, source_target_pairs={{0,12},{1,13},{2,14},{3,15},{4,8},{5,9},{6,10},{7,11},{8,4},{9,5},... | collective-permute-start | bytes 12296 | tf_op jit(solution)/shard_map/ppermute | solution.py:530
  81.3 4.3 %collective-permute-start.6 = (f32[8,128]{1,0:T(8,128)S(1)}, f32[8,128]{1,0:T(8,128)S(1)}, u32[]{:S(2)}, u32[]{:S(2)}) collective-permute-start(f32[8,128]{1,0:T(8,128)S(1)} %add_add_fusion.1), channel_id=1, source_target_pairs={{0,4},{1,5},{2,6},{3,7},{4,0},{5,1},{6,2},{7,3},{8,12},{9,13},{10,... | collective-permute-start | bytes 12296 | tf_op jit(solution)/shard_map/ppermute | solution.py:530
  84.1 15.1 %collective-permute-start.7 = (f32[8,128]{1,0:T(8,128)S(1)}, f32[8,128]{1,0:T(8,128)S(1)}, u32[]{:S(2)}, u32[]{:S(2)}) collective-permute-start(f32[8,128]{1,0:T(8,128)S(1)} %add_add_fusion.1), channel_id=1, source_target_pairs={{0,8},{1,9},{2,10},{3,11},{4,12},{5,13},{6,14},{7,15},{8,0},{9,1},... | collective-permute-start | bytes 12296 | tf_op jit(solution)/shard_map/ppermute | solution.py:530
  100.8 23.2 %collective-permute-start.9 = (bf16[32,128]{1,0:T(8,128)(2,1)S(1)}, bf16[32,128]{1,0:T(8,128)(2,1)S(1)}, u32[]{:S(2)}, u32[]{:S(2)}) collective-permute-start(bf16[32,128]{1,0:T(8,128)(2,1)S(1)} %rows.1), channel_id=1, source_target_pairs={{0,0},{1,16},{2,32},{3,48},{4,64},{5,80},{6,96},{7,112},{8,1},{9,1... | collective-permute-start | bytes 24584 | tf_op jit(solution)/shard_map/ppermute | solution.py:547

commit v3 on v2

--- a/solution.py
+++ b/solution.py
@@ -56,10 +56,10 @@
 
 def conv(block, before, taps):
     joined = jnp.concatenate([before, block], 0)
-    h = taps[4:5] + taps[0:1] * pltpu.roll(joined, 3, 0)[8:]
-    h = h + taps[1:2] * pltpu.roll(joined, 2, 0)[8:]
-    h = h + taps[2:3] * pltpu.roll(joined, 1, 0)[8:]
-    h = h + taps[3:4] * block
+    late = pltpu.roll(joined, 1, 0)
+    older = taps[1:2] * joined + taps[0:1] * late
+    h = taps[4:5] + pltpu.roll(older, 2, 0)[8:]
+    h = h + taps[2:3] * late[8:] + taps[3:4] * block
     return (h + h * jnp.tanh(h)).astype(BF16)
 
 
@@ -72,6 +72,14 @@
 
 def spread_heads(rows, spread):
     return dot(rows, spread)
+
+
+def over_channels(rows, q):
+    left = iota((rows.shape[0], 128), 1) < HEAD
+    first = q * QUAD // HEAD
+    return jnp.concatenate(
+        [jnp.where(left, rows[:, h:h + 1], rows[:, h + 1:h + 2])
+         for h in range(first, first + QUAD // HEAD, 2)], 1)
 
 
 def pair_halves(rows):
@@ -120,10 +128,12 @@
             heads = slice(b * SPAN, (b + 1) * SPAN)
             rdt_ref[b] = jnp.concatenate([r[heads], dt[heads]], 0)
             er_ref[b] = pair_halves(er[heads].T)
-            factors[b, 0:BLOCK, :] = pair_halves(tail[heads].T)
-            factors[b, BLOCK:, :] = pair_halves(decay[heads].T[:16])
+            factors[b] = tail[heads].T
+            rows = spread_heads(pair_halves(decay[heads].T[:16]), spread[...])
+            decays[b:b + 1, :] = rows[0:1]
             whole = whole + wide[heads]
-        decays[...] = pair_halves(jnp.exp2(whole).T[:16])
+        rows = spread_heads(pair_halves(jnp.exp2(whole).T[:16]), spread[...])
+        decays[blocks:blocks + 8, :] = rows[0:8]
         for b in range(blocks):
             bc_in = bc_ref[spans[b], :].astype(F32)
             bc = conv(bc_in, before, wbc[...])
@@ -142,19 +152,17 @@
             xc = conv(x_in, prevx[:, cols], wx[:, cols])
             prevx[:, cols] = x_in[BLOCK - 8:]
             xc_ref[span, cols] = xc
-            factor = spread_heads(lhs, spread[:, cols])
-            carried = (xc.astype(F32) * factor[:BLOCK]).astype(BF16)
+            carried = (xc.astype(F32) * over_channels(lhs, q)).astype(BF16)
             car_ref[span, cols] = carried
             fresh = dot(b_across, carried)
-            state[:, cols] = state[:, cols] * factor[BLOCK:BLOCK + 1] + fresh
+            state[:, cols] = state[:, cols] * decays[pl.ds(block_at, 1), cols] + fresh
 
     @pl.when(step == pl.num_programs(0) - 1)
     def _():
-        rows = spread_heads(decays[...], spread[...])
         for c in range(RANKS):
             cols = slice(c * 128, (c + 1) * 128)
             send_ref[c, 0:STATE, :] = state[:, cols]
-            send_ref[c, STATE:, :] = rows[0:8, cols]
+            send_ref[c, STATE:, :] = decays[blocks:blocks + 8, cols]
 
 
 def inner_kernel(at_ref, xc_ref, bc_ref, rdt_ref, alog_ref, bias_ref, skip_ref, yl_ref, skip):
@@ -242,28 +250,27 @@
             state[:, c * 128:(c + 1) * 128] = in_ref[c, 0:STATE, :]
 
     subs = yl_ref.shape[0] // BLOCK
-    for sub in range(subs):
+    scale = None
+    for sub in range(subs + 1):
         span = slice(sub * BLOCK, (sub + 1) * BLOCK)
-        b_across = bt_ref[sub]
-        c_now = c_ref[span, :]
-        factors = er_ref[sub]
+        done = slice((sub - 1) * BLOCK, sub * BLOCK)
         total = jnp.zeros((BLOCK, 128), F32)
         for q in range(WIDTH // QUAD):
             cols = slice(q * QUAD, (q + 1) * QUAD)
-            factor = spread_heads(factors, spread[:, cols])
-            held = state[:, cols]
-            y = yl_ref[span, cols].astype(F32) + dot(c_now, held.astype(BF16)) * factor
-            fresh = dot(b_across, car_ref[span, cols])
-            state[:, cols] = held * factor[BLOCK - 1:BLOCK] + fresh
-            m = y * silu(z_ref[span, cols].astype(F32))
-            mixed[span, cols] = m
-            sq = m * m
-            total = total + sq[:, :128] + sq[:, 128:]
+            if sub < subs:
+                factor = spread_heads(er_ref[sub], spread[:, cols])
+                held = state[:, cols]
+                y = yl_ref[span, cols].astype(F32) + dot(c_ref[span, :], held.astype(BF16)) * factor
+                fresh = dot(bt_ref[sub], car_ref[span, cols])
+                state[:, cols] = held * factor[BLOCK - 1:BLOCK] + fresh
+                m = y * silu(z_ref[span, cols].astype(F32))
+                mixed[span, cols] = m
+                sq = m * m
+                total = total + sum(sq[:, i:i + 128] for i in range(0, QUAD, 128))
+            if sub > 0:
+                out_ref[done, cols] = (mixed[done, cols] * scale * gain_ref[:, cols]).astype(BF16)
         mean = jnp.sum(total, axis=1, keepdims=True) * (1.0 / WIDTH)
         scale = lax.rsqrt(mean + EPSILON)
-        for q in range(WIDTH // QUAD):
-            cols = slice(q * QUAD, (q + 1) * QUAD)
-            out_ref[span, cols] = (mixed[span, cols] * scale * gain_ref[:, cols]).astype(BF16)
 
 
 def two_heads(at_ref, ref):
@@ -397,8 +404,8 @@
             scratch_shapes=[pltpu.VMEM((8, WIDTH), F32), pltpu.VMEM((STATE, WIDTH), F32),
                             pltpu.VMEM((2 * SPAN, WIDTH), BF16), pltpu.VMEM((8, WIDTH), F32),
                             pltpu.VMEM((8, 2 * STATE), F32),
-                            pltpu.VMEM((blocks, BLOCK + 16, 2 * SPAN), BF16),
-                            pltpu.VMEM((16, 2 * SPAN), BF16)],
+                            pltpu.VMEM((blocks, BLOCK, SPAN), F32),
+                            pltpu.VMEM((blocks + 8, WIDTH), F32)],
         ),
         out_shape=[pltpu.HBM(shape, dtype) for shape, dtype in shapes],
         compiler_params=params(),
@@ -481,7 +488,6 @@
     got = lax.all_to_all(send, "ctx", 0, 0)
 
     yl = inner_call(here, far(xc), far(bc), far(rdt), *per_head)
-
     got, yl = lax.optimization_barrier((got, yl))
 
     lines = ROWS * 16

time: 127 us -> 124 us (0.976)
  Pallas kernels: 53.1 us -> 50.7 us
    pallas_call x1, Pallas kernels: 18.8 us -> 16.3 us  [prep_call(): pl.pallas_call(prep_kernel, grid_spec=pltpu.PrefetchScalarGridSpec(num_sc...]
where the time goes in v3:
time: 124 us; the launch traced here: 123 us
  Pallas kernels  50.7 us (41%)
  starting transfers between devices  47.2 us (38%)
  waiting for transfers between devices  20.7 us (17%)
  local copies, waits for them, and re-layouts  3.79 us (3%)
    pallas_call x1, Pallas kernels, prep_call(): pl.pallas_call(prep_kernel, grid_spec=pltpu.PrefetchScalarGridSpec(num_sc...  16.3 us
    ppermute x6, waiting for transfers between devices, local(): lax.ppermute(squares, ('ctx', 'head'), [(i, i ^ d) for i in range(128)])  16.3 us
    ppermute x1, starting transfers between devices, local(): first = lax.ppermute(first, ('ctx', 'head'), [(b, a) for a, b in owners])  11.9 us
    pallas_call x1, Pallas kernels, gate_call(): pl.pallas_call(out_kernel, grid_spec=pltpu.PrefetchScalarGridSpec(num_sca...  11.4 us
    pallas_call x1, Pallas kernels, inner_call(): pl.pallas_call(inner_kernel, grid_spec=pltpu.PrefetchScalarGridSpec(num_s...  11.3 us
    ppermute x6, starting transfers between devices, local(): lax.ppermute(squares, ('ctx', 'head'), [(i, i ^ d) for i in range(128)])  7.76 us
    pallas_call x1, Pallas kernels, local(): pl.pallas_call(decode_kernel, grid_spec=pltpu.PrefetchScalarGridSpec(num_...  7.31 us
    all_to_all x1, starting transfers between devices, local(): enter = lax.all_to_all(enter, 'ctx', 0, 0)  6.32 us
  transfers between devices with their start and end apart: 12, of which 7 were waited for; matrix products, arithmetic and copies ran while one was open for 2% of the time, Pallas kernels for 24%

profile of v3, /device:TPU:3, one launch (start us, length us, event | category | flops | bytes accessed | tf_op | source)
XLA Modules:
  0.0 123.4 jit_solution(14523471261546025459)
XLA Ops:
  0.6 0.7 slice_bitcast_fusion
  1.3 0.8 slice.9
  2.1 3.5 %collective-permute-start = (bf16[3,2560]{1,0:T(4,128)(2,1)S(1)}, bf16[3,2560]{1,0:T(4,128)(2,1)S(1)}, u32[]{:S(2)}, u32[]{:S(2)}) collective-permute-start(bf16[3,2560]{1,0:T(4,128)(2,1)S(1)} %pad_maximum_fusion), channel_id=1, source_target_pairs={{0,8},{8,16},{16,24},{24,32},{32,40},{40,48},{48,56},{56,64},{64,7... | collective-permute-start | bytes 46088 | tf_op jit(solution)/shard_map/ppermute | solution.py:474
  5.7 1.4 %copy.21 = bf16[128,8,2,256]{3,1,2,0:T(8,128)(2,1)S(1)} copy(bf16[128,8,2,256]{3,2,1,0:T(2,128)(2,1)} %bitcast.39) | data formatting | bytes 2097152
  7.1 1.8 %collective-permute-done.edge_ref = bf16[3,2560]{1,0:T(4,128)(2,1)S(1)} collective-permute-done((bf16[3,2560]{1,0:T(4,128)(2,1)S(1)}, bf16[3,2560]{1,0:T(4,128)(2,1)S(1)}, u32[]{:S(2)}, u32[]{:S(2)}) %collective-permute-start) | collective-permute-done | bytes 15392 | tf_op jit(solution)/shard_map/ppermute | solution.py:474
  8.9 16.3 %prep.1 = (bf16[1024,2048]{1,0:T(8,128)(2,1)}, bf16[1024,2048]{1,0:T(8,128)(2,1)}, bf16[1024,512]{1,0:T(8,128)(2,1)}, bf16[8,256,128]{2,1,0:T(8,128)(2,1)}, f32[...) custom-call(s32[1]{0:T(128)} %bitcast.at_ref, bf16[1024,2048]{1,0:T(8,128)(2,1)} %x_ref.2, ...), custom_call_target="tpu_custom_call" | custom-call | flops 8000000000 | bytes 20971520 | tf_op jit(solution)/shard_map/prep/pallas_call | solution.py:395
  25.3 0.0 copy-start
  25.3 0.0 copy-start.1
  25.3 0.0 copy-start.2
  25.3 0.0 copy-start.3
  25.3 5.7 %all-to-all-start = ((f32[16,264,128]{2,1,0:T(8,128)}), f32[16,264,128]{2,1,0:T(8,128)S(1)}, u32[]{:S(2)}, u32[]{:S(2)}) async-start(f32[16,264,128]{2,1,0:T(8,128)} %get-tuple-element.19), calls=%async_computation | async-start | bytes 4325376 | tf_op jit(solution)/shard_map/all_to_all | solution.py:488
  31.0 0.0 copy-done
  31.1 0.8 constant_dynamic-slice_fusion
  32.0 6.3 %collective-permute-start.1 = (bf16[128,256]{1,0:T(8,128)(2,1)S(1)}, bf16[128,256]{1,0:T(8,128)(2,1)S(1)}, u32[]{:S(2)}, u32[]{:S(2)}) collective-permute-start(bf16[128,256]{1,0:T(8,128)(2,1)S(1)} %bitcast.43), channel_id=1, source_target_pairs={{0,0},{16,1},{32,2},{48,3},{64,4},{80,5},{96,6},{112,7},{1,8},{17,... | collective-permute-start | bytes 196616 | tf_op jit(solution)/shard_map/ppermute | solution.py:477
  38.3 0.1 pad_add_fusion.at_ref
  38.4 0.0 copy-done.1
  38.4 0.0 copy-done.2
  38.4 0.0 copy-done.3
  38.4 7.3 %decode.1 = (f32[4,128,128]{2,1,0:T(8,128)S(1)}, f32[8,128]{1,0:T(8,128)S(1)}, f32[96,128]{1,0:T(8,128)S(1)}, f32[32,256]{1,0:T(8,128)S(1)}) custom-call(s32[3]{0:T(128)S(1)} %pad_add_fusion.at_ref, f32[256]{0:T(256)S(1)} %copy-done.1, f32[256]{0:T(256)S(1)} %copy-done.2, f32[256]{0:T(256)S(1)} %copy-done.3, s32[32]{0:T(128)S(1)} %copy-done, ...), custom_call_target="tpu_custom_call" | custom-call | flops 2000000000 | bytes 6291456 | tf_op jit(solution)/shard_map/decode/pallas_call | solution.py:496
  45.7 5.7 %collective-permute-start.2 = (f32[96,128]{1,0:T(8,128)S(1)}, f32[96,128]{1,0:T(8,128)S(1)}, u32[]{:S(2)}, u32[]{:S(2)}) collective-permute-start(f32[96,128]{1,0:T(8,128)S(1)} %get-tuple-element.29), channel_id=1, source_target_pairs={{0,0},{16,1},{32,2},{48,3},{64,4},{80,5},{96,6},{112,7},{1,8},{17,... | collective-permute-start | bytes 147464 | tf_op jit(solution)/shard_map/ppermute | solution.py:520
  51.4 11.3 %inner.1.yl_ref = bf16[1024,2048]{1,0:T(8,128)(2,1)} custom-call(s32[1]{0:T(128)} %bitcast.at_ref, bf16[1024,2048]{1,0:T(8,128)(2,1)} %get-tuple-element.20.xc_ref, bf16[1024,512]{1,0:T(8,128)(2,1)} %get-tuple-element.21.bc_ref.c_ref, f32[8,64,128]{2,1,0:T(8,128)} %get-tuple-element.22.rdt_ref, f32[1,256]{1,0:T(1,128)} %bitcast.34, f32[1,256]{1,0:T(1,128)} %bitcast.36, ...), custom_call_target="tpu_custom_call" | custom-call | flops 8000000000 | bytes 20971520 | tf_op jit(solution)/shard_map/inner/pallas_call | solution.py:421
  62.7 0.0 all-to-all-done.got_ref
  62.7 1.7 %collective-permute-done.2.rows_ref = f32[96,128]{1,0:T(8,128)S(1)} collective-permute-done((f32[96,128]{1,0:T(8,128)S(1)}, f32[96,128]{1,0:T(8,128)S(1)}, u32[]{:S(2)}, u32[]{:S(2)}) %collective-permute-start.2) | collective-permute-done | bytes 49184 | tf_op jit(solution)/shard_map/ppermute | solution.py:520
  64.4 0.0 collective-permute-done.1.prior_ref
  64.4 1.9 %scan.1 = (f32[16,264,128]{2,1,0:T(8,128)}, f32[32,128]{1,0:T(8,128)S(1)}) custom-call(f32[16,264,128]{2,1,0:T(8,128)S(1)} %all-to-all-done.got_ref, bf16[128,256]{1,0:T(8,128)(2,1)S(1)} %collective-permute-done.1.prior_ref, f32[32,256]{1,0:T(8,128)S(1)} %get-tuple-element.28.reads_ref, f32[96,128]{1,0:T(8,128)S(1)} %collective-permute-done.2.rows_ref), custom_call_target="tpu_custom_call" | custom-call | flops 100000000 | bytes 4194304 | tf_op jit(solution)/shard_map/scan/pallas_call | solution.py:522
  66.3 6.3 %all-to-all-start.1 = ((f32[16,264,128]{2,1,0:T(8,128)}), f32[16,264,128]{2,1,0:T(8,128)S(1)}, u32[]{:S(2)}, u32[]{:S(2)}) async-start(f32[16,264,128]{2,1,0:T(8,128)} %get-tuple-element.30), calls=%async_computation.1 | async-start | bytes 4325376 | tf_op jit(solution)/shard_map/all_to_all | solution.py:532
  72.7 0.0 collective-permute-start.5
  72.7 2.3 %collective-permute-start.3 = (f32[8,128]{1,0:T(8,128)S(1)}, f32[8,128]{1,0:T(8,128)S(1)}, u32[]{:S(2)}, u32[]{:S(2)}) collective-permute-start(f32[8,128]{1,0:T(8,128)S(1)} %get-tuple-element.31), channel_id=1, source_target_pairs={{0,1},{1,0},{2,3},{3,2},{4,5},{5,4},{6,7},{7,6},{8,9},{9,8},{10,11... | collective-permute-start | bytes 12296 | tf_op jit(solution)/shard_map/ppermute | solution.py:536
  75.0 1.3 %collective-permute-start.4 = (f32[8,128]{1,0:T(8,128)S(1)}, f32[8,128]{1,0:T(8,128)S(1)}, u32[]{:S(2)}, u32[]{:S(2)}) collective-permute-start(f32[8,128]{1,0:T(8,128)S(1)} %get-tuple-element.31), channel_id=1, source_target_pairs={{0,2},{1,3},{2,0},{3,1},{4,6},{5,7},{6,4},{7,5},{8,10},{9,11},{10,... | collective-permute-start | bytes 12296 | tf_op jit(solution)/shard_map/ppermute | solution.py:536
  76.3 0.0 collective-permute-done.5
  76.3 0.0 collective-permute-done.3
  76.3 1.5 %collective-permute-done.4 = f32[8,128]{1,0:T(8,128)S(1)} collective-permute-done((f32[8,128]{1,0:T(8,128)S(1)}, f32[8,128]{1,0:T(8,128)S(1)}, u32[]{:S(2)}, u32[]{:S(2)}) %collective-permute-start.4) | collective-permute-done | bytes 4128 | tf_op jit(solution)/shard_map/ppermute | solution.py:536
  77.8 1.0 collective-permute-start.8
  78.8 2.8 %collective-permute-start.6 = (f32[8,128]{1,0:T(8,128)S(1)}, f32[8,128]{1,0:T(8,128)S(1)}, u32[]{:S(2)}, u32[]{:S(2)}) collective-permute-start(f32[8,128]{1,0:T(8,128)S(1)} %add_add_fusion.1), channel_id=1, source_target_pairs={{0,4},{1,5},{2,6},{3,7},{4,0},{5,1},{6,2},{7,3},{8,12},{9,13},{10,... | collective-permute-start | bytes 12296 | tf_op jit(solution)/shard_map/ppermute | solution.py:536
  81.6 0.3 collective-permute-start.7
  81.9 1.0 collective-permute-done.8
  82.9 0.1 collective-permute-done.6
  83.1 13.7 %collective-permute-done.7 = f32[8,128]{1,0:T(8,128)S(1)} collective-permute-done((f32[8,128]{1,0:T(8,128)S(1)}, f32[8,128]{1,0:T(8,128)S(1)}, u32[]{:S(2)}, u32[]{:S(2)}) %collective-permute-start.7) | collective-permute-done | bytes 4128 | tf_op jit(solution)/shard_map/ppermute | solution.py:536
  96.8 0.9 all-to-all-done.1.in_ref.sums_ref
  97.6 0.7 rows.1
  98.4 11.9 %collective-permute-start.9 = (bf16[32,128]{1,0:T(8,128)(2,1)S(1)}, bf16[32,128]{1,0:T(8,128)(2,1)S(1)}, u32[]{:S(2)}, u32[]{:S(2)}) collective-permute-start(bf16[32,128]{1,0:T(8,128)(2,1)S(1)} %rows.1), channel_id=1, source_target_pairs={{0,0},{1,16},{2,32},{3,48},{4,64},{5,80},{6,96},{7,112},{8,1},{9,1... | collective-permute-start | bytes 24584 | tf_op jit(solution)/shard_map/ppermute | solution.py:553
  110.3 11.4 %gate.1 = bf16[1024,2048]{1,0:T(8,128)(2,1)} custom-call(s32[1]{0:T(128)} %bitcast.at_ref, bf16[1024,2048]{1,0:T(8,128)(2,1)} %inner.1.yl_ref, bf16[1024,2048]{1,0:T(8,128)(2,1)} %get-tuple-element.24.car_ref, bf16[1024,512]{1,0:T(8,128)(2,1)} %get-tuple-element.21.bc_ref.c_ref, bf16[8,256,128]{2,1,0:T(8,128)(2,1)} %get-tuple-element.25.bt_ref, ...), custom_call_target="tpu_custom_call" | custom-call | flops 4000000000 | bytes 16777216 | tf_op jit(solution)/shard_map/gate/pallas_call | solution.py:440
  121.7 0.0 collective-permute-done.9.rows_ref
  121.7 1.7 %norm.1 = bf16[4,128,128]{2,1,0:T(8,128)(2,1)} custom-call(s32[1]{0:T(128)} %bitcast.17.at_ref, f32[4,128,128]{2,1,0:T(8,128)S(1)} %get-tuple-element.33.m_ref, f32[8,128]{1,0:T(8,128)S(1)} %add_add_fusion.sq_ref, bf16[32,128]{1,0:T(8,128)(2,1)S(1)} %collective-permute-done.9.rows_ref, s32[1,128]{1,0:T(1,128)} %bitcast.47, f32[1,16384]{1,0:T(1,128)} %bitcast.42), custom_call_target="tpu_custom_call" | custom-call | flops 10000000 | bytes 524288 | tf_op jit(solution)/shard_map/norm/pallas_call | solution.py:558
  (4 shorter events, 0.0 us)
Async XLA Ops:
  2.1 6.8 %collective-permute-start = (bf16[3,2560]{1,0:T(4,128)(2,1)S(1)}, bf16[3,2560]{1,0:T(4,128)(2,1)S(1)}, u32[]{:S(2)}, u32[]{:S(2)}) collective-permute-start(bf16[3,2560]{1,0:T(4,128)(2,1)S(1)} %pad_maximum_fusion), channel_id=1, source_target_pairs={{0,8},{8,16},{16,24},{24,32},{32,40},{40,48},{48,56},{56,64},{64,7... | collective-permute-start | bytes 46088 | tf_op jit(solution)/shard_map/ppermute | solution.py:474
  25.3 5.7 %copy-start = (s32[32]{0:T(128)S(1)}, s32[32]{0:T(128)}, u32[]{:S(2)}) copy-start(s32[32]{0:T(128)} %slot_ref.1) | copy-start | bytes 388
  25.3 13.1 %copy-start.1 = (f32[256]{0:T(256)S(1)}, f32[256]{0:T(256)}, u32[]{:S(2)}) copy-start(f32[256]{0:T(256)} %alog_ref.1) | copy-start | bytes 3076
  25.3 13.1 %copy-start.2 = (f32[256]{0:T(256)S(1)}, f32[256]{0:T(256)}, u32[]{:S(2)}) copy-start(f32[256]{0:T(256)} %bias_ref.1) | copy-start | bytes 3076
  25.3 13.1 %copy-start.3 = (f32[256]{0:T(256)S(1)}, f32[256]{0:T(256)}, u32[]{:S(2)}) copy-start(f32[256]{0:T(256)} %skip_ref.1) | copy-start | bytes 3076
  25.3 37.4 %all-to-all-start = ((f32[16,264,128]{2,1,0:T(8,128)}), f32[16,264,128]{2,1,0:T(8,128)S(1)}, u32[]{:S(2)}, u32[]{:S(2)}) async-start(f32[16,264,128]{2,1,0:T(8,128)} %get-tuple-element.19), calls=%async_computation | async-start | bytes 4325376 | tf_op jit(solution)/shard_map/all_to_all | solution.py:488
  32.0 32.5 %collective-permute-start.1 = (bf16[128,256]{1,0:T(8,128)(2,1)S(1)}, bf16[128,256]{1,0:T(8,128)(2,1)S(1)}, u32[]{:S(2)}, u32[]{:S(2)}) collective-permute-start(bf16[128,256]{1,0:T(8,128)(2,1)S(1)} %bitcast.43), channel_id=1, source_target_pairs={{0,0},{16,1},{32,2},{48,3},{64,4},{80,5},{96,6},{112,7},{1,8},{17,... | collective-permute-start | bytes 196616 | tf_op jit(solution)/shard_map/ppermute | solution.py:477
  45.7 18.7 %collective-permute-start.2 = (f32[96,128]{1,0:T(8,128)S(1)}, f32[96,128]{1,0:T(8,128)S(1)}, u32[]{:S(2)}, u32[]{:S(2)}) collective-permute-start(f32[96,128]{1,0:T(8,128)S(1)} %get-tuple-element.29), channel_id=1, source_target_pairs={{0,0},{16,1},{32,2},{48,3},{64,4},{80,5},{96,6},{112,7},{1,8},{17,... | collective-permute-start | bytes 147464 | tf_op jit(solution)/shard_map/ppermute | solution.py:520
  66.3 31.3 %all-to-all-start.1 = ((f32[16,264,128]{2,1,0:T(8,128)}), f32[16,264,128]{2,1,0:T(8,128)S(1)}, u32[]{:S(2)}, u32[]{:S(2)}) async-start(f32[16,264,128]{2,1,0:T(8,128)} %get-tuple-element.30), calls=%async_computation.1 | async-start | bytes 4325376 | tf_op jit(solution)/shard_map/all_to_all | solution.py:532
  72.7 3.6 %collective-permute-start.5 = (f32[8,128]{1,0:T(8,128)S(1)}, f32[8,128]{1,0:T(8,128)S(1)}, u32[]{:S(2)}, u32[]{:S(2)}) collective-permute-start(f32[8,128]{1,0:T(8,128)S(1)} %get-tuple-element.31), channel_id=1, source_target_pairs={{0,3},{1,2},{2,1},{3,0},{4,7},{5,6},{6,5},{7,4},{8,11},{9,10},{10,... | collective-permute-start | bytes 12296 | tf_op jit(solution)/shard_map/ppermute | solution.py:536
  72.7 3.6 %collective-permute-start.3 = (f32[8,128]{1,0:T(8,128)S(1)}, f32[8,128]{1,0:T(8,128)S(1)}, u32[]{:S(2)}, u32[]{:S(2)}) collective-permute-start(f32[8,128]{1,0:T(8,128)S(1)} %get-tuple-element.31), channel_id=1, source_target_pairs={{0,1},{1,0},{2,3},{3,2},{4,5},{5,4},{6,7},{7,6},{8,9},{9,8},{10,11... | collective-permute-start | bytes 12296 | tf_op jit(solution)/shard_map/ppermute | solution.py:536
  75.0 2.8 %collective-permute-start.4 = (f32[8,128]{1,0:T(8,128)S(1)}, f32[8,128]{1,0:T(8,128)S(1)}, u32[]{:S(2)}, u32[]{:S(2)}) collective-permute-start(f32[8,128]{1,0:T(8,128)S(1)} %get-tuple-element.31), channel_id=1, source_target_pairs={{0,2},{1,3},{2,0},{3,1},{4,6},{5,7},{6,4},{7,5},{8,10},{9,11},{10,... | collective-permute-start | bytes 12296 | tf_op jit(solution)/shard_map/ppermute | solution.py:536
  77.8 5.2 %collective-permute-start.8 = (f32[8,128]{1,0:T(8,128)S(1)}, f32[8,128]{1,0:T(8,128)S(1)}, u32[]{:S(2)}, u32[]{:S(2)}) collective-permute-start(f32[8,128]{1,0:T(8,128)S(1)} %add_add_fusion.1), channel_id=1, source_target_pairs={{0,12},{1,13},{2,14},{3,15},{4,8},{5,9},{6,10},{7,11},{8,4},{9,5},... | collective-permute-start | bytes 12296 | tf_op jit(solution)/shard_map/ppermute | solution.py:536
  78.8 4.3 %collective-permute-start.6 = (f32[8,128]{1,0:T(8,128)S(1)}, f32[8,128]{1,0:T(8,128)S(1)}, u32[]{:S(2)}, u32[]{:S(2)}) collective-permute-start(f32[8,128]{1,0:T(8,128)S(1)} %add_add_fusion.1), channel_id=1, source_target_pairs={{0,4},{1,5},{2,6},{3,7},{4,0},{5,1},{6,2},{7,3},{8,12},{9,13},{10,... | collective-permute-start | bytes 12296 | tf_op jit(solution)/shard_map/ppermute | solution.py:536
  81.6 15.1 %collective-permute-start.7 = (f32[8,128]{1,0:T(8,128)S(1)}, f32[8,128]{1,0:T(8,128)S(1)}, u32[]{:S(2)}, u32[]{:S(2)}) collective-permute-start(f32[8,128]{1,0:T(8,128)S(1)} %add_add_fusion.1), channel_id=1, source_target_pairs={{0,8},{1,9},{2,10},{3,11},{4,12},{5,13},{6,14},{7,15},{8,0},{9,1},... | collective-permute-start | bytes 12296 | tf_op jit(solution)/shard_map/ppermute | solution.py:536
  98.4 23.3 %collective-permute-start.9 = (bf16[32,128]{1,0:T(8,128)(2,1)S(1)}, bf16[32,128]{1,0:T(8,128)(2,1)S(1)}, u32[]{:S(2)}, u32[]{:S(2)}) collective-permute-start(bf16[32,128]{1,0:T(8,128)(2,1)S(1)} %rows.1), channel_id=1, source_target_pairs={{0,0},{1,16},{2,32},{3,48},{4,64},{5,80},{6,96},{7,112},{8,1},{9,1... | collective-permute-start | bytes 24584 | tf_op jit(solution)/shard_map/ppermute | solution.py:553

commit v4 on v3

--- a/solution.py
+++ b/solution.py
@@ -352,13 +352,20 @@
                 rows_ref[at:at + 8, :] = dot(chosen, hi) + dot(chosen, lo)
 
 
-def norm_kernel(at_ref, m_ref, sq_ref, rows_ref, traj_ref, gain_ref, out_ref):
-    chosen = chosen_rows(traj_ref[...]).astype(BF16)
-    first = dot(chosen, jnp.ones((8, 128), BF16), ((0,), (0,))) > 0.5
+def norm_kernel(at_ref, m_ref, sq_ref, traj_ref, gain_ref, out_ref, chosen_ref):
+    chosen = chosen_rows(traj_ref[...])
+    chosen_ref[...] = chosen
+    first = dot(chosen.astype(BF16), jnp.ones((8, 128), BF16), ((0,), (0,))) > 0.5
     for k in range(STEPS):
         out = m_ref[k] * scales(sq_ref[k:k + 1, :]) * gain_ref[...]
+        out_ref[k] = jnp.where(first, 0.0, out).astype(BF16)
+
+
+def patch_kernel(rest_ref, rows_ref, chosen_ref, out_ref):
+    chosen = chosen_ref[...].astype(BF16)
+    for k in range(STEPS):
         rows = dot(chosen, rows_ref[k * 8:(k + 1) * 8, :].astype(BF16), ((0,), (0,)))
-        out_ref[k] = jnp.where(first, rows, out).astype(BF16)
+        out_ref[k] = (rest_ref[k].astype(F32) + rows).astype(BF16)
 
 
 def full(shape):
@@ -473,8 +480,6 @@
         [x_tokens[tokens - 3:], bc_tokens[tokens - 3:].reshape(3, 2 * STATE)], 1)
     edge = lax.ppermute(edge, "ctx", [(i, i + 1) for i in range(RANKS - 1)])
     owners = [(16 * g + c, 8 * c + g) for c in range(RANKS) for g in range(8)]
-    prior = state_cache[traj_slot[0]].reshape(128, STATE)
-    prior = lax.ppermute(prior, ("ctx", "head"), owners)
 
     traj = far(row_traj.reshape(1, ROWS))
     here = jnp.reshape(head_at, (1,))
@@ -517,7 +522,10 @@
     )(at, a_log, dt_bias, d_skip, traj_slot, far(state_cache.reshape(-1, 128, STATE)),
       far(bc_decode.reshape(STEPS * lines, STATE)), far(x_decode),
       far(jnp.swapaxes(dt_decode, 1, 2)), traj, far(z_decode))
+    rows_dec, slots = lax.optimization_barrier((rows_dec, traj_slot))
     rows_dec = lax.ppermute(rows_dec, ("ctx", "head"), owners)
+    prior = state_cache[slots[0]].reshape(128, STATE)
+    prior = lax.ppermute(prior, ("ctx", "head"), owners)
 
     enter, first = pl.pallas_call(
         scan_kernel,
@@ -535,7 +543,22 @@
         squares = squares + sum(
             lax.ppermute(squares, ("ctx", "head"), [(i, i ^ d) for i in range(128)]) for d in away)
 
-    enter, squares = lax.optimization_barrier((enter, squares))
+    rest, chosen = pl.pallas_call(
+        norm_kernel,
+        grid_spec=pltpu.PrefetchScalarGridSpec(
+            num_scalar_prefetch=1,
+            grid=(1,),
+            in_specs=[full((STEPS, ROWS, 128)), full((8, ROWS)), full((1, ROWS)),
+                      pl.BlockSpec((1, 128), lambda b, at: (0, at[0]))],
+            out_specs=[full((STEPS, ROWS, 128)), full((8, ROWS))],
+        ),
+        out_shape=[jax.ShapeDtypeStruct((STEPS, ROWS, 128), BF16),
+                   jax.ShapeDtypeStruct((8, ROWS), F32)],
+        compiler_params=params(),
+        cost_estimate=cost(10**7, 2**19),
+        name="norm",
+    )(jnp.reshape(flat, (1,)), mixed, squares, traj, far(norm_gain.reshape(1, -1)))
+    enter, rest = lax.optimization_barrier((enter, rest))
     first = pl.pallas_call(
         rows_kernel,
         grid_spec=pltpu.PrefetchScalarGridSpec(
@@ -556,20 +579,14 @@
                             far(norm_gain.reshape(1, -1)))
 
     decode_out = pl.pallas_call(
-        norm_kernel,
-        grid_spec=pltpu.PrefetchScalarGridSpec(
-            num_scalar_prefetch=1,
-            grid=(1,),
-            in_specs=[full((STEPS, ROWS, 128)), full((8, ROWS)), full((8 * STEPS, 128)),
-                      full((1, ROWS)), pl.BlockSpec((1, 128), lambda b, at: (0, at[0]))],
-            out_specs=full((STEPS, ROWS, 128)),
-        ),
+        patch_kernel,
+        in_specs=[vmem] * 3,
+        out_specs=vmem,
         out_shape=jax.ShapeDtypeStruct((STEPS, ROWS, 128), BF16),
-        compiler_params=params(),
-        cost_estimate=cost(10**7, 2**19),
-        name="norm",
-    )(jnp.reshape(flat, (1,)), mixed, squares, first, traj,
-      far(norm_gain.reshape(1, -1)))
+        compiler_params=params(16),
+        cost_estimate=cost(10**7, 2**18),
+        name="patch",
+    )(rest, first, chosen)
     return (prefill_out, decode_out)
 
 

time: 124 us -> 123 us (level)
  transfers between devices with their start and end apart: 12 -> 12, of which waited for: 7 -> 6; matrix products, arithmetic and copies ran while one was open for 2% -> 2% of each run, Pallas kernels for 24% -> 25%
where the time goes in v4:
time: 123 us
  Pallas kernels  50.9 us (41%)
  starting transfers between devices  47.1 us (38%)
  waiting for transfers between devices  19.8 us (16%)
  local copies, waits for them, and re-layouts  3.79 us (3%)
    pallas_call x1, Pallas kernels, prep_call(): pl.pallas_call(prep_kernel, grid_spec=pltpu.PrefetchScalarGridSpec(num_sc...  16.4 us
    ppermute x6, waiting for transfers between devices, local(): lax.ppermute(squares, ('ctx', 'head'), [(i, i ^ d) for i in range(128)])  16.3 us
    ppermute x1, starting transfers between devices, local(): first = lax.ppermute(first, ('ctx', 'head'), [(b, a) for a, b in owners])  11.8 us
    pallas_call x1, Pallas kernels, gate_call(): pl.pallas_call(out_kernel, grid_spec=pltpu.PrefetchScalarGridSpec(num_sca...  11.4 us
    pallas_call x1, Pallas kernels, inner_call(): pl.pallas_call(inner_kernel, grid_spec=pltpu.PrefetchScalarGridSpec(num_s...  11.3 us
    ppermute x6, starting transfers between devices, local(): lax.ppermute(squares, ('ctx', 'head'), [(i, i ^ d) for i in range(128)])  7.76 us
    pallas_call x1, Pallas kernels, local(): pl.pallas_call(decode_kernel, grid_spec=pltpu.PrefetchScalarGridSpec(num_...  7.32 us
    all_to_all x1, starting transfers between devices, local(): enter = lax.all_to_all(enter, 'ctx', 0, 0)  6.32 us
  transfers between devices with their start and end apart: 12, of which 6 were waited for; matrix products, arithmetic and copies ran while one was open for 2% of the time, Pallas kernels for 25%

profile of v4, /device:TPU:3, one launch (start us, length us, event | category | flops | bytes accessed | tf_op | source)
XLA Modules:
  0.0 122.6 jit_solution(5234639749049111304)
XLA Ops:
  0.6 0.7 slice_bitcast_fusion
  1.3 0.8 slice.9
  2.1 3.5 %collective-permute-start = (bf16[3,2560]{1,0:T(4,128)(2,1)S(1)}, bf16[3,2560]{1,0:T(4,128)(2,1)S(1)}, u32[]{:S(2)}, u32[]{:S(2)}) collective-permute-start(bf16[3,2560]{1,0:T(4,128)(2,1)S(1)} %pad_maximum_fusion), channel_id=1, source_target_pairs={{0,8},{8,16},{16,24},{24,32},{32,40},{40,48},{48,56},{56,64},{64,7... | collective-permute-start | bytes 46088 | tf_op jit(solution)/shard_map/ppermute | solution.py:481
  5.7 1.4 %copy.21 = bf16[128,8,2,256]{3,1,2,0:T(8,128)(2,1)S(1)} copy(bf16[128,8,2,256]{3,2,1,0:T(2,128)(2,1)} %bitcast.39) | data formatting | bytes 2097152
  7.1 1.8 %collective-permute-done.edge_ref = bf16[3,2560]{1,0:T(4,128)(2,1)S(1)} collective-permute-done((bf16[3,2560]{1,0:T(4,128)(2,1)S(1)}, bf16[3,2560]{1,0:T(4,128)(2,1)S(1)}, u32[]{:S(2)}, u32[]{:S(2)}) %collective-permute-start) | collective-permute-done | bytes 15392 | tf_op jit(solution)/shard_map/ppermute | solution.py:481
  8.9 16.4 %prep.1 = (bf16[1024,2048]{1,0:T(8,128)(2,1)}, bf16[1024,2048]{1,0:T(8,128)(2,1)}, bf16[1024,512]{1,0:T(8,128)(2,1)}, bf16[8,256,128]{2,1,0:T(8,128)(2,1)}, f32[...) custom-call(s32[1]{0:T(128)} %bitcast.at_ref, bf16[1024,2048]{1,0:T(8,128)(2,1)} %x_ref.2, ...), custom_call_target="tpu_custom_call" | custom-call | flops 8000000000 | bytes 20971520 | tf_op jit(solution)/shard_map/prep/pallas_call | solution.py:402
  25.3 0.0 copy-start
  25.3 0.0 copy-start.1
  25.3 0.0 copy-start.2
  25.3 0.0 copy-start.3
  25.3 5.7 %all-to-all-start = ((f32[16,264,128]{2,1,0:T(8,128)}), f32[16,264,128]{2,1,0:T(8,128)S(1)}, u32[]{:S(2)}, u32[]{:S(2)}) async-start(f32[16,264,128]{2,1,0:T(8,128)} %get-tuple-element.23), calls=%async_computation | async-start | bytes 4325376 | tf_op jit(solution)/shard_map/all_to_all | solution.py:493
  31.0 0.1 pad_add_fusion.at_ref
  31.1 0.0 copy-done
  31.1 0.0 copy-done.1
  31.1 0.0 copy-done.2
  31.1 0.0 copy-done.3
  31.1 7.3 %decode.1 = (f32[4,128,128]{2,1,0:T(8,128)S(1)}, f32[8,128]{1,0:T(8,128)S(1)}, f32[96,128]{1,0:T(8,128)S(1)}, f32[32,256]{1,0:T(8,128)S(1)}) custom-call(s32[3]{0:T(128)S(1)} %pad_add_fusion.at_ref, f32[256]{0:T(256)S(1)} %copy-done.1, f32[256]{0:T(256)S(1)} %copy-done.2, f32[256]{0:T(256)S(1)} %copy-done.3, s32[32]{0:T(128)S(1)} %copy-done, ...), custom_call_target="tpu_custom_call" | custom-call | flops 2000000000 | bytes 6291456 | tf_op jit(solution)/shard_map/decode/pallas_call | solution.py:501
  38.6 0.8 constant_dynamic-slice_fusion
  39.4 6.3 %collective-permute-start.1 = (bf16[128,256]{1,0:T(8,128)(2,1)S(1)}, bf16[128,256]{1,0:T(8,128)(2,1)S(1)}, u32[]{:S(2)}, u32[]{:S(2)}) collective-permute-start(bf16[128,256]{1,0:T(8,128)(2,1)S(1)} %bitcast.43), channel_id=1, source_target_pairs={{0,0},{16,1},{32,2},{48,3},{64,4},{80,5},{96,6},{112,7},{1,8},{17,... | collective-permute-start | bytes 196616 | tf_op jit(solution)/shard_map/ppermute | solution.py:528
  45.7 5.7 %collective-permute-start.2 = (f32[96,128]{1,0:T(8,128)S(1)}, f32[96,128]{1,0:T(8,128)S(1)}, u32[]{:S(2)}, u32[]{:S(2)}) collective-permute-start(f32[96,128]{1,0:T(8,128)S(1)} %get-tuple-element.35), channel_id=1, source_target_pairs={{0,0},{16,1},{32,2},{48,3},{64,4},{80,5},{96,6},{112,7},{1,8},{17,... | collective-permute-start | bytes 147464 | tf_op jit(solution)/shard_map/ppermute | solution.py:526
  51.4 11.3 %inner.1.yl_ref = bf16[1024,2048]{1,0:T(8,128)(2,1)} custom-call(s32[1]{0:T(128)} %bitcast.at_ref, bf16[1024,2048]{1,0:T(8,128)(2,1)} %get-tuple-element.24.xc_ref, bf16[1024,512]{1,0:T(8,128)(2,1)} %get-tuple-element.25.bc_ref.c_ref, f32[8,64,128]{2,1,0:T(8,128)} %get-tuple-element.26.rdt_ref, f32[1,256]{1,0:T(1,128)} %bitcast.34, f32[1,256]{1,0:T(1,128)} %bitcast.36, ...), custom_call_target="tpu_custom_call" | custom-call | flops 8000000000 | bytes 20971520 | tf_op jit(solution)/shard_map/inner/pallas_call | solution.py:428
  62.7 0.0 all-to-all-done.got_ref
  62.7 1.7 %collective-permute-done.2.rows_ref = f32[96,128]{1,0:T(8,128)S(1)} collective-permute-done((f32[96,128]{1,0:T(8,128)S(1)}, f32[96,128]{1,0:T(8,128)S(1)}, u32[]{:S(2)}, u32[]{:S(2)}) %collective-permute-start.2) | collective-permute-done | bytes 49184 | tf_op jit(solution)/shard_map/ppermute | solution.py:526
  64.5 0.0 collective-permute-done.1.prior_ref
  64.5 1.9 %scan.1 = (f32[16,264,128]{2,1,0:T(8,128)}, f32[32,128]{1,0:T(8,128)S(1)}) custom-call(f32[16,264,128]{2,1,0:T(8,128)S(1)} %all-to-all-done.got_ref, bf16[128,256]{1,0:T(8,128)(2,1)S(1)} %collective-permute-done.1.prior_ref, f32[32,256]{1,0:T(8,128)S(1)} %get-tuple-element.34.reads_ref, f32[96,128]{1,0:T(8,128)S(1)} %collective-permute-done.2.rows_ref), custom_call_target="tpu_custom_call" | custom-call | flops 100000000 | bytes 4194304 | tf_op jit(solution)/shard_map/scan/pallas_call | solution.py:530
  66.4 6.3 %all-to-all-start.1 = ((f32[16,264,128]{2,1,0:T(8,128)}), f32[16,264,128]{2,1,0:T(8,128)S(1)}, u32[]{:S(2)}, u32[]{:S(2)}) async-start(f32[16,264,128]{2,1,0:T(8,128)} %get-tuple-element.36), calls=%async_computation.1 | async-start | bytes 4325376 | tf_op jit(solution)/shard_map/all_to_all | solution.py:540
  72.7 0.2 collective-permute-start.5
  72.8 2.2 %collective-permute-start.3 = (f32[8,128]{1,0:T(8,128)S(1)}, f32[8,128]{1,0:T(8,128)S(1)}, u32[]{:S(2)}, u32[]{:S(2)}) collective-permute-start(f32[8,128]{1,0:T(8,128)S(1)} %get-tuple-element.38), channel_id=1, source_target_pairs={{0,1},{1,0},{2,3},{3,2},{4,5},{5,4},{6,7},{7,6},{8,9},{9,8},{10,11... | collective-permute-start | bytes 12296 | tf_op jit(solution)/shard_map/ppermute | solution.py:544
  75.0 1.3 %collective-permute-start.4 = (f32[8,128]{1,0:T(8,128)S(1)}, f32[8,128]{1,0:T(8,128)S(1)}, u32[]{:S(2)}, u32[]{:S(2)}) collective-permute-start(f32[8,128]{1,0:T(8,128)S(1)} %get-tuple-element.38), channel_id=1, source_target_pairs={{0,2},{1,3},{2,0},{3,1},{4,6},{5,7},{6,4},{7,5},{8,10},{9,11},{10,... | collective-permute-start | bytes 12296 | tf_op jit(solution)/shard_map/ppermute | solution.py:544
  76.3 0.0 collective-permute-done.5
  76.3 0.0 collective-permute-done.3
  76.3 1.5 %collective-permute-done.4 = f32[8,128]{1,0:T(8,128)S(1)} collective-permute-done((f32[8,128]{1,0:T(8,128)S(1)}, f32[8,128]{1,0:T(8,128)S(1)}, u32[]{:S(2)}, u32[]{:S(2)}) %collective-permute-start.4) | collective-permute-done | bytes 4128 | tf_op jit(solution)/shard_map/ppermute | solution.py:544
  77.8 1.8 %collective-permute-start.8 = (f32[8,128]{1,0:T(8,128)S(1)}, f32[8,128]{1,0:T(8,128)S(1)}, u32[]{:S(2)}, u32[]{:S(2)}) collective-permute-start(f32[8,128]{1,0:T(8,128)S(1)} %add_add_fusion.1), channel_id=1, source_target_pairs={{0,12},{1,13},{2,14},{3,15},{4,8},{5,9},{6,10},{7,11},{8,4},{9,5},... | collective-permute-start | bytes 12296 | tf_op jit(solution)/shard_map/ppermute | solution.py:544
  79.6 2.1 %collective-permute-start.6 = (f32[8,128]{1,0:T(8,128)S(1)}, f32[8,128]{1,0:T(8,128)S(1)}, u32[]{:S(2)}, u32[]{:S(2)}) collective-permute-start(f32[8,128]{1,0:T(8,128)S(1)} %add_add_fusion.1), channel_id=1, source_target_pairs={{0,4},{1,5},{2,6},{3,7},{4,0},{5,1},{6,2},{7,3},{8,12},{9,13},{10,... | collective-permute-start | bytes 12296 | tf_op jit(solution)/shard_map/ppermute | solution.py:544
  81.7 0.3 collective-permute-start.7
  81.9 1.0 collective-permute-done.8
  82.9 0.9 collective-permute-done.6
  83.8 12.9 %collective-permute-done.7 = f32[8,128]{1,0:T(8,128)S(1)} collective-permute-done((f32[8,128]{1,0:T(8,128)S(1)}, f32[8,128]{1,0:T(8,128)S(1)}, u32[]{:S(2)}, u32[]{:S(2)}) %collective-permute-start.7) | collective-permute-done | bytes 4128 | tf_op jit(solution)/shard_map/ppermute | solution.py:544
  96.8 1.0 norm.1
  97.8 0.0 all-to-all-done.1.in_ref.sums_ref
  97.8 0.7 rows.1
  98.5 11.8 %collective-permute-start.9 = (bf16[32,128]{1,0:T(8,128)(2,1)S(1)}, bf16[32,128]{1,0:T(8,128)(2,1)S(1)}, u32[]{:S(2)}, u32[]{:S(2)}) collective-permute-start(bf16[32,128]{1,0:T(8,128)(2,1)S(1)} %rows.1), channel_id=1, source_target_pairs={{0,0},{1,16},{2,32},{3,48},{4,64},{5,80},{6,96},{7,112},{8,1},{9,1... | collective-permute-start | bytes 24584 | tf_op jit(solution)/shard_map/ppermute | solution.py:576
  110.3 11.4 %gate.1 = bf16[1024,2048]{1,0:T(8,128)(2,1)} custom-call(s32[1]{0:T(128)} %bitcast.at_ref, bf16[1024,2048]{1,0:T(8,128)(2,1)} %inner.1.yl_ref, bf16[1024,2048]{1,0:T(8,128)(2,1)} %get-tuple-element.28.car_ref, bf16[1024,512]{1,0:T(8,128)(2,1)} %get-tuple-element.25.bc_ref.c_ref, bf16[8,256,128]{2,1,0:T(8,128)(2,1)} %get-tuple-element.29.bt_ref, ...), custom_call_target="tpu_custom_call" | custom-call | flops 4000000000 | bytes 16777216 | tf_op jit(solution)/shard_map/gate/pallas_call | solution.py:447
  121.7 0.0 collective-permute-done.9.rows_ref
  121.7 0.9 patch.1
  (4 shorter events, 0.0 us)
Async XLA Ops:
  2.1 6.8 %collective-permute-start = (bf16[3,2560]{1,0:T(4,128)(2,1)S(1)}, bf16[3,2560]{1,0:T(4,128)(2,1)S(1)}, u32[]{:S(2)}, u32[]{:S(2)}) collective-permute-start(bf16[3,2560]{1,0:T(4,128)(2,1)S(1)} %pad_maximum_fusion), channel_id=1, source_target_pairs={{0,8},{8,16},{16,24},{24,32},{32,40},{40,48},{48,56},{56,64},{64,7... | collective-permute-start | bytes 46088 | tf_op jit(solution)/shard_map/ppermute | solution.py:481
  25.3 5.8 %copy-start = (s32[32]{0:T(128)S(1)}, s32[32]{0:T(128)}, u32[]{:S(2)}) copy-start(s32[32]{0:T(128)} %slot_ref.1) | copy-start | bytes 388
  25.3 5.8 %copy-start.1 = (f32[256]{0:T(256)S(1)}, f32[256]{0:T(256)}, u32[]{:S(2)}) copy-start(f32[256]{0:T(256)} %alog_ref.1) | copy-start | bytes 3076
  25.3 5.8 %copy-start.2 = (f32[256]{0:T(256)S(1)}, f32[256]{0:T(256)}, u32[]{:S(2)}) copy-start(f32[256]{0:T(256)} %bias_ref.1) | copy-start | bytes 3076
  25.3 5.8 %copy-start.3 = (f32[256]{0:T(256)S(1)}, f32[256]{0:T(256)}, u32[]{:S(2)}) copy-start(f32[256]{0:T(256)} %skip_ref.1) | copy-start | bytes 3076
  25.3 37.4 %all-to-all-start = ((f32[16,264,128]{2,1,0:T(8,128)}), f32[16,264,128]{2,1,0:T(8,128)S(1)}, u32[]{:S(2)}, u32[]{:S(2)}) async-start(f32[16,264,128]{2,1,0:T(8,128)} %get-tuple-element.23), calls=%async_computation | async-start | bytes 4325376 | tf_op jit(solution)/shard_map/all_to_all | solution.py:493
  39.4 25.0 %collective-permute-start.1 = (bf16[128,256]{1,0:T(8,128)(2,1)S(1)}, bf16[128,256]{1,0:T(8,128)(2,1)S(1)}, u32[]{:S(2)}, u32[]{:S(2)}) collective-permute-start(bf16[128,256]{1,0:T(8,128)(2,1)S(1)} %bitcast.43), channel_id=1, source_target_pairs={{0,0},{16,1},{32,2},{48,3},{64,4},{80,5},{96,6},{112,7},{1,8},{17,... | collective-permute-start | bytes 196616 | tf_op jit(solution)/shard_map/ppermute | solution.py:528
  45.7 18.7 %collective-permute-start.2 = (f32[96,128]{1,0:T(8,128)S(1)}, f32[96,128]{1,0:T(8,128)S(1)}, u32[]{:S(2)}, u32[]{:S(2)}) collective-permute-start(f32[96,128]{1,0:T(8,128)S(1)} %get-tuple-element.35), channel_id=1, source_target_pairs={{0,0},{16,1},{32,2},{48,3},{64,4},{80,5},{96,6},{112,7},{1,8},{17,... | collective-permute-start | bytes 147464 | tf_op jit(solution)/shard_map/ppermute | solution.py:526
  66.4 31.4 %all-to-all-start.1 = ((f32[16,264,128]{2,1,0:T(8,128)}), f32[16,264,128]{2,1,0:T(8,128)S(1)}, u32[]{:S(2)}, u32[]{:S(2)}) async-start(f32[16,264,128]{2,1,0:T(8,128)} %get-tuple-element.36), calls=%async_computation.1 | async-start | bytes 4325376 | tf_op jit(solution)/shard_map/all_to_all | solution.py:540
  72.7 3.6 %collective-permute-start.5 = (f32[8,128]{1,0:T(8,128)S(1)}, f32[8,128]{1,0:T(8,128)S(1)}, u32[]{:S(2)}, u32[]{:S(2)}) collective-permute-start(f32[8,128]{1,0:T(8,128)S(1)} %get-tuple-element.38), channel_id=1, source_target_pairs={{0,3},{1,2},{2,1},{3,0},{4,7},{5,6},{6,5},{7,4},{8,11},{9,10},{10,... | collective-permute-start | bytes 12296 | tf_op jit(solution)/shard_map/ppermute | solution.py:544
  72.8 3.5 %collective-permute-start.3 = (f32[8,128]{1,0:T(8,128)S(1)}, f32[8,128]{1,0:T(8,128)S(1)}, u32[]{:S(2)}, u32[]{:S(2)}) collective-permute-start(f32[8,128]{1,0:T(8,128)S(1)} %get-tuple-element.38), channel_id=1, source_target_pairs={{0,1},{1,0},{2,3},{3,2},{4,5},{5,4},{6,7},{7,6},{8,9},{9,8},{10,11... | collective-permute-start | bytes 12296 | tf_op jit(solution)/shard_map/ppermute | solution.py:544
  75.0 2.8 %collective-permute-start.4 = (f32[8,128]{1,0:T(8,128)S(1)}, f32[8,128]{1,0:T(8,128)S(1)}, u32[]{:S(2)}, u32[]{:S(2)}) collective-permute-start(f32[8,128]{1,0:T(8,128)S(1)} %get-tuple-element.38), channel_id=1, source_target_pairs={{0,2},{1,3},{2,0},{3,1},{4,6},{5,7},{6,4},{7,5},{8,10},{9,11},{10,... | collective-permute-start | bytes 12296 | tf_op jit(solution)/shard_map/ppermute | solution.py:544
  77.8 5.2 %collective-permute-start.8 = (f32[8,128]{1,0:T(8,128)S(1)}, f32[8,128]{1,0:T(8,128)S(1)}, u32[]{:S(2)}, u32[]{:S(2)}) collective-permute-start(f32[8,128]{1,0:T(8,128)S(1)} %add_add_fusion.1), channel_id=1, source_target_pairs={{0,12},{1,13},{2,14},{3,15},{4,8},{5,9},{6,10},{7,11},{8,4},{9,5},... | collective-permute-start | bytes 12296 | tf_op jit(solution)/shard_map/ppermute | solution.py:544
  79.6 4.3 %collective-permute-start.6 = (f32[8,128]{1,0:T(8,128)S(1)}, f32[8,128]{1,0:T(8,128)S(1)}, u32[]{:S(2)}, u32[]{:S(2)}) collective-permute-start(f32[8,128]{1,0:T(8,128)S(1)} %add_add_fusion.1), channel_id=1, source_target_pairs={{0,4},{1,5},{2,6},{3,7},{4,0},{5,1},{6,2},{7,3},{8,12},{9,13},{10,... | collective-permute-start | bytes 12296 | tf_op jit(solution)/shard_map/ppermute | solution.py:544
  81.7 15.1 %collective-permute-start.7 = (f32[8,128]{1,0:T(8,128)S(1)}, f32[8,128]{1,0:T(8,128)S(1)}, u32[]{:S(2)}, u32[]{:S(2)}) collective-permute-start(f32[8,128]{1,0:T(8,128)S(1)} %add_add_fusion.1), channel_id=1, source_target_pairs={{0,8},{1,9},{2,10},{3,11},{4,12},{5,13},{6,14},{7,15},{8,0},{9,1},... | collective-permute-start | bytes 12296 | tf_op jit(solution)/shard_map/ppermute | solution.py:544
  98.5 23.2 %collective-permute-start.9 = (bf16[32,128]{1,0:T(8,128)(2,1)S(1)}, bf16[32,128]{1,0:T(8,128)(2,1)S(1)}, u32[]{:S(2)}, u32[]{:S(2)}) collective-permute-start(bf16[32,128]{1,0:T(8,128)(2,1)S(1)} %rows.1), channel_id=1, source_target_pairs={{0,0},{1,16},{2,32},{3,48},{4,64},{5,80},{6,96},{7,112},{8,1},{9,1... | collective-permute-start | bytes 24584 | tf_op jit(solution)/shard_map/ppermute | solution.py:576

commit v5 on v4

--- a/solution.py
+++ b/solution.py
@@ -206,16 +206,17 @@
     return jnp.where((rank == iota((8, ROWS), 0).astype(F32)) & (hit > 0.5), 1.0, 0.0)
 
 
-def scan_kernel(got_ref, prior_ref, reads_ref, rows_ref, enter_ref, mixed_ref):
-    held = prior_ref[...].astype(F32).T
+def scan_kernel(got_ref, sent_ref, reads_ref, enter_ref, mixed_ref):
+    held = sent_ref[0:128, :].astype(F32).T
     for c in range(RANKS):
         enter_ref[c, 0:STATE, :] = held
         held = held * got_ref[c, STATE:STATE + 1, :] + got_ref[c, 0:STATE, :]
     hi, lo = halves(held)
     reads = reads_ref[...].astype(BF16)
     count = 8 * STEPS
-    y = rows_ref[0:count] + rows_ref[count:2 * count] * (dot(reads, hi) + dot(reads, lo))
-    m = y * rows_ref[2 * count:]
+    rows = sent_ref[128:, 0:128].astype(F32) + sent_ref[128:, 128:].astype(F32)
+    y = rows[0:count] + rows[count:2 * count] * (dot(reads, hi) + dot(reads, lo))
+    m = y * rows[2 * count:]
     mixed_ref[...] = m
     sums = row_sums(jnp.concatenate([m * m, jnp.zeros((128 - count, 128), F32)], 0))
     for c in range(RANKS):
@@ -281,7 +282,7 @@
 
 def decode_kernel(at_ref, alog_ref, bias_ref, skip_ref, slot_ref, cache_ref, bc_ref, x_ref, dt_ref,
                   traj_ref, z_ref, m_ref, sq_ref, rows_ref, reads_ref,
-                  order, held_b, held_c, sorted_c, reads):
+                  order, held_b, held_c, sorted_c, reads, kept):
     step = pl.program_id(0)
 
     @pl.when(step == 0)
@@ -349,7 +350,8 @@
             for i, part in enumerate((y, total, gate)):
                 hi, lo = halves(part)
                 at = 8 * (STEPS * i + k)
-                rows_ref[at:at + 8, :] = dot(chosen, hi) + dot(chosen, lo)
+                kept[at:at + 8, :] = dot(chosen, hi) + dot(chosen, lo)
+        rows_ref[...] = pair_halves(kept[...])
 
 
 def norm_kernel(at_ref, m_ref, sq_ref, traj_ref, gain_ref, out_ref, chosen_ref):
@@ -506,15 +508,15 @@
             in_specs=[smem] * 4 + [full(state_cache.reshape(-1, 128, STATE).shape),
                                    pl.BlockSpec((lines, STATE), lambda k, *_: (k, 0)),
                                    whole, full((STEPS, 2, ROWS)), full((1, ROWS)), whole],
-            out_specs=[whole, full((8, ROWS)), full((24 * STEPS, 128)),
+            out_specs=[whole, full((8, ROWS)), full((24 * STEPS, 256)),
                        pl.BlockSpec((8, STATE), lambda k, *_: (k, 0))],
             scratch_shapes=[pltpu.VMEM((ROWS, ROWS), BF16)]
             + [pltpu.VMEM((STEPS, ROWS, STATE), BF16)] * 3
-            + [pltpu.VMEM((STEPS, ROWS, 128), F32)],
+            + [pltpu.VMEM((STEPS, ROWS, 128), F32), pltpu.VMEM((24 * STEPS, 128), F32)],
         ),
         out_shape=[jax.ShapeDtypeStruct((STEPS, ROWS, 128), F32),
                    jax.ShapeDtypeStruct((8, ROWS), F32),
-                   jax.ShapeDtypeStruct((24 * STEPS, 128), F32),
+                   jax.ShapeDtypeStruct((24 * STEPS, 256), BF16),
                    jax.ShapeDtypeStruct((8 * STEPS, STATE), F32)],
         compiler_params=params(),
         cost_estimate=cost(2 * 10**9, 6 * 2**20),
@@ -522,21 +524,19 @@
     )(at, a_log, dt_bias, d_skip, traj_slot, far(state_cache.reshape(-1, 128, STATE)),
       far(bc_decode.reshape(STEPS * lines, STATE)), far(x_decode),
       far(jnp.swapaxes(dt_decode, 1, 2)), traj, far(z_decode))
-    rows_dec, slots = lax.optimization_barrier((rows_dec, traj_slot))
-    rows_dec = lax.ppermute(rows_dec, ("ctx", "head"), owners)
-    prior = state_cache[slots[0]].reshape(128, STATE)
-    prior = lax.ppermute(prior, ("ctx", "head"), owners)
+    prior = state_cache[traj_slot[0]].reshape(128, STATE)
+    sent = lax.ppermute(jnp.concatenate([prior, rows_dec], 0), ("ctx", "head"), owners)
 
     enter, first = pl.pallas_call(
         scan_kernel,
-        in_specs=[vmem] * 4,
+        in_specs=[vmem] * 3,
         out_specs=[vmem] * 2,
         out_shape=[pltpu.HBM((RANKS, STATE + 8, 128), F32),
                    jax.ShapeDtypeStruct((8 * STEPS, 128), F32)],
         compiler_params=params(16),
         cost_estimate=cost(10**8, 4 * 2**20),
         name="scan",
-    )(got, prior, reads, rows_dec)
+    )(got, sent, reads)
     enter = lax.all_to_all(enter, "ctx", 0, 0)
 
     for away in ((1, 2, 3), (4, 8, 12)):

time: 123 us -> 123 us (level)
  starting transfers between devices: 47.1 us -> 40 us
  waiting for transfers between devices: 19.8 us -> 26.1 us
    ppermute x2 -> x1, starting transfers between devices: 12 us -> 6.31 us  [local(): lax.ppermute(jnp.concatenate([prior, rows_dec], 0), ('ctx', 'head'), owners)]
    ppermute x2 -> x1, waiting for transfers between devices: 1.71 us -> 7.35 us  [local(): lax.ppermute(jnp.concatenate([prior, rows_dec], 0), ('ctx', 'head'), owners)]
    ppermute x1, starting transfers between devices: 11.8 us -> 10.4 us  [local(): first = lax.ppermute(first, ('ctx', 'head'), [(b, a) for a, b in owners])]
  transfers between devices with their start and end apart: 12 -> 11, of which waited for: 6 -> 8; matrix products, arithmetic and copies ran while one was open for 2% -> 2% of each run, Pallas kernels for 25% -> 25%
where the time goes in v5:
time: 123 us; the launch traced here: 122 us
  Pallas kernels  50.9 us (41%)
  starting transfers between devices  40 us (33%)
  waiting for transfers between devices  26.1 us (21%)
  local copies, waits for them, and re-layouts  3.79 us (3%)
    ppermute x6, waiting for transfers between devices, local(): lax.ppermute(squares, ('ctx', 'head'), [(i, i ^ d) for i in range(128)])  16.9 us
    pallas_call x1, Pallas kernels, prep_call(): pl.pallas_call(prep_kernel, grid_spec=pltpu.PrefetchScalarGridSpec(num_sc...  16.3 us
    pallas_call x1, Pallas kernels, gate_call(): pl.pallas_call(out_kernel, grid_spec=pltpu.PrefetchScalarGridSpec(num_sca...  11.4 us
    pallas_call x1, Pallas kernels, inner_call(): pl.pallas_call(inner_kernel, grid_spec=pltpu.PrefetchScalarGridSpec(num_s...  11.3 us
    ppermute x1, starting transfers between devices, local(): first = lax.ppermute(first, ('ctx', 'head'), [(b, a) for a, b in owners])  10.4 us
    ppermute x1, waiting for transfers between devices, local(): lax.ppermute(jnp.concatenate([prior, rows_dec], 0), ('ctx', 'head'), owners)  7.35 us
    ppermute x6, starting transfers between devices, local(): lax.ppermute(squares, ('ctx', 'head'), [(i, i ^ d) for i in range(128)])  7.35 us
    pallas_call x1, Pallas kernels, local(): pl.pallas_call(decode_kernel, grid_spec=pltpu.PrefetchScalarGridSpec(num_...  7.33 us
  transfers between devices with their start and end apart: 11, of which 8 were waited for; matrix products, arithmetic and copies ran while one was open for 2% of the time, Pallas kernels for 25%

profile of v5, /device:TPU:3, one launch (start us, length us, event | category | flops | bytes accessed | tf_op | source)
XLA Modules:
  0.0 121.8 jit_solution(10012932639212497076)
XLA Ops:
  0.6 0.7 slice_bitcast_fusion
  1.3 0.8 slice.9
  2.1 3.5 %collective-permute-start = (bf16[3,2560]{1,0:T(4,128)(2,1)S(1)}, bf16[3,2560]{1,0:T(4,128)(2,1)S(1)}, u32[]{:S(2)}, u32[]{:S(2)}) collective-permute-start(bf16[3,2560]{1,0:T(4,128)(2,1)S(1)} %pad_maximum_fusion.1), channel_id=1, source_target_pairs={{0,8},{8,16},{16,24},{24,32},{32,40},{40,48},{48,56},{56,64},{64,7... | collective-permute-start | bytes 46088 | tf_op jit(solution)/shard_map/ppermute | solution.py:483
  5.7 1.4 %copy.21 = bf16[128,8,2,256]{3,1,2,0:T(8,128)(2,1)S(1)} copy(bf16[128,8,2,256]{3,2,1,0:T(2,128)(2,1)} %bitcast.39) | data formatting | bytes 2097152
  7.1 1.8 %collective-permute-done.edge_ref = bf16[3,2560]{1,0:T(4,128)(2,1)S(1)} collective-permute-done((bf16[3,2560]{1,0:T(4,128)(2,1)S(1)}, bf16[3,2560]{1,0:T(4,128)(2,1)S(1)}, u32[]{:S(2)}, u32[]{:S(2)}) %collective-permute-start) | collective-permute-done | bytes 15392 | tf_op jit(solution)/shard_map/ppermute | solution.py:483
  8.9 16.3 %prep.1 = (bf16[1024,2048]{1,0:T(8,128)(2,1)}, bf16[1024,2048]{1,0:T(8,128)(2,1)}, bf16[1024,512]{1,0:T(8,128)(2,1)}, bf16[8,256,128]{2,1,0:T(8,128)(2,1)}, f32[...) custom-call(s32[1]{0:T(128)} %bitcast.at_ref, bf16[1024,2048]{1,0:T(8,128)(2,1)} %x_ref.2, ...), custom_call_target="tpu_custom_call" | custom-call | flops 8000000000 | bytes 20971520 | tf_op jit(solution)/shard_map/prep/pallas_call | solution.py:404
  25.3 0.0 copy-start
  25.3 0.0 copy-start.1
  25.3 0.0 copy-start.2
  25.3 0.0 copy-start.3
  25.3 5.7 %all-to-all-start = ((f32[16,264,128]{2,1,0:T(8,128)}), f32[16,264,128]{2,1,0:T(8,128)S(1)}, u32[]{:S(2)}, u32[]{:S(2)}) async-start(f32[16,264,128]{2,1,0:T(8,128)} %get-tuple-element.21), calls=%async_computation | async-start | bytes 4325376 | tf_op jit(solution)/shard_map/all_to_all | solution.py:495
  31.0 0.0 copy-done
  31.1 0.1 pad_add_fusion.at_ref
  31.2 0.8 constant_dynamic-slice_fusion
  32.1 0.0 copy-done.1
  32.1 0.0 copy-done.2
  32.1 0.0 copy-done.3
  32.1 7.3 %decode.1 = (f32[4,128,128]{2,1,0:T(8,128)S(1)}, f32[8,128]{1,0:T(8,128)S(1)}, bf16[96,256]{1,0:T(8,128)(2,1)S(1)}, f32[32,256]{1,0:T(8,128)S(1)}) custom-call(s32[3]{0:T(128)S(1)} %pad_add_fusion.at_ref, f32[256]{0:T(256)S(1)} %copy-done.1, f32[256]{0:T(256)S(1)} %copy-done.2, f32[256]{0:T(256)S(1)} %copy-done.3, s32[32]{0:T(128)S(1)} %copy-done, ...), custom_call_target="tpu_custom_call" | custom-call | flops 2000000000 | bytes 6291456 | tf_op jit(solution)/shard_map/decode/pallas_call | solution.py:503
  39.4 6.3 %collective-permute-start.1 = (bf16[224,256]{1,0:T(8,128)(2,1)S(1)}, bf16[224,256]{1,0:T(8,128)(2,1)S(1)}, u32[]{:S(2)}, u32[]{:S(2)}) collective-permute-start(bf16[224,256]{1,0:T(8,128)(2,1)S(1)} %pad_maximum_fusion), channel_id=1, source_target_pairs={{0,0},{16,1},{32,2},{48,3},{64,4},{80,5},{96,6},{112,7},{1,8},{17,... | collective-permute-start | bytes 344072 | tf_op jit(solution)/shard_map/ppermute | solution.py:528
  45.7 11.3 %inner.1.yl_ref = bf16[1024,2048]{1,0:T(8,128)(2,1)} custom-call(s32[1]{0:T(128)} %bitcast.at_ref, bf16[1024,2048]{1,0:T(8,128)(2,1)} %get-tuple-element.22.xc_ref, bf16[1024,512]{1,0:T(8,128)(2,1)} %get-tuple-element.23.bc_ref.c_ref, f32[8,64,128]{2,1,0:T(8,128)} %get-tuple-element.24.rdt_ref, f32[1,256]{1,0:T(1,128)} %bitcast.34, f32[1,256]{1,0:T(1,128)} %bitcast.36, ...), custom_call_target="tpu_custom_call" | custom-call | flops 8000000000 | bytes 20971520 | tf_op jit(solution)/shard_map/inner/pallas_call | solution.py:430
  57.1 0.0 all-to-all-done.got_ref
  57.1 7.3 %collective-permute-done.1.sent_ref = bf16[224,256]{1,0:T(8,128)(2,1)S(1)} collective-permute-done((bf16[224,256]{1,0:T(8,128)(2,1)S(1)}, bf16[224,256]{1,0:T(8,128)(2,1)S(1)}, u32[]{:S(2)}, u32[]{:S(2)}) %collective-permute-start.1) | collective-permute-done | bytes 114720 | tf_op jit(solution)/shard_map/ppermute | solution.py:528
  64.4 1.9 %scan.1 = (f32[16,264,128]{2,1,0:T(8,128)}, f32[32,128]{1,0:T(8,128)S(1)}) custom-call(f32[16,264,128]{2,1,0:T(8,128)S(1)} %all-to-all-done.got_ref, bf16[224,256]{1,0:T(8,128)(2,1)S(1)} %collective-permute-done.1.sent_ref, f32[32,256]{1,0:T(8,128)S(1)} %get-tuple-element.31.reads_ref), custom_call_target="tpu_custom_call" | custom-call | flops 100000000 | bytes 4194304 | tf_op jit(solution)/shard_map/scan/pallas_call | solution.py:530
  66.3 6.7 %all-to-all-start.1 = ((f32[16,264,128]{2,1,0:T(8,128)}), f32[16,264,128]{2,1,0:T(8,128)S(1)}, u32[]{:S(2)}, u32[]{:S(2)}) async-start(f32[16,264,128]{2,1,0:T(8,128)} %get-tuple-element.32), calls=%async_computation.1 | async-start | bytes 4325376 | tf_op jit(solution)/shard_map/all_to_all | solution.py:540
  73.1 0.0 collective-permute-start.4
  73.1 1.9 %collective-permute-start.2 = (f32[8,128]{1,0:T(8,128)S(1)}, f32[8,128]{1,0:T(8,128)S(1)}, u32[]{:S(2)}, u32[]{:S(2)}) collective-permute-start(f32[8,128]{1,0:T(8,128)S(1)} %get-tuple-element.34), channel_id=1, source_target_pairs={{0,1},{1,0},{2,3},{3,2},{4,5},{5,4},{6,7},{7,6},{8,9},{9,8},{10,11... | collective-permute-start | bytes 12296 | tf_op jit(solution)/shard_map/ppermute | solution.py:544
  75.0 1.3 %collective-permute-start.3 = (f32[8,128]{1,0:T(8,128)S(1)}, f32[8,128]{1,0:T(8,128)S(1)}, u32[]{:S(2)}, u32[]{:S(2)}) collective-permute-start(f32[8,128]{1,0:T(8,128)S(1)} %get-tuple-element.34), channel_id=1, source_target_pairs={{0,2},{1,3},{2,0},{3,1},{4,6},{5,7},{6,4},{7,5},{8,10},{9,11},{10,... | collective-permute-start | bytes 12296 | tf_op jit(solution)/shard_map/ppermute | solution.py:544
  76.3 0.1 collective-permute-done.4
  76.4 0.0 collective-permute-done.2
  76.4 1.4 %collective-permute-done.3 = f32[8,128]{1,0:T(8,128)S(1)} collective-permute-done((f32[8,128]{1,0:T(8,128)S(1)}, f32[8,128]{1,0:T(8,128)S(1)}, u32[]{:S(2)}, u32[]{:S(2)}) %collective-permute-start.3) | collective-permute-done | bytes 4128 | tf_op jit(solution)/shard_map/ppermute | solution.py:544
  77.8 1.6 %collective-permute-start.7 = (f32[8,128]{1,0:T(8,128)S(1)}, f32[8,128]{1,0:T(8,128)S(1)}, u32[]{:S(2)}, u32[]{:S(2)}) collective-permute-start(f32[8,128]{1,0:T(8,128)S(1)} %add_add_fusion.1), channel_id=1, source_target_pairs={{0,12},{1,13},{2,14},{3,15},{4,8},{5,9},{6,10},{7,11},{8,4},{9,5},... | collective-permute-start | bytes 12296 | tf_op jit(solution)/shard_map/ppermute | solution.py:544
  79.4 2.3 %collective-permute-start.5 = (f32[8,128]{1,0:T(8,128)S(1)}, f32[8,128]{1,0:T(8,128)S(1)}, u32[]{:S(2)}, u32[]{:S(2)}) collective-permute-start(f32[8,128]{1,0:T(8,128)S(1)} %add_add_fusion.1), channel_id=1, source_target_pairs={{0,4},{1,5},{2,6},{3,7},{4,0},{5,1},{6,2},{7,3},{8,12},{9,13},{10,... | collective-permute-start | bytes 12296 | tf_op jit(solution)/shard_map/ppermute | solution.py:544
  81.7 0.3 collective-permute-start.6
  81.9 1.0 collective-permute-done.7
  83.0 0.7 collective-permute-done.5
  83.6 13.7 %collective-permute-done.6 = f32[8,128]{1,0:T(8,128)S(1)} collective-permute-done((f32[8,128]{1,0:T(8,128)S(1)}, f32[8,128]{1,0:T(8,128)S(1)}, u32[]{:S(2)}, u32[]{:S(2)}) %collective-permute-start.6) | collective-permute-done | bytes 4128 | tf_op jit(solution)/shard_map/ppermute | solution.py:544
  97.3 1.0 norm.1
  98.3 0.1 all-to-all-done.1.in_ref.sums_ref
  98.4 0.7 rows.1
  99.2 10.4 %collective-permute-start.8 = (bf16[32,128]{1,0:T(8,128)(2,1)S(1)}, bf16[32,128]{1,0:T(8,128)(2,1)S(1)}, u32[]{:S(2)}, u32[]{:S(2)}) collective-permute-start(bf16[32,128]{1,0:T(8,128)(2,1)S(1)} %rows.1), channel_id=1, source_target_pairs={{0,0},{1,16},{2,32},{3,48},{4,64},{5,80},{6,96},{7,112},{8,1},{9,1... | collective-permute-start | bytes 24584 | tf_op jit(solution)/shard_map/ppermute | solution.py:576
  109.5 11.4 %gate.1 = bf16[1024,2048]{1,0:T(8,128)(2,1)} custom-call(s32[1]{0:T(128)} %bitcast.at_ref, bf16[1024,2048]{1,0:T(8,128)(2,1)} %inner.1.yl_ref, bf16[1024,2048]{1,0:T(8,128)(2,1)} %get-tuple-element.26.car_ref, bf16[1024,512]{1,0:T(8,128)(2,1)} %get-tuple-element.23.bc_ref.c_ref, bf16[8,256,128]{2,1,0:T(8,128)(2,1)} %get-tuple-element.27.bt_ref, ...), custom_call_target="tpu_custom_call" | custom-call | flops 4000000000 | bytes 16777216 | tf_op jit(solution)/shard_map/gate/pallas_call | solution.py:449
  120.9 0.0 collective-permute-done.8.rows_ref
  120.9 0.9 patch.1
  (5 shorter events, 0.0 us)
Async XLA Ops:
  2.1 6.8 %collective-permute-start = (bf16[3,2560]{1,0:T(4,128)(2,1)S(1)}, bf16[3,2560]{1,0:T(4,128)(2,1)S(1)}, u32[]{:S(2)}, u32[]{:S(2)}) collective-permute-start(bf16[3,2560]{1,0:T(4,128)(2,1)S(1)} %pad_maximum_fusion.1), channel_id=1, source_target_pairs={{0,8},{8,16},{16,24},{24,32},{32,40},{40,48},{48,56},{56,64},{64,7... | collective-permute-start | bytes 46088 | tf_op jit(solution)/shard_map/ppermute | solution.py:483
  25.3 5.7 %copy-start = (s32[32]{0:T(128)S(1)}, s32[32]{0:T(128)}, u32[]{:S(2)}) copy-start(s32[32]{0:T(128)} %slot_ref.1) | copy-start | bytes 388
  25.3 6.8 %copy-start.1 = (f32[256]{0:T(256)S(1)}, f32[256]{0:T(256)}, u32[]{:S(2)}) copy-start(f32[256]{0:T(256)} %alog_ref.1) | copy-start | bytes 3076
  25.3 6.8 %copy-start.2 = (f32[256]{0:T(256)S(1)}, f32[256]{0:T(256)}, u32[]{:S(2)}) copy-start(f32[256]{0:T(256)} %bias_ref.1) | copy-start | bytes 3076
  25.3 6.8 %copy-start.3 = (f32[256]{0:T(256)S(1)}, f32[256]{0:T(256)}, u32[]{:S(2)}) copy-start(f32[256]{0:T(256)} %skip_ref.1) | copy-start | bytes 3076
  25.3 31.8 %all-to-all-start = ((f32[16,264,128]{2,1,0:T(8,128)}), f32[16,264,128]{2,1,0:T(8,128)S(1)}, u32[]{:S(2)}, u32[]{:S(2)}) async-start(f32[16,264,128]{2,1,0:T(8,128)} %get-tuple-element.21), calls=%async_computation | async-start | bytes 4325376 | tf_op jit(solution)/shard_map/all_to_all | solution.py:495
  39.4 25.0 %collective-permute-start.1 = (bf16[224,256]{1,0:T(8,128)(2,1)S(1)}, bf16[224,256]{1,0:T(8,128)(2,1)S(1)}, u32[]{:S(2)}, u32[]{:S(2)}) collective-permute-start(bf16[224,256]{1,0:T(8,128)(2,1)S(1)} %pad_maximum_fusion), channel_id=1, source_target_pairs={{0,0},{16,1},{32,2},{48,3},{64,4},{80,5},{96,6},{112,7},{1,8},{17,... | collective-permute-start | bytes 344072 | tf_op jit(solution)/shard_map/ppermute | solution.py:528
  66.3 32.1 %all-to-all-start.1 = ((f32[16,264,128]{2,1,0:T(8,128)}), f32[16,264,128]{2,1,0:T(8,128)S(1)}, u32[]{:S(2)}, u32[]{:S(2)}) async-start(f32[16,264,128]{2,1,0:T(8,128)} %get-tuple-element.32), calls=%async_computation.1 | async-start | bytes 4325376 | tf_op jit(solution)/shard_map/all_to_all | solution.py:540
  73.1 3.3 %collective-permute-start.4 = (f32[8,128]{1,0:T(8,128)S(1)}, f32[8,128]{1,0:T(8,128)S(1)}, u32[]{:S(2)}, u32[]{:S(2)}) collective-permute-start(f32[8,128]{1,0:T(8,128)S(1)} %get-tuple-element.34), channel_id=1, source_target_pairs={{0,3},{1,2},{2,1},{3,0},{4,7},{5,6},{6,5},{7,4},{8,11},{9,10},{10,... | collective-permute-start | bytes 12296 | tf_op jit(solution)/shard_map/ppermute | solution.py:544
  73.1 3.3 %collective-permute-start.2 = (f32[8,128]{1,0:T(8,128)S(1)}, f32[8,128]{1,0:T(8,128)S(1)}, u32[]{:S(2)}, u32[]{:S(2)}) collective-permute-start(f32[8,128]{1,0:T(8,128)S(1)} %get-tuple-element.34), channel_id=1, source_target_pairs={{0,1},{1,0},{2,3},{3,2},{4,5},{5,4},{6,7},{7,6},{8,9},{9,8},{10,11... | collective-permute-start | bytes 12296 | tf_op jit(solution)/shard_map/ppermute | solution.py:544
  75.0 2.8 %collective-permute-start.3 = (f32[8,128]{1,0:T(8,128)S(1)}, f32[8,128]{1,0:T(8,128)S(1)}, u32[]{:S(2)}, u32[]{:S(2)}) collective-permute-start(f32[8,128]{1,0:T(8,128)S(1)} %get-tuple-element.34), channel_id=1, source_target_pairs={{0,2},{1,3},{2,0},{3,1},{4,6},{5,7},{6,4},{7,5},{8,10},{9,11},{10,... | collective-permute-start | bytes 12296 | tf_op jit(solution)/shard_map/ppermute | solution.py:544
  77.8 5.2 %collective-permute-start.7 = (f32[8,128]{1,0:T(8,128)S(1)}, f32[8,128]{1,0:T(8,128)S(1)}, u32[]{:S(2)}, u32[]{:S(2)}) collective-permute-start(f32[8,128]{1,0:T(8,128)S(1)} %add_add_fusion.1), channel_id=1, source_target_pairs={{0,12},{1,13},{2,14},{3,15},{4,8},{5,9},{6,10},{7,11},{8,4},{9,5},... | collective-permute-start | bytes 12296 | tf_op jit(solution)/shard_map/ppermute | solution.py:544
  79.4 4.3 %collective-permute-start.5 = (f32[8,128]{1,0:T(8,128)S(1)}, f32[8,128]{1,0:T(8,128)S(1)}, u32[]{:S(2)}, u32[]{:S(2)}) collective-permute-start(f32[8,128]{1,0:T(8,128)S(1)} %add_add_fusion.1), channel_id=1, source_target_pairs={{0,4},{1,5},{2,6},{3,7},{4,0},{5,1},{6,2},{7,3},{8,12},{9,13},{10,... | collective-permute-start | bytes 12296 | tf_op jit(solution)/shard_map/ppermute | solution.py:544
  81.7 15.6 %collective-permute-start.6 = (f32[8,128]{1,0:T(8,128)S(1)}, f32[8,128]{1,0:T(8,128)S(1)}, u32[]{:S(2)}, u32[]{:S(2)}) collective-permute-start(f32[8,128]{1,0:T(8,128)S(1)} %add_add_fusion.1), channel_id=1, source_target_pairs={{0,8},{1,9},{2,10},{3,11},{4,12},{5,13},{6,14},{7,15},{8,0},{9,1},... | collective-permute-start | bytes 12296 | tf_op jit(solution)/shard_map/ppermute | solution.py:544
  99.2 21.8 %collective-permute-start.8 = (bf16[32,128]{1,0:T(8,128)(2,1)S(1)}, bf16[32,128]{1,0:T(8,128)(2,1)S(1)}, u32[]{:S(2)}, u32[]{:S(2)}) collective-permute-start(bf16[32,128]{1,0:T(8,128)(2,1)S(1)} %rows.1), channel_id=1, source_target_pairs={{0,0},{1,16},{2,32},{3,48},{4,64},{5,80},{6,96},{7,112},{8,1},{9,1... | collective-permute-start | bytes 24584 | tf_op jit(solution)/shard_map/ppermute | solution.py:576
